TPU v7x, 32 devices: a whole 2x2x4 slice. The times are simulated.
32 devices in a mesh: grp: 2 (over y), epoch: 4 (over z), tile: 2 (over x), sub: 2 (over core).
Axes of the slice: x: 2, y: 2, z: 4, core: 2. Of those that a mesh axis runs over, the one named last changes fastest.
Arguments:
- epoch_images: float32 [32, 512, 512], P(('grp', 'epoch'), ('tile', 'sub')), parts along dimension 0, may hold values from -8 to 8
- psf_bank: float32 [16, 16, 16], replicated, may hold values from 0.05 to 1
- psf_index: int32 [32], P(('grp', 'epoch')), parts along dimension 0, may hold values from 0 to 15
- flux_scale: float32 [32], P(('grp', 'epoch')), parts along dimension 0, may hold values from 0.3 to 3
- noise_level: float32 [32], P(('grp', 'epoch')), parts along dimension 0, may hold values from 0.5 to 2
- src_row: int32 [8192], P('grp'), parts along dimension 0, may hold values from 0 to 511
- src_col: int32 [8192], P('grp'), parts along dimension 0, may hold values from 0 to 511
Outputs:
- difference: float32 [32, 512, 512], P(('grp', 'epoch'), ('tile', 'sub')), parts along dimension 0
- fluxes: float32 [32, 4096], P(('grp', 'epoch'), ('tile', 'sub')), parts along dimension 0
There are 2 independent parts, one for each index of `grp`. A program takes and returns all parts, laid end to end along the dimension named above; an argument that names none is the same for every part. Nothing has to cross between parts.
All inputs are finite; a program needn't handle non-finite values.
Results may differ from a plain program's by a relative error of at most 0.0003.
Values sent between devices are 32-bit elements; how exact they have to be, the bound alone decides.
No kernel may reach another device: no remote copies, remote signals or barrier semaphores. Data moves between devices by JAX's collectives and lax.ppermute only.
A program may use at most 128 MiB of HBM per device.

v0:
```python
import math

import jax
import jax.numpy as jnp
import ml_dtypes
import numpy as np
from jax import lax
from jax.experimental import pallas as pl
from jax.experimental.pallas import tpu as pltpu
from jax.sharding import PartitionSpec as P

reg_floor = 0.01
vmem_limit = 40 * 1024 * 1024
bf16, f32 = jnp.bfloat16, jnp.float32
edge_rows = 16


def halves(table):
    table = np.asarray(table, np.float64)
    high = table.astype(ml_dtypes.bfloat16)
    return np.stack([high, (table - high.astype(np.float64)).astype(ml_dtypes.bfloat16)])


def split(value):
    high = value.astype(bf16)
    return high, (value - high.astype(f32)).astype(bf16)


def angle(first, second, length):
    return np.outer(first, second) % length * (2.0 * math.pi / length)


def mul(left, right, transposed=False):
    dims = (((1,), (1,)), ((), ())) if transposed else (((1,), (0,)), ((), ()))
    return lax.dot_general(left, right, dims, preferred_element_type=f32)


def mul3(left, right, transposed=False):
    return (
        mul(left[0], right[0], transposed)
        + mul(left[1], right[0], transposed)
        + mul(left[0], right[1], transposed)
    )


class Plan:
    def __init__(self, side, slabs, stamp):
        self.side, self.slabs, self.stamp = side, slabs, stamp
        half = self.half = side // 2
        cols = self.cols = half // slabs
        lanes = self.lanes = 2 * cols
        rows = self.rows = side // slabs
        pairs = self.pairs = slabs // 2
        self.halo = stamp // 2
        self.tall = rows + 2 * self.halo
        self.band = cols + 8
        owner = np.arange(slabs)[:, None]
        freq = 2 * (cols * (owner % pairs) + np.arange(cols)[None, :]) + owner // pairs
        short = np.arange(half)
        taps = np.arange(stamp) - stamp // 2
        order = np.concatenate([2 * short, 2 * short + 1])

        ahead = np.zeros((slabs, 2, cols, half))
        back = np.zeros((slabs, 2, cols, half))
        coef = np.zeros((stamp, 2, slabs, 2, cols))
        shift = np.zeros((slabs, 2, self.band, 2, stamp))
        for d in range(slabs):
            th = angle(freq[d], short, side)
            ahead[d, 0], ahead[d, 1] = np.cos(th), -np.sin(th)
            back[d, 0], back[d, 1] = 2 * np.cos(th) / side, -2 * np.sin(th) / side
            tb = angle(taps, freq[d], side)
            coef[:, 0, d, 0] = coef[:, 0, d, 1] = np.cos(tb)
            coef[:, 1, d, 0], coef[:, 1, d, 1] = np.sin(tb), -np.sin(tb)
            te = angle(np.concatenate([freq[d], [half]]), taps, side)
            ce, se = np.cos(te), np.sin(te)
            shift[d, 0, : cols + 1, 0], shift[d, 0, : cols + 1, 1] = ce, -se
            shift[d, 1, : cols + 1, 0], shift[d, 1, : cols + 1, 1] = -se, -ce
        nyquist = np.cos(math.pi * short)
        ahead[0, 1, 0] = nyquist
        back[0, 0, 0], back[0, 1, 0] = 1.0 / side, nyquist / side
        coef[:, 0, 0, 1, 0], coef[:, 1, 0, 1, 0] = np.cos(math.pi * taps), 0.0
        self.ahead = halves(ahead.reshape(slabs, lanes, half))
        self.back = halves(back.reshape(slabs, lanes, half))
        self.coef = coef.reshape(stamp, 2 * slabs * lanes).astype(np.float32)
        self.shift = halves(shift.reshape(slabs, 2 * self.band, 2 * stamp))

        down = np.zeros((2, 2, half, half))
        up = np.zeros((2, half, 2 * half))
        for odd in range(2):
            th = angle(short, 2 * short + odd, side)
            down[odd, 0], down[odd, 1] = np.cos(th), np.sin(th)
            up[odd, :, :half], up[odd, :, half:] = np.cos(th) / side, np.sin(th) / side
        self.down = halves(down.reshape(2, 2, pairs, rows, half))
        self.up = halves(up)
        tu = angle(taps, order, side)
        high, low = halves(np.concatenate([np.cos(tu), np.sin(tu)], 0))
        self.spread = np.concatenate([high, high, low, np.zeros_like(high)], 0)


def call(kernel, outs, ins, scratch=(), aliases=None):
    space = {"s": pltpu.SMEM, "v": pltpu.VMEM, "h": pl.ANY, "m": pltpu.HBM}
    return pl.pallas_call(
        kernel,
        out_shape=tuple(jax.ShapeDtypeStruct(shape, f32) for _, shape in outs),
        in_specs=[pl.BlockSpec(memory_space=space[kind]) for kind, _ in ins],
        out_specs=tuple(pl.BlockSpec(memory_space=space[kind]) for kind, _ in outs),
        scratch_shapes=list(scratch),
        input_output_aliases=aliases or {},
        compiler_params=pltpu.CompilerParams(vmem_limit_bytes=vmem_limit),
        cost_estimate=pl.CostEstimate(flops=0, bytes_accessed=0, transcendentals=0),
    )(*[a for _, a in ins])


def filter_taps(plan, bank_ref, coef_ref, index_ref, epochs, factor, taps_ref):
    stamp, slabs, lanes = plan.stamp, plan.slabs, plan.lanes
    filters = []
    for e in range(epochs):
        own = bank_ref[index_ref[e]]
        own = own / jnp.sum(own, keepdims=True)
        filters.append(factor(e, own))
    taps = jnp.dot(
        jnp.concatenate(filters, 0), coef_ref[...],
        precision=lax.Precision.HIGHEST, preferred_element_type=f32,
    )
    for kind in range(2):
        for d in range(slabs):
            start = (kind * slabs + d) * lanes
            taps_ref[kind, d] = taps[:, start : start + lanes]


def swap_halves(plan, value):
    return jnp.concatenate([value[:, plan.cols :], value[:, : plan.cols]], 1)


def row_transform(plan, place, index, flux, noise, images, bank):
    epochs, rows, side = images.shape
    width = epochs * rows
    half, slabs, pairs, lanes, tall, stamp = (
        plan.half, plan.slabs, plan.pairs, plan.lanes, plan.tall, plan.stamp,
    )
    step = tall // 2

    def kernel(place_ref, index_ref, flux_ref, noise_ref, bank_ref, coef_ref, image_ref, table_ref, *rest):
        outs, numers = rest[:slabs], rest[slabs : 2 * slabs]
        x_ref, both_ref, taps_ref, padded, gathered, sems = rest[2 * slabs :]
        copies = [
            pltpu.make_async_copy(image_ref, x_ref, sems.at[0]),
            pltpu.make_async_copy(table_ref, both_ref, sems.at[1]),
        ]
        for copy in copies:
            copy.start()
        filter_taps(
            plan, bank_ref, coef_ref, index_ref, epochs,
            lambda e, own: own * (flux_ref[e] / (noise_ref[e] * noise_ref[e])), taps_ref,
        )
        padded[:, :, :stamp] = jnp.zeros((slabs, epochs, stamp, lanes), f32)
        padded[:, :, stamp + rows :] = jnp.zeros((slabs, epochs, stamp, lanes), f32)
        for copy in copies:
            copy.wait()
        q = place_ref[0]
        x = x_ref[...].reshape(width, side)
        first, second = x[:, :half], x[:, half:]
        total = first + second
        change = first - second
        flag = jnp.broadcast_to((q >= pairs).astype(jnp.int32), (1, 1)) > 0
        for group in range(2):
            pick = flag if group == 0 else jnp.logical_not(flag)
            data = split(jnp.where(pick, change, total))
            owners = [q ^ (group * pairs + m) for m in range(pairs)]
            table = [jnp.concatenate([both_ref[n, d] for d in owners], 0) for n in range(2)]
            upright = mul3(data, table, True)
            result = mul3(table, data, True)
            for m in range(pairs):
                here = slice(m * lanes, (m + 1) * lanes)
                outs[group * pairs + m][...] = result[here]
                for e in range(epochs):
                    padded[group * pairs + m, e, stamp : stamp + rows] = upright[
                        e * rows : (e + 1) * rows, here
                    ]

        @pl.loop(0, slabs)
        def _(m):
            d = q ^ m
            for start in range(0, tall, step):
                straight = jnp.zeros((step, lanes), f32)
                crossed = jnp.zeros((step, lanes), f32)
                for e in range(epochs):
                    for a in range(stamp):
                        value = padded[m, e, start + a : start + a + step, :]
                        at = e * stamp + a
                        straight += taps_ref[0, d, at : at + 1] * value
                        crossed += taps_ref[1, d, at : at + 1] * value
                gathered[m, start : start + step] = straight + swap_halves(plan, crossed)

        for m in range(slabs):
            numers[m][...] = gathered[m]

    flat = call(
        kernel,
        [("v", (lanes, width))] * slabs + [("v", (tall, lanes))] * slabs,
        [("s", place), ("s", index), ("s", flux), ("s", noise), ("v", bank), ("v", plan.coef),
         ("m", images), ("m", plan.ahead)],
        [pltpu.VMEM(images.shape, f32), pltpu.VMEM(plan.ahead.shape, bf16),
         pltpu.VMEM((2, slabs, epochs * stamp, lanes), f32),
         pltpu.VMEM((slabs, epochs, rows + 2 * stamp, lanes), f32),
         pltpu.VMEM((slabs, tall, lanes), f32), pltpu.SemaphoreType.DMA((2,))],
    )
    return list(flat[:slabs]), list(flat[slabs:])


def numerator(plan, place, index, flux, noise, blocks, pieces):
    slabs, cols, rows, half, side, lanes, halo, tall = (
        plan.slabs, plan.cols, plan.rows, plan.half, plan.side, plan.lanes, plan.halo, plan.tall,
    )
    epochs = index.shape[0]
    piece = side // pieces

    def kernel(place_ref, index_ref, flux_ref, noise_ref, *rest):
        ins, table_ref = rest[:slabs], rest[slabs]
        outs = rest[slabs + 1 : slabs + 1 + pieces]
        whole, parts = rest[slabs + 1 + pieces :]
        q, z = place_ref[0], place_ref[1] if pieces > 1 else 0
        whole[...] = jnp.zeros((side + 2 * halo, lanes), f32)
        for m in range(slabs):
            at = pl.multiple_of((q ^ m) * rows, rows)
            whole[pl.ds(at, tall)] += ins[m][...]
        whole[side : side + halo] += whole[:halo]
        whole[halo : 2 * halo] += whole[side + halo :]
        top, bottom = whole[halo : halo + half], whole[halo + half : halo + side]
        row = lax.broadcasted_iota(jnp.int32, (cols, half), 0)
        first = (q == 0).astype(f32)
        keep = 1.0 - first * (row == 0).astype(f32)
        line = lax.broadcasted_iota(jnp.int32, (edge_rows, half), 0)
        for odd in range(2):
            value = (top - bottom if odd else top + bottom).T
            re, im = value[:cols], value[cols:]
            edge = jnp.broadcast_to(im[:1] * first, (edge_rows, half))
            im = im * keep
            left = jnp.concatenate(
                [
                    jnp.concatenate([re, im, jnp.where(line == 0, edge, 0.0)], 0),
                    jnp.concatenate([im, -re, jnp.where(line == 1, -edge, 0.0)], 0),
                ],
                1,
            )
            table = [
                jnp.concatenate([table_ref[n, odd, kind].reshape(half, half) for kind in range(2)], 0)
                for n in range(2)
            ]
            plane = mul3(split(left), table)[: lanes + 8]
            step = min(piece, half)
            for i in range(half // step):
                at = odd * half + i * step
                parts[at // piece, :, at % piece : at % piece + step] = plane[:, i * step : (i + 1) * step]
        lane = lax.broadcasted_iota(jnp.int32, (1, piece), 1)
        shares = jnp.zeros((1, piece), f32)
        for e in range(epochs):
            ratio = flux_ref[e] / noise_ref[e]
            shares += jnp.where(lane == index_ref[e], ratio * ratio, 0.0)
        for m in range(pieces):
            parts[m, lanes + 2 : lanes + 3] = shares
        for m in range(pieces):
            outs[m][...] = parts[z ^ m]

    return call(
        kernel,
        [("v", (lanes + 8, piece))] * pieces,
        [("s", place), ("s", index), ("s", flux), ("s", noise)] + [("v", b) for b in blocks]
        + [("v", plan.down)],
        [pltpu.VMEM((side + 2 * halo, lanes), f32), pltpu.VMEM((pieces, lanes + 8, piece), f32)],
    )


def psf_planes(plan, place, bank, index):
    epochs = index.shape[0]
    count, stamp = bank.shape[:2]
    side, cols, band, slabs, lanes = plan.side, plan.cols, plan.band, plan.slabs, plan.lanes
    body = epochs * cols
    size = body + edge_rows
    pitch = 8 * stamp

    def kernel(
        place_ref, index_ref, bank_ref, shift_ref, spread_ref, coef_ref,
        spectrum_ref, power_ref, taps_ref, right_ref, plane_ref,
    ):
        q = place_ref[0]
        stamps = bank_ref[...]
        stamps = stamps / jnp.sum(jnp.sum(stamps, axis=2, keepdims=True), axis=1, keepdims=True)
        blank = jnp.zeros((stamp, stamp), f32)
        for k in range(count):
            pair = jnp.concatenate(
                [jnp.concatenate([stamps[k], blank], 1), jnp.concatenate([blank, stamps[k]], 1)], 0
            )
            for copy in range(4):
                at = k * pitch + copy * 2 * stamp
                right_ref[at : at + 2 * stamp] = pair
        right = split(right_ref[...])
        mixed = mul3((shift_ref[0, q], shift_ref[1, q]), right, True)
        lane = lax.broadcasted_iota(jnp.int32, mixed.shape, 1) % pitch
        middle = (lane >= 2 * stamp) & (lane < 4 * stamp)
        high = mixed.astype(bf16).astype(f32)
        left = jnp.where(middle, mixed - high, high).astype(bf16)
        for k in range(count):
            plane = mul(left[:, k * pitch : (k + 1) * pitch], spread_ref[...])
            plane_ref[k] = plane
            power_ref[k] = plane[:band] * plane[:band] + plane[band:] * plane[band:]
        for e in range(epochs):
            k = index_ref[e]
            for base, start in ((0, 0), (size, band)):
                value = plane_ref[k, start : start + band]
                spectrum_ref[base + e * cols : base + (e + 1) * cols] = value[:cols]
                spectrum_ref[base + body + e : base + body + e + 1] = value[cols : cols + 1]
        none = jnp.zeros((edge_rows - epochs, side), f32)
        spectrum_ref[body + epochs : size] = none
        spectrum_ref[size + body + epochs :] = none
        filter_taps(
            plan, bank_ref, coef_ref, index_ref, epochs,
            lambda e, own: own / jnp.sum(own * own, keepdims=True), taps_ref,
        )

    return call(
        kernel,
        [("v", (2 * size, side)), ("v", (count, band, side)), ("v", (2, slabs, epochs * stamp, lanes))],
        [("s", place), ("s", index), ("v", bank), ("v", plan.shift), ("v", plan.spread), ("v", plan.coef)],
        [pltpu.VMEM((count * pitch, 2 * stamp), f32), pltpu.VMEM((count, 2 * band, side), f32)],
    )


def filter_gains(plan, flux, noise, share, spectrum, power):
    epochs = flux.shape[0]
    count = power.shape[0]
    side, cols = plan.side, plan.cols
    body = epochs * cols
    size = body + edge_rows
    row = plan.lanes + 2

    def kernel(flux_ref, noise_ref, share_ref, spectrum_ref, power_ref, gain_ref, cross_ref):
        shares = [jnp.broadcast_to(share_ref[row : row + 1, k : k + 1], (8, side)) for k in range(count)]
        none = jnp.zeros((edge_rows - epochs, side), f32)
        gain_ref[body + epochs : size] = none
        cross_ref[body + epochs : size] = none
        cross_ref[size + body + epochs :] = none
        for block in range(plan.band // 8):
            total = jnp.full((8, side), reg_floor, f32)
            for k in range(count):
                total += shares[k] * power_ref[k, block * 8 : block * 8 + 8]
            edge = block == cols // 8
            total = total[:1] if edge else total
            lines = 1 if edge else 8
            root = jnp.sqrt(total)
            inverse_root = 1.0 / root
            for e in range(epochs):
                at = body + e if edge else e * cols + block * 8
                re = spectrum_ref[at : at + lines]
                im = spectrum_ref[size + at : size + at + lines]
                scale, sigma = flux_ref[e], noise_ref[e]
                inverse = lax.rsqrt(
                    sigma * sigma * total + scale * scale * (re * re + im * im) + reg_floor
                )
                ratio = scale * inverse * inverse_root
                gain_ref[at : at + lines] = root * inverse
                cross_ref[at : at + lines] = ratio * re
                cross_ref[size + at : size + at + lines] = ratio * im

    return call(
        kernel,
        [("v", (size, side)), ("v", (2 * size, side))],
        [("s", flux), ("s", noise), ("v", share), ("v", spectrum), ("v", power)],
    )


def column_transform(plan, place, blocks):
    slabs, pairs, cols, rows, half, side = plan.slabs, plan.pairs, plan.cols, plan.rows, plan.half, plan.side
    epochs = blocks[0].shape[1] // rows
    body = epochs * cols
    size = body + edge_rows

    def kernel(place_ref, *rest):
        ins = rest[:slabs]
        table_ref, plane_ref, left_high, left_low = rest[slabs:]
        q = place_ref[0]
        first = (q == 0).astype(f32)
        sign = jnp.where(q < pairs, 1.0, -1.0).astype(f32)
        row = lax.broadcasted_iota(jnp.int32, (cols, rows), 0)
        keep = 1.0 - first * (row == 0).astype(f32)

        def put(row_at, lane_at, entry):
            where = (slice(row_at, row_at + entry.shape[0]), slice(lane_at, lane_at + rows))
            left_high[where], left_low[where] = split(entry)

        for odd in range(2):
            for m in range(pairs):
                near, far = ins[m][...], ins[m + pairs][...]
                value = sign * (near - far) if odd else near + far
                edges = []
                for e in range(epochs):
                    re = value[:cols, e * rows : (e + 1) * rows]
                    im = value[cols:, e * rows : (e + 1) * rows]
                    edges.append(im[:1] * first)
                    im = im * keep
                    put(e * cols, m * rows, re)
                    put(e * cols, half + m * rows, im)
                    put(size + e * cols, m * rows, im)
                    put(size + e * cols, half + m * rows, -re)
                edge = jnp.concatenate(edges + [jnp.zeros((edge_rows - epochs, rows), f32)], 0)
                put(body, m * rows, edge)
                put(body, half + m * rows, jnp.zeros_like(edge))
                put(size + body, m * rows, jnp.zeros_like(edge))
                put(size + body, half + m * rows, -edge)
            order = [(q ^ m) % pairs for m in range(pairs)]
            table = [
                jnp.concatenate([table_ref[n, odd, kind, i] for kind in range(2) for i in order], 0)
                for n in range(2)
            ]
            plane_ref[:, odd * half : (odd + 1) * half] = mul3((left_high[...], left_low[...]), table)

    (plane,) = call(
        kernel,
        [("v", (2 * size, side))],
        [("s", place)] + [("v", b) for b in blocks] + [("v", plan.down)],
        [pltpu.VMEM((2 * size, side), bf16), pltpu.VMEM((2 * size, side), bf16)],
    )
    return plane


def column_inverse(plan, place, spectrum, gain, cross, numer, begin, end):
    slabs, cols, rows, half, side, lanes, halo, tall = (
        plan.slabs, plan.cols, plan.rows, plan.half, plan.side, plan.lanes, plan.halo, plan.tall,
    )
    size = gain.shape[0]
    body = size - edge_rows
    epochs = end - begin
    pieces = len(numer)
    piece = side // pieces

    def kernel(place_ref, spectrum_ref, gain_ref, cross_ref, *rest):
        numer_refs, table_ref = rest[:pieces], rest[pieces]
        outs = rest[pieces + 1 : pieces + 1 + slabs]
        whole, right_high, right_low, planes = rest[pieces + 1 + slabs :]
        q, z = place_ref[0], place_ref[1] if pieces > 1 else 0
        for m in range(pieces):
            whole[z ^ m] = numer_refs[m][...]
        flag = jnp.broadcast_to(q, (cols, half)) == 0
        packed = flag & (lax.broadcasted_iota(jnp.int32, (cols, half), 0) == 0)
        results = []
        for odd in range(2):
            here = slice(odd * half, (odd + 1) * half)
            step = min(piece, half)
            parts = [
                whole[at // piece, :, at % piece : at % piece + step]
                for at in range(odd * half, (odd + 1) * half, step)
            ]
            numer_all = parts[0] if len(parts) == 1 else jnp.concatenate(parts, 1)

            def difference(start, stop, nre, nim):
                gain_, cre = gain_ref[start:stop, here], cross_ref[start:stop, here]
                cim = cross_ref[size + start : size + stop, here]
                re = gain_ * spectrum_ref[start:stop, here] - (cre * nre - cim * nim)
                im = gain_ * spectrum_ref[size + start : size + stop, here] - (cre * nim + cim * nre)
                return re, im

            edge_re, edge_im = difference(
                body, size, numer_all[lanes : lanes + 1], numer_all[lanes + 1 : lanes + 2]
            )
            for i in range(epochs):
                e = begin + i
                re, im = difference(e * cols, (e + 1) * cols, numer_all[:cols], numer_all[cols:lanes])
                im_left = jnp.where(packed, edge_re[e : e + 1], im)
                im_right = jnp.where(packed, -edge_im[e : e + 1], re)
                for base, start, entry in (
                    (0, 0, re), (0, half, -im), (cols, 0, im_left), (cols, half, im_right),
                ):
                    where = (
                        slice(i * lanes + base, i * lanes + base + cols),
                        slice(start, start + half),
                    )
                    right_high[where], right_low[where] = split(entry)
            results.append(
                mul3((table_ref[0, odd], table_ref[1, odd]), (right_high[...], right_low[...]), True)
            )
        planes[halo : halo + half] = results[0] + results[1]
        planes[halo + half : halo + side] = results[0] - results[1]
        planes[:halo] = planes[side : side + halo]
        planes[halo + side :] = planes[halo : 2 * halo]
        for m in range(slabs):
            start = pl.multiple_of((q ^ m) * rows, rows)
            for i in range(epochs):
                outs[m][i] = planes[pl.ds(start, tall), i * lanes : (i + 1) * lanes]

    return call(
        kernel,
        [("v", (epochs, tall, lanes))] * slabs,
        [("s", place), ("v", spectrum), ("v", gain), ("v", cross)] + [("v", n) for n in numer]
        + [("v", plan.up)],
        [pltpu.VMEM((pieces, lanes + 8, piece), f32),
         pltpu.VMEM((epochs * lanes, side), bf16), pltpu.VMEM((epochs * lanes, side), bf16),
         pltpu.VMEM((side + 2 * halo, epochs * lanes), f32)],
    )


def row_inverse(plan, place, blocks, taps, begin, epochs, difference, src_row, src_col):
    slabs, pairs, rows, half, side, lanes, halo, stamp = (
        plan.slabs, plan.pairs, plan.rows, plan.half, plan.side, plan.lanes, plan.halo, plan.stamp,
    )
    mine = blocks[0].shape[0]
    groups, group = src_row.shape
    each = groups // slabs
    total = mine * rows
    step = min(64, rows)

    def kernel(place_ref, row_ref, col_ref, taps_ref, *rest):
        ins, table_ref = rest[:slabs], rest[slabs]
        rest = rest[slabs + 1 + (difference is not None) :]
        diff_ref, outs = rest[0], rest[1 : 1 + slabs]
        left_high, left_low, image_ref, flux_ref, picked, sem = rest[1 + slabs :]
        q = place_ref[0]
        for m in range(slabs):
            d = q ^ m
            here = slice(m * lanes, (m + 1) * lanes)
            for i in range(mine):
                base = i * rows
                left_high[base : base + rows, here], left_low[base : base + rows, here] = split(
                    ins[m][i, halo : halo + rows, :]
                )
                for start in range(0, rows, step):
                    straight = jnp.zeros((step, lanes), f32)
                    crossed = jnp.zeros((step, lanes), f32)
                    for a in range(stamp):
                        value = ins[m][i, start + a : start + a + step, :]
                        at = (begin + i) * stamp + a
                        straight += taps_ref[0, d, at : at + 1] * value
                        crossed += taps_ref[1, d, at : at + 1] * value
                    at = total + base + start
                    left_high[at : at + step, here], left_low[at : at + step, here] = split(
                        straight + swap_halves(plan, crossed)
                    )

        sums = []
        for side_ in range(2):
            members = [side_ * pairs + m for m in range(pairs)]
            table = [jnp.concatenate([table_ref[n, q ^ m] for m in members], 0) for n in range(2)]
            here = slice(side_ * pairs * lanes, (side_ + 1) * pairs * lanes)
            sums.append(mul3((left_high[:, here], left_low[:, here]), table))
        sign = jnp.where(q < pairs, 1.0, -1.0).astype(f32)
        for lane_half in range(2):
            value = sums[0] + sums[1] if lane_half == 0 else sign * (sums[0] - sums[1])
            here = slice(lane_half * half, (lane_half + 1) * half)
            image_ref[:, :, here] = value[:total].reshape(mine, rows, half)
            flux_ref[:total, here], flux_ref[total:, here] = split(value[total:])
        copy = pltpu.make_async_copy(image_ref, diff_ref.at[pl.ds(begin, mine)], sem)
        copy.start()
        column = lax.broadcasted_iota(jnp.int32, (side, group), 0)
        line = lax.broadcasted_iota(jnp.int32, (rows, group), 0)
        for g in range(groups):
            chosen = (column == col_ref[g : g + 1]).astype(f32).astype(bf16)
            values = mul(flux_ref[...], chosen)
            values = values[:total] + values[total:]
            inside = line == row_ref[g : g + 1] - q * rows
            found = [
                jnp.sum(
                    jnp.where(inside, values[e * rows : (e + 1) * rows], 0.0), axis=0, keepdims=True
                )
                for e in range(mine)
            ]
            where = (g % each) * group
            picked[g // each, :, where : where + group] = jnp.concatenate(found, 0)
        for m in range(slabs):
            outs[m][...] = picked[q ^ m]
        copy.wait()

    ins = [("s", place), ("v", src_row), ("v", src_col), ("v", taps)]
    ins += [("v", b) for b in blocks] + [("v", plan.back)]
    aliases = {}
    if difference is not None:
        aliases = {len(ins): 0}
        ins.append(("h", difference))
    left = pltpu.VMEM((2 * total, side), bf16)
    return call(
        kernel,
        [("h", (epochs, rows, side))] + [("v", (mine, each * group))] * slabs,
        ins,
        [left, left, pltpu.VMEM((mine, rows, side), f32), left,
         pltpu.VMEM((slabs, mine, each * group), f32), pltpu.SemaphoreType.DMA(())],
        aliases=aliases,
    )


def trade(parts, axes, count):
    result = list(parts)
    for m in reversed(range(1, count)):
        result[m] = lax.ppermute(parts[m], axes, [(i, i ^ m) for i in range(count)])
    return result


def make_shards(mesh):
    slabs = mesh.shape["tile"] * mesh.shape["sub"]
    ranks = mesh.shape["epoch"]
    slab_axes = ("tile", "sub")

    def shards(epoch_images, psf_bank, psf_index, flux_scale, noise_level, src_row, src_col):
        epochs, rows, side = epoch_images.shape
        plan = Plan(side, slabs, psf_bank.shape[1])
        place = jnp.stack([lax.axis_index(slab_axes), lax.axis_index("epoch")]).astype(jnp.int32)
        direct = ranks & (ranks - 1) == 0 and side // ranks % 128 == 0
        pieces = ranks if direct else 1
        parties = 2 if epochs % 2 == 0 else 1
        group = math.gcd(512, src_row.shape[0] // slabs)
        scalars = (psf_index, flux_scale, noise_level)

        blocks, numer = row_transform(plan, place, *scalars, epoch_images, psf_bank)
        numer = trade(numer, slab_axes, slabs)
        numer = numerator(plan, place, *scalars, numer, pieces)
        blocks, numer = lax.optimization_barrier((blocks, numer))
        blocks = trade(blocks, slab_axes, slabs)
        spectrum, power, taps = psf_planes(plan, place, psf_bank, psf_index)
        if direct:
            own = sum(trade(numer, "epoch", ranks))
            numer = trade([own] * ranks, "epoch", ranks)
        else:
            own = lax.psum(numer[0], "epoch")
            numer = [own]
        images = column_transform(plan, place, blocks)
        gain, cross = filter_gains(plan, flux_scale, noise_level, own, spectrum, power)

        difference, fluxes = None, []
        each = epochs // parties
        returned = [
            trade(
                column_inverse(plan, place, images, gain, cross, numer, i * each, (i + 1) * each),
                slab_axes, slabs,
            )
            for i in range(parties)
        ]
        for i in range(parties):
            difference, *picked = row_inverse(
                plan, place, returned[i], taps, i * each, epochs, difference,
                src_row.reshape(-1, group), src_col.reshape(-1, group),
            )
            fluxes.append(sum(trade(picked, slab_axes, slabs)))
        return difference, jnp.concatenate(fluxes, 0)

    return shards


def solution(mesh):
    in_specs = (
        P(("grp", "epoch"), ("tile", "sub"), None),
        P(),
        P(("grp", "epoch")),
        P(("grp", "epoch")),
        P(("grp", "epoch")),
        P("grp"),
        P("grp"),
    )
    out_specs = (P(("grp", "epoch"), ("tile", "sub"), None), P(("grp", "epoch"), ("tile", "sub")))
    return jax.shard_map(
        make_shards(mesh), mesh=mesh, in_specs=in_specs, out_specs=out_specs, check_vma=False
    )
```

profile of v0, /device:TPU:0, one launch (start us, length us, event | category | flops | bytes accessed | tf_op | source)
XLA Modules:
  0.0 70.9 jit_solution(6508980076130907235)
XLA Ops:
  0.6 0.0 copy-start
  0.6 0.1 pad_add_fusion.place_ref
  0.7 1.3 %copy-done.3 = f32[4,128,512]{2,1,0:T(8,128)S(1)} copy-done((f32[4,128,512]{2,1,0:T(8,128)S(1)}, f32[4,128,512]{2,1,0:T(8,128)}, u32[]{:S(2)}) %copy-start.3) | copy-done | bytes 1048600
  2.0 1.0 %copy-done.4 = bf16[2,4,128,256]{3,2,1,0:T(8,128)(2,1)S(1)} copy-done((bf16[2,4,128,256]{3,2,1,0:T(8,128)(2,1)S(1)}, bf16[2,4,128,256]{3,2,1,0:T(8,128)(2,1)}, u32[]{:S(2)}) %copy-start.4) | copy-done | bytes 524312
  3.1 0.9 %copy-done.5 = f32[16,16,16]{2,1,0:T(8,128)S(1)} copy-done((f32[16,16,16]{2,1,0:T(8,128)S(1)}, f32[16,16,16]{2,1,0:T(8,128)}, u32[]{:S(2)}) %copy-start.5) | copy-done | bytes 16408
  4.0 0.8 %copy-done.8 = f32[16,1024]{1,0:T(8,128)S(1)} copy-done((f32[16,1024]{1,0:T(8,128)S(1)}, f32[16,1024]{1,0:T(8,128)}, u32[]{:S(2)}) %copy-start.8) | copy-done | bytes 65560
  4.8 0.7 copy-done.11
  5.5 0.7 copy-done.12
  6.1 0.7 copy-done.13
  6.8 5.9 %shard_map.150 = (f32[128,512]{1,0:T(8,128)S(1)}, f32[128,512]{1,0:T(8,128)S(1)}, f32[128,512]{1,0:T(8,128)S(1)}, f32[128,512]{1,0:T(8,128)S(1)}, f32[144,128]{1...) custom-call(s32[2]{0:T(128)S(1)} %pad_add_fusion.place_ref, ...), custom_call_target="tpu_custom_call" | custom-call | tf_op jit(solution)/shard_map/pallas_call | solution.py:102
  12.7 0.0 copy-start.7
  12.7 0.0 copy-start.9
  12.7 0.5 collective-permute-start
  13.2 2.6 %collective-permute-start.1 = (f32[144,128]{1,0:T(8,128)S(1)}, f32[144,128]{1,0:T(8,128)S(1)}, u32[]{:S(2)}, u32[]{:S(2)}) collective-permute-start(f32[144,128]{1,0:T(8,128)S(1)} %get-tuple-element.52), channel_id=1, source_target_pairs={{0,2},{1,3},{2,0},{3,1},{4,6},{5,7},{6,4},{7,5},{8,10},{9,11},{10,... | collective-permute-start | bytes 221192 | tf_op jit(solution)/shard_map/ppermute | solution.py:591
  15.8 0.1 collective-permute-start.2
  15.9 2.8 %collective-permute-done.1.rest_2_ = f32[144,128]{1,0:T(8,128)S(1)} collective-permute-done((f32[144,128]{1,0:T(8,128)S(1)}, f32[144,128]{1,0:T(8,128)S(1)}, u32[]{:S(2)}, u32[]{:S(2)}) %collective-permute-start.1) | collective-permute-done | bytes 73760 | tf_op jit(solution)/shard_map/ppermute | solution.py:591
  18.7 1.4 %collective-permute-done.2.rest_3_ = f32[144,128]{1,0:T(8,128)S(1)} collective-permute-done((f32[144,128]{1,0:T(8,128)S(1)}, f32[144,128]{1,0:T(8,128)S(1)}, u32[]{:S(2)}, u32[]{:S(2)}) %collective-permute-start.2) | collective-permute-done | bytes 73760 | tf_op jit(solution)/shard_map/ppermute | solution.py:591
  20.0 1.1 %shard_map.151 = (f32[136,128]{1,0:T(8,128)S(1)}, f32[136,128]{1,0:T(8,128)S(1)}, f32[136,128]{1,0:T(8,128)S(1)}, f32[136,128]{1,0:T(8,128)S(1)}) custom-call(s32[2]{0:T(128)S(1)} %pad_add_fusion.place_ref, s32[4]{0:T(128)S(1)} %copy-done.11, f32[4]{0:T(128)S(1)} %copy-done.12, f32[4]{0:T(128)S(1)} %copy-done.14, f32[144,128]{1,0:T(8,128)S(1)} %get-tuple-element.50.rest_0_, ...), custom_call_target="tpu_custom_call" | custom-call | tf_op jit(solution)/shard_map/pallas_call | solution.py:102
  21.2 1.9 %collective-permute-start.6 = (f32[136,128]{1,0:T(8,128)S(1)}, f32[136,128]{1,0:T(8,128)S(1)}, u32[]{:S(2)}, u32[]{:S(2)}) collective-permute-start(f32[136,128]{1,0:T(8,128)S(1)} %get-tuple-element.63), channel_id=1, source_target_pairs={{0,4},{4,0},{8,12},{12,8},{1,5},{5,1},{9,13},{13,9},{2,6},{6,2},{1... | collective-permute-start | bytes 208904 | tf_op jit(solution)/shard_map/ppermute | solution.py:591
  23.1 2.6 %collective-permute-start.7 = (f32[136,128]{1,0:T(8,128)S(1)}, f32[136,128]{1,0:T(8,128)S(1)}, u32[]{:S(2)}, u32[]{:S(2)}) collective-permute-start(f32[136,128]{1,0:T(8,128)S(1)} %get-tuple-element.64), channel_id=1, source_target_pairs={{0,8},{4,12},{8,0},{12,4},{1,9},{5,13},{9,1},{13,5},{2,10},{6,14},... | collective-permute-start | bytes 208904 | tf_op jit(solution)/shard_map/ppermute | solution.py:591
  25.7 1.5 %collective-permute-start.4 = (f32[128,512]{1,0:T(8,128)S(1)}, f32[128,512]{1,0:T(8,128)S(1)}, u32[]{:S(2)}, u32[]{:S(2)}) collective-permute-start(f32[128,512]{1,0:T(8,128)S(1)} %get-tuple-element.60), channel_id=1, source_target_pairs={{0,2},{1,3},{2,0},{3,1},{4,6},{5,7},{6,4},{7,5},{8,10},{9,11},{10,... | collective-permute-start | bytes 786440 | tf_op jit(solution)/shard_map/ppermute | solution.py:591
  27.1 0.4 collective-permute-start.5
  27.5 3.3 %collective-permute-done.7 = f32[136,128]{1,0:T(8,128)S(1)} collective-permute-done((f32[136,128]{1,0:T(8,128)S(1)}, f32[136,128]{1,0:T(8,128)S(1)}, u32[]{:S(2)}, u32[]{:S(2)}) %collective-permute-start.7) | collective-permute-done | bytes 69664 | tf_op jit(solution)/shard_map/ppermute | solution.py:591
  30.9 1.0 %collective-permute-done.8 = f32[136,128]{1,0:T(8,128)S(1)} collective-permute-done((f32[136,128]{1,0:T(8,128)S(1)}, f32[136,128]{1,0:T(8,128)S(1)}, u32[]{:S(2)}, u32[]{:S(2)}) %collective-permute-start.8) | collective-permute-done | bytes 69664 | tf_op jit(solution)/shard_map/ppermute | solution.py:591
  31.9 2.1 %collective-permute-start.10 = (f32[136,128]{1,0:T(8,128)S(1)}, f32[136,128]{1,0:T(8,128)S(1)}, u32[]{:S(2)}, u32[]{:S(2)}) collective-permute-start(f32[136,128]{1,0:T(8,128)S(1)} %add_add_fusion.share_ref.rest_0_), channel_id=1, source_target_pairs={{0,8},{4,12},{8,0},{12,4},{1,9},{5,13},{9,1},{13,5},{2,10},{6,14},... | collective-permute-start | bytes 208904 | tf_op jit(solution)/shard_map/ppermute | solution.py:591
  34.0 1.4 %collective-permute-start.11 = (f32[136,128]{1,0:T(8,128)S(1)}, f32[136,128]{1,0:T(8,128)S(1)}, u32[]{:S(2)}, u32[]{:S(2)}) collective-permute-start(f32[136,128]{1,0:T(8,128)S(1)} %add_add_fusion.share_ref.rest_0_), channel_id=1, source_target_pairs={{0,12},{4,8},{8,4},{12,0},{1,13},{5,9},{9,5},{13,1},{2,14},{6,10},... | collective-permute-start | bytes 208904 | tf_op jit(solution)/shard_map/ppermute | solution.py:591
  35.4 0.0 collective-permute-start.9
  35.5 2.3 %shard_map.149 = (f32[544,512]{1,0:T(8,128)S(1)}, f32[16,72,512]{2,1,0:T(8,128)S(1)}, f32[2,4,64,128]{3,2,1,0:T(8,128)S(1)}) custom-call(s32[2]{0:T(128)S(1)} %pad_add_fusion.place_ref, s32[4]{0:T(128)S(1)} %copy-done.11, f32[16,16,16]{2,1,0:T(8,128)S(1)} %copy-done.6, bf16[2,4,144,32]{3,2,1,0:T(8,128)(2,1)S(1)} %copy-done.7, ...), custom_call_target="tpu_custom_call" | custom-call | tf_op jit(solution)/shard_map/pallas_call | solution.py:102
  37.8 1.1 %shard_map.153 = (f32[272,512]{1,0:T(8,128)S(1)}, f32[544,512]{1,0:T(8,128)S(1)}) custom-call(f32[4]{0:T(128)S(1)} %copy-done.12, f32[4]{0:T(128)S(1)} %copy-done.14, f32[136,128]{1,0:T(8,128)S(1)} %add_add_fusion.share_ref.rest_0_, f32[544,512]{1,0:T(8,128)S(1)} %get-tuple-element.66.spectrum_ref, f32[16,72,512]{2,1,0:T(8,128)S(1)} %get-tuple-element.67.power_ref), custom_call_target="tpu_custom_call" | custom-call | tf_op jit(solution)/shard_map/pallas_call | solution.py:102
  39.0 0.6 collective-permute-done.5.rest_3_
  39.6 1.8 %shard_map.152.spectrum_ref = f32[544,512]{1,0:T(8,128)S(1)} custom-call(s32[2]{0:T(128)S(1)} %pad_add_fusion.place_ref, f32[128,512]{1,0:T(8,128)S(1)} %get-tuple-element.58.rest_0_, f32[128,512]{1,0:T(8,128)S(1)} %collective-permute-done.3.rest_1_, f32[128,512]{1,0:T(8,128)S(1)} %collective-permute-done.4.rest_2_, ...), custom_call_target="tpu_custom_call" | custom-call | tf_op jit(solution)/shard_map/pallas_call | solution.py:102
  41.5 1.4 %shard_map.155 = (f32[2,144,128]{2,1,0:T(8,128)S(1)}, f32[2,144,128]{2,1,0:T(8,128)S(1)}, f32[2,144,128]{2,1,0:T(8,128)S(1)}, f32[2,144,128]{2,1,0:T(8,128)S(1)}) custom-call(s32[2]{0:T(128)S(1)} %pad_add_fusion.place_ref, f32[544,512]{1,0:T(8,128)S(1)} %shard_map.152.spectrum_ref, f32[272,512]{1,0:T(8,128)S(1)} %get-tuple-element.68.gain_ref, ...), custom_call_target="tpu_custom_call" | custom-call | tf_op jit(solution)/shard_map/pallas_call | solution.py:102
  42.9 0.6 collective-permute-start.15
  43.4 1.5 %collective-permute-start.16 = (f32[2,144,128]{2,1,0:T(8,128)S(1)}, f32[2,144,128]{2,1,0:T(8,128)S(1)}, u32[]{:S(2)}, u32[]{:S(2)}) collective-permute-start(f32[2,144,128]{2,1,0:T(8,128)S(1)} %get-tuple-element.76), channel_id=1, source_target_pairs={{0,2},{1,3},{2,0},{3,1},{4,6},{5,7},{6,4},{7,5},{8,10},{9,11},{10,... | collective-permute-start | bytes 442376 | tf_op jit(solution)/shard_map/ppermute | solution.py:591
  44.9 1.4 %shard_map.154 = (f32[2,144,128]{2,1,0:T(8,128)S(1)}, f32[2,144,128]{2,1,0:T(8,128)S(1)}, f32[2,144,128]{2,1,0:T(8,128)S(1)}, f32[2,144,128]{2,1,0:T(8,128)S(1)}) custom-call(s32[2]{0:T(128)S(1)} %pad_add_fusion.place_ref, f32[544,512]{1,0:T(8,128)S(1)} %shard_map.152.spectrum_ref, f32[272,512]{1,0:T(8,128)S(1)} %get-tuple-element.68.gain_ref, ...), custom_call_target="tpu_custom_call" | custom-call | tf_op jit(solution)/shard_map/pallas_call | solution.py:102
  46.3 0.7 %collective-permute-start.12 = (f32[2,144,128]{2,1,0:T(8,128)S(1)}, f32[2,144,128]{2,1,0:T(8,128)S(1)}, u32[]{:S(2)}, u32[]{:S(2)}) collective-permute-start(f32[2,144,128]{2,1,0:T(8,128)S(1)} %get-tuple-element.71), channel_id=1, source_target_pairs={{0,1},{1,0},{2,3},{3,2},{4,5},{5,4},{6,7},{7,6},{8,9},{9,8},{10,11... | collective-permute-start | bytes 442376 | tf_op jit(solution)/shard_map/ppermute | solution.py:591
  47.0 1.5 %collective-permute-start.13 = (f32[2,144,128]{2,1,0:T(8,128)S(1)}, f32[2,144,128]{2,1,0:T(8,128)S(1)}, u32[]{:S(2)}, u32[]{:S(2)}) collective-permute-start(f32[2,144,128]{2,1,0:T(8,128)S(1)} %get-tuple-element.72), channel_id=1, source_target_pairs={{0,2},{1,3},{2,0},{3,1},{4,6},{5,7},{6,4},{7,5},{8,10},{9,11},{10,... | collective-permute-start | bytes 442376 | tf_op jit(solution)/shard_map/ppermute | solution.py:591
  48.5 1.6 %collective-permute-done.16.rest_2_ = f32[2,144,128]{2,1,0:T(8,128)S(1)} collective-permute-done((f32[2,144,128]{2,1,0:T(8,128)S(1)}, f32[2,144,128]{2,1,0:T(8,128)S(1)}, u32[]{:S(2)}, u32[]{:S(2)}) %collective-permute-start.16) | collective-permute-done | bytes 147488 | tf_op jit(solution)/shard_map/ppermute | solution.py:591
  50.1 2.2 %collective-permute-done.17.rest_3_ = f32[2,144,128]{2,1,0:T(8,128)S(1)} collective-permute-done((f32[2,144,128]{2,1,0:T(8,128)S(1)}, f32[2,144,128]{2,1,0:T(8,128)S(1)}, u32[]{:S(2)}, u32[]{:S(2)}) %collective-permute-start.17) | collective-permute-done | bytes 147488 | tf_op jit(solution)/shard_map/ppermute | solution.py:591
  52.3 5.4 %shard_map.156 = (f32[4,128,512]{2,1,0:T(8,128)}, f32[2,1024]{1,0:T(2,128)S(1)}, f32[2,1024]{1,0:T(2,128)S(1)}, f32[2,1024]{1,0:T(2,128)S(1)}, f32[2,1024]{1,0:T(2,128)S(1)}) custom-call(s32[2]{0:T(128)S(1)} %pad_add_fusion.place_ref, s32[8,512]{1,0:T(8,128)S(1)} %reshape.12.row_ref, s32[8,512]{1,0:T(8,128)S(1)} %reshape.13.col_ref, ...), custom_call_target="tpu_custom_call" | custom-call | tf_op jit(solution)/shard_map/pallas_call | solution.py:102
  57.7 0.9 %collective-permute-start.18 = (f32[2,1024]{1,0:T(2,128)S(1)}, f32[2,1024]{1,0:T(2,128)S(1)}, u32[]{:S(2)}, u32[]{:S(2)}) collective-permute-start(f32[2,1024]{1,0:T(2,128)S(1)} %get-tuple-element.81), channel_id=1, source_target_pairs={{0,1},{1,0},{2,3},{3,2},{4,5},{5,4},{6,7},{7,6},{8,9},{9,8},{10,11... | collective-permute-start | bytes 24584 | tf_op jit(solution)/shard_map/ppermute | solution.py:591
  58.6 1.5 %collective-permute-start.19 = (f32[2,1024]{1,0:T(2,128)S(1)}, f32[2,1024]{1,0:T(2,128)S(1)}, u32[]{:S(2)}, u32[]{:S(2)}) collective-permute-start(f32[2,1024]{1,0:T(2,128)S(1)} %get-tuple-element.82), channel_id=1, source_target_pairs={{0,2},{1,3},{2,0},{3,1},{4,6},{5,7},{6,4},{7,5},{8,10},{9,11},{10,... | collective-permute-start | bytes 24584 | tf_op jit(solution)/shard_map/ppermute | solution.py:591
  60.1 4.8 %shard_map.157 = (f32[4,128,512]{2,1,0:T(8,128)}, f32[2,1024]{1,0:T(2,128)S(1)}, f32[2,1024]{1,0:T(2,128)S(1)}, f32[2,1024]{1,0:T(2,128)S(1)}, f32[2,1024]{1,0:T(2,128)S(1)}) custom-call(s32[2]{0:T(128)S(1)} %pad_add_fusion.place_ref, s32[8,512]{1,0:T(8,128)S(1)} %reshape.12.row_ref, s32[8,512]{1,0:T(8,128)S(1)} %reshape.13.col_ref, ...), custom_call_target="tpu_custom_call", output_to_operand_aliasing={{0}: (9, {})} | custom-call | tf_op jit(solution)/shard_map/pallas_call | solution.py:102
  64.9 0.7 collective-permute-start.21
  65.6 1.5 %collective-permute-start.22 = (f32[2,1024]{1,0:T(2,128)S(1)}, f32[2,1024]{1,0:T(2,128)S(1)}, u32[]{:S(2)}, u32[]{:S(2)}) collective-permute-start(f32[2,1024]{1,0:T(2,128)S(1)} %get-tuple-element.86), channel_id=1, source_target_pairs={{0,2},{1,3},{2,0},{3,1},{4,6},{5,7},{6,4},{7,5},{8,10},{9,11},{10,... | collective-permute-start | bytes 24584 | tf_op jit(solution)/shard_map/ppermute | solution.py:591
  67.1 2.1 %collective-permute-done.22 = f32[2,1024]{1,0:T(2,128)S(1)} collective-permute-done((f32[2,1024]{1,0:T(2,128)S(1)}, f32[2,1024]{1,0:T(2,128)S(1)}, u32[]{:S(2)}, u32[]{:S(2)}) %collective-permute-start.22) | collective-permute-done | bytes 8224 | tf_op jit(solution)/shard_map/ppermute | solution.py:591
  69.3 1.0 %collective-permute-done.23 = f32[2,1024]{1,0:T(2,128)S(1)} collective-permute-done((f32[2,1024]{1,0:T(2,128)S(1)}, f32[2,1024]{1,0:T(2,128)S(1)}, u32[]{:S(2)}, u32[]{:S(2)}) %collective-permute-start.23) | collective-permute-done | bytes 8224 | tf_op jit(solution)/shard_map/ppermute | solution.py:591
  70.3 0.6 pad_maximum_fusion
  (50 shorter events, 0.2 us)
Async XLA Ops:
  0.6 19.4 %copy-start = (bf16[2,2,2,2,128,256]{5,4,3,2,1,0:T(8,128)(2,1)S(1)}, bf16[2,2,2,2,128,256]{5,4,3,2,1,0:T(8,128)(2,1)}, u32[]{:S(2)}) copy-start(bf16[2,2,2,2,128,256]{5,4,3,2,1,0:T(8,128)(2,1)} %constant.29.clone.rest_4_) | copy-start | bytes 3145732
  0.7 1.3 %copy-start.3 = (f32[4,128,512]{2,1,0:T(8,128)S(1)}, f32[4,128,512]{2,1,0:T(8,128)}, u32[]{:S(2)}) copy-start(f32[4,128,512]{2,1,0:T(8,128)} %image_ref.1) | copy-start | bytes 3145732
  2.0 1.0 %copy-start.4 = (bf16[2,4,128,256]{3,2,1,0:T(8,128)(2,1)S(1)}, bf16[2,4,128,256]{3,2,1,0:T(8,128)(2,1)}, u32[]{:S(2)}) copy-start(bf16[2,4,128,256]{3,2,1,0:T(8,128)(2,1)} %constant.28.clone.table_ref) | copy-start | bytes 1572868
  3.1 0.9 %copy-start.5 = (f32[16,16,16]{2,1,0:T(8,128)S(1)}, f32[16,16,16]{2,1,0:T(8,128)}, u32[]{:S(2)}) copy-start(f32[16,16,16]{2,1,0:T(8,128)} %bank_ref.3) | copy-start | bytes 49156
  4.0 0.8 %copy-start.8 = (f32[16,1024]{1,0:T(8,128)S(1)}, f32[16,1024]{1,0:T(8,128)}, u32[]{:S(2)}) copy-start(f32[16,1024]{1,0:T(8,128)} %constant.27.clone.coef_ref) | copy-start | bytes 196612
  4.8 0.7 copy-start.11
  5.5 0.7 copy-start.12
  6.1 0.7 copy-start.13
  6.8 13.2 %copy-start.14 = (f32[4]{0:T(128)S(1)}, f32[4]{0:T(128)}, u32[]{:S(2)}) copy-start(f32[4]{0:T(128)} %noise_ref.5) | copy-start | bytes 52
  12.7 22.8 %copy-start.6 = (f32[16,16,16]{2,1,0:T(8,128)S(1)}, f32[16,16,16]{2,1,0:T(8,128)}, u32[]{:S(2)}) copy-start(f32[16,16,16]{2,1,0:T(8,128)} %bank_ref.3) | copy-start | bytes 49156
  12.7 22.8 %copy-start.7 = (bf16[2,4,144,32]{3,2,1,0:T(8,128)(2,1)S(1)}, bf16[2,4,144,32]{3,2,1,0:T(8,128)(2,1)}, u32[]{:S(2)}) copy-start(bf16[2,4,144,32]{3,2,1,0:T(8,128)(2,1)} %constant.30.clone.shift_ref) | copy-start | bytes 221188
  12.7 22.8 %copy-start.9 = (f32[16,1024]{1,0:T(8,128)S(1)}, f32[16,1024]{1,0:T(8,128)}, u32[]{:S(2)}) copy-start(f32[16,1024]{1,0:T(8,128)} %constant.27.clone.coef_ref) | copy-start | bytes 196612
  12.7 22.8 %copy-start.10 = (bf16[128,512]{1,0:T(8,128)(2,1)S(1)}, bf16[128,512]{1,0:T(8,128)(2,1)}, u32[]{:S(2)}) copy-start(bf16[128,512]{1,0:T(8,128)(2,1)} %constant.31.clone.spread_ref) | copy-start | bytes 393220
  12.7 3.2 %collective-permute-start = (f32[144,128]{1,0:T(8,128)S(1)}, f32[144,128]{1,0:T(8,128)S(1)}, u32[]{:S(2)}, u32[]{:S(2)}) collective-permute-start(f32[144,128]{1,0:T(8,128)S(1)} %get-tuple-element.51), channel_id=1, source_target_pairs={{0,1},{1,0},{2,3},{3,2},{4,5},{5,4},{6,7},{7,6},{8,9},{9,8},{10,11... | collective-permute-start | bytes 221192 | tf_op jit(solution)/shard_map/ppermute | solution.py:591
  13.2 5.4 %collective-permute-start.1 = (f32[144,128]{1,0:T(8,128)S(1)}, f32[144,128]{1,0:T(8,128)S(1)}, u32[]{:S(2)}, u32[]{:S(2)}) collective-permute-start(f32[144,128]{1,0:T(8,128)S(1)} %get-tuple-element.52), channel_id=1, source_target_pairs={{0,2},{1,3},{2,0},{3,1},{4,6},{5,7},{6,4},{7,5},{8,10},{9,11},{10,... | collective-permute-start | bytes 221192 | tf_op jit(solution)/shard_map/ppermute | solution.py:591
  15.8 4.2 %collective-permute-start.2 = (f32[144,128]{1,0:T(8,128)S(1)}, f32[144,128]{1,0:T(8,128)S(1)}, u32[]{:S(2)}, u32[]{:S(2)}) collective-permute-start(f32[144,128]{1,0:T(8,128)S(1)} %get-tuple-element.53), channel_id=1, source_target_pairs={{0,3},{1,2},{2,1},{3,0},{4,7},{5,6},{6,5},{7,4},{8,11},{9,10},{10,... | collective-permute-start | bytes 221192 | tf_op jit(solution)/shard_map/ppermute | solution.py:591
  21.2 6.0 %collective-permute-start.6 = (f32[136,128]{1,0:T(8,128)S(1)}, f32[136,128]{1,0:T(8,128)S(1)}, u32[]{:S(2)}, u32[]{:S(2)}) collective-permute-start(f32[136,128]{1,0:T(8,128)S(1)} %get-tuple-element.63), channel_id=1, source_target_pairs={{0,4},{4,0},{8,12},{12,8},{1,5},{5,1},{9,13},{13,9},{2,6},{6,2},{1... | collective-permute-start | bytes 208904 | tf_op jit(solution)/shard_map/ppermute | solution.py:591
  23.1 7.8 %collective-permute-start.7 = (f32[136,128]{1,0:T(8,128)S(1)}, f32[136,128]{1,0:T(8,128)S(1)}, u32[]{:S(2)}, u32[]{:S(2)}) collective-permute-start(f32[136,128]{1,0:T(8,128)S(1)} %get-tuple-element.64), channel_id=1, source_target_pairs={{0,8},{4,12},{8,0},{12,4},{1,9},{5,13},{9,1},{13,5},{2,10},{6,14},... | collective-permute-start | bytes 208904 | tf_op jit(solution)/shard_map/ppermute | solution.py:591
  25.7 6.2 %collective-permute-start.8 = (f32[136,128]{1,0:T(8,128)S(1)}, f32[136,128]{1,0:T(8,128)S(1)}, u32[]{:S(2)}, u32[]{:S(2)}) collective-permute-start(f32[136,128]{1,0:T(8,128)S(1)} %get-tuple-element.65), channel_id=1, source_target_pairs={{0,12},{4,8},{8,4},{12,0},{1,13},{5,9},{9,5},{13,1},{2,14},{6,10},... | collective-permute-start | bytes 208904 | tf_op jit(solution)/shard_map/ppermute | solution.py:591
  25.7 9.8 %collective-permute-start.3 = (f32[128,512]{1,0:T(8,128)S(1)}, f32[128,512]{1,0:T(8,128)S(1)}, u32[]{:S(2)}, u32[]{:S(2)}) collective-permute-start(f32[128,512]{1,0:T(8,128)S(1)} %get-tuple-element.59), channel_id=1, source_target_pairs={{0,1},{1,0},{2,3},{3,2},{4,5},{5,4},{6,7},{7,6},{8,9},{9,8},{10,11... | collective-permute-start | bytes 786440 | tf_op jit(solution)/shard_map/ppermute | solution.py:591
  25.7 13.3 %collective-permute-start.4 = (f32[128,512]{1,0:T(8,128)S(1)}, f32[128,512]{1,0:T(8,128)S(1)}, u32[]{:S(2)}, u32[]{:S(2)}) collective-permute-start(f32[128,512]{1,0:T(8,128)S(1)} %get-tuple-element.60), channel_id=1, source_target_pairs={{0,2},{1,3},{2,0},{3,1},{4,6},{5,7},{6,4},{7,5},{8,10},{9,11},{10,... | collective-permute-start | bytes 786440 | tf_op jit(solution)/shard_map/ppermute | solution.py:591
  27.1 12.5 %collective-permute-start.5 = (f32[128,512]{1,0:T(8,128)S(1)}, f32[128,512]{1,0:T(8,128)S(1)}, u32[]{:S(2)}, u32[]{:S(2)}) collective-permute-start(f32[128,512]{1,0:T(8,128)S(1)} %get-tuple-element.61), channel_id=1, source_target_pairs={{0,3},{1,2},{2,1},{3,0},{4,7},{5,6},{6,5},{7,4},{8,11},{9,10},{10,... | collective-permute-start | bytes 786440 | tf_op jit(solution)/shard_map/ppermute | solution.py:591
  31.9 9.6 %collective-permute-start.10 = (f32[136,128]{1,0:T(8,128)S(1)}, f32[136,128]{1,0:T(8,128)S(1)}, u32[]{:S(2)}, u32[]{:S(2)}) collective-permute-start(f32[136,128]{1,0:T(8,128)S(1)} %add_add_fusion.share_ref.rest_0_), channel_id=1, source_target_pairs={{0,8},{4,12},{8,0},{12,4},{1,9},{5,13},{9,1},{13,5},{2,10},{6,14},... | collective-permute-start | bytes 208904 | tf_op jit(solution)/shard_map/ppermute | solution.py:591
  34.0 7.5 %collective-permute-start.11 = (f32[136,128]{1,0:T(8,128)S(1)}, f32[136,128]{1,0:T(8,128)S(1)}, u32[]{:S(2)}, u32[]{:S(2)}) collective-permute-start(f32[136,128]{1,0:T(8,128)S(1)} %add_add_fusion.share_ref.rest_0_), channel_id=1, source_target_pairs={{0,12},{4,8},{8,4},{12,0},{1,13},{5,9},{9,5},{13,1},{2,14},{6,10},... | collective-permute-start | bytes 208904 | tf_op jit(solution)/shard_map/ppermute | solution.py:591
  35.4 6.0 %collective-permute-start.9 = (f32[136,128]{1,0:T(8,128)S(1)}, f32[136,128]{1,0:T(8,128)S(1)}, u32[]{:S(2)}, u32[]{:S(2)}) collective-permute-start(f32[136,128]{1,0:T(8,128)S(1)} %add_add_fusion.share_ref.rest_0_), channel_id=1, source_target_pairs={{0,4},{4,0},{8,12},{12,8},{1,5},{5,1},{9,13},{13,9},{2,6},{6,2},{1... | collective-permute-start | bytes 208904 | tf_op jit(solution)/shard_map/ppermute | solution.py:591
  39.0 2.5 %copy-start.1 = (bf16[2,2,256,512]{3,2,1,0:T(8,128)(2,1)S(1)}, bf16[2,2,256,512]{3,2,1,0:T(8,128)(2,1)}, u32[]{:S(2)}) copy-start(bf16[2,2,256,512]{3,2,1,0:T(8,128)(2,1)} %constant.32.clone.rest_4_) | copy-start | bytes 3145732
  42.9 5.6 %collective-permute-start.15 = (f32[2,144,128]{2,1,0:T(8,128)S(1)}, f32[2,144,128]{2,1,0:T(8,128)S(1)}, u32[]{:S(2)}, u32[]{:S(2)}) collective-permute-start(f32[2,144,128]{2,1,0:T(8,128)S(1)} %get-tuple-element.75), channel_id=1, source_target_pairs={{0,1},{1,0},{2,3},{3,2},{4,5},{5,4},{6,7},{7,6},{8,9},{9,8},{10,11... | collective-permute-start | bytes 442376 | tf_op jit(solution)/shard_map/ppermute | solution.py:591
  43.4 6.7 %collective-permute-start.16 = (f32[2,144,128]{2,1,0:T(8,128)S(1)}, f32[2,144,128]{2,1,0:T(8,128)S(1)}, u32[]{:S(2)}, u32[]{:S(2)}) collective-permute-start(f32[2,144,128]{2,1,0:T(8,128)S(1)} %get-tuple-element.76), channel_id=1, source_target_pairs={{0,2},{1,3},{2,0},{3,1},{4,6},{5,7},{6,4},{7,5},{8,10},{9,11},{10,... | collective-permute-start | bytes 442376 | tf_op jit(solution)/shard_map/ppermute | solution.py:591
  44.9 3.6 %copy-start.15 = (s32[4096]{0:T(1024)S(1)}, s32[4096]{0:T(1024)}, u32[]{:S(2)}) copy-start(s32[4096]{0:T(1024)} %param.19) | copy-start | bytes 49156
  44.9 3.6 %copy-start.16 = (s32[4096]{0:T(1024)S(1)}, s32[4096]{0:T(1024)}, u32[]{:S(2)}) copy-start(s32[4096]{0:T(1024)} %param.20) | copy-start | bytes 49156
  44.9 7.4 %copy-start.2 = (bf16[2,4,128,256]{3,2,1,0:T(8,128)(2,1)S(1)}, bf16[2,4,128,256]{3,2,1,0:T(8,128)(2,1)}, u32[]{:S(2)}) copy-start(bf16[2,4,128,256]{3,2,1,0:T(8,128)(2,1)} %constant.33.clone.rest_4_) | copy-start | bytes 1572868
  44.9 7.4 %collective-permute-start.17 = (f32[2,144,128]{2,1,0:T(8,128)S(1)}, f32[2,144,128]{2,1,0:T(8,128)S(1)}, u32[]{:S(2)}, u32[]{:S(2)}) collective-permute-start(f32[2,144,128]{2,1,0:T(8,128)S(1)} %get-tuple-element.77), channel_id=1, source_target_pairs={{0,3},{1,2},{2,1},{3,0},{4,7},{5,6},{6,5},{7,4},{8,11},{9,10},{10,... | collective-permute-start | bytes 442376 | tf_op jit(solution)/shard_map/ppermute | solution.py:591
  46.3 13.8 %collective-permute-start.12 = (f32[2,144,128]{2,1,0:T(8,128)S(1)}, f32[2,144,128]{2,1,0:T(8,128)S(1)}, u32[]{:S(2)}, u32[]{:S(2)}) collective-permute-start(f32[2,144,128]{2,1,0:T(8,128)S(1)} %get-tuple-element.71), channel_id=1, source_target_pairs={{0,1},{1,0},{2,3},{3,2},{4,5},{5,4},{6,7},{7,6},{8,9},{9,8},{10,11... | collective-permute-start | bytes 442376 | tf_op jit(solution)/shard_map/ppermute | solution.py:591
  47.0 13.0 %collective-permute-start.13 = (f32[2,144,128]{2,1,0:T(8,128)S(1)}, f32[2,144,128]{2,1,0:T(8,128)S(1)}, u32[]{:S(2)}, u32[]{:S(2)}) collective-permute-start(f32[2,144,128]{2,1,0:T(8,128)S(1)} %get-tuple-element.72), channel_id=1, source_target_pairs={{0,2},{1,3},{2,0},{3,1},{4,6},{5,7},{6,4},{7,5},{8,10},{9,11},{10,... | collective-permute-start | bytes 442376 | tf_op jit(solution)/shard_map/ppermute | solution.py:591
  48.5 11.6 %collective-permute-start.14 = (f32[2,144,128]{2,1,0:T(8,128)S(1)}, f32[2,144,128]{2,1,0:T(8,128)S(1)}, u32[]{:S(2)}, u32[]{:S(2)}) collective-permute-start(f32[2,144,128]{2,1,0:T(8,128)S(1)} %get-tuple-element.73), channel_id=1, source_target_pairs={{0,3},{1,2},{2,1},{3,0},{4,7},{5,6},{6,5},{7,4},{8,11},{9,10},{10,... | collective-permute-start | bytes 442376 | tf_op jit(solution)/shard_map/ppermute | solution.py:591
  57.7 9.4 %collective-permute-start.18 = (f32[2,1024]{1,0:T(2,128)S(1)}, f32[2,1024]{1,0:T(2,128)S(1)}, u32[]{:S(2)}, u32[]{:S(2)}) collective-permute-start(f32[2,1024]{1,0:T(2,128)S(1)} %get-tuple-element.81), channel_id=1, source_target_pairs={{0,1},{1,0},{2,3},{3,2},{4,5},{5,4},{6,7},{7,6},{8,9},{9,8},{10,11... | collective-permute-start | bytes 24584 | tf_op jit(solution)/shard_map/ppermute | solution.py:591
  58.6 8.6 %collective-permute-start.19 = (f32[2,1024]{1,0:T(2,128)S(1)}, f32[2,1024]{1,0:T(2,128)S(1)}, u32[]{:S(2)}, u32[]{:S(2)}) collective-permute-start(f32[2,1024]{1,0:T(2,128)S(1)} %get-tuple-element.82), channel_id=1, source_target_pairs={{0,2},{1,3},{2,0},{3,1},{4,6},{5,7},{6,4},{7,5},{8,10},{9,11},{10,... | collective-permute-start | bytes 24584 | tf_op jit(solution)/shard_map/ppermute | solution.py:591
  60.0 7.1 %collective-permute-start.20 = (f32[2,1024]{1,0:T(2,128)S(1)}, f32[2,1024]{1,0:T(2,128)S(1)}, u32[]{:S(2)}, u32[]{:S(2)}) collective-permute-start(f32[2,1024]{1,0:T(2,128)S(1)} %get-tuple-element.83), channel_id=1, source_target_pairs={{0,3},{1,2},{2,1},{3,0},{4,7},{5,6},{6,5},{7,4},{8,11},{9,10},{10,... | collective-permute-start | bytes 24584 | tf_op jit(solution)/shard_map/ppermute | solution.py:591
  64.9 2.2 %collective-permute-start.21 = (f32[2,1024]{1,0:T(2,128)S(1)}, f32[2,1024]{1,0:T(2,128)S(1)}, u32[]{:S(2)}, u32[]{:S(2)}) collective-permute-start(f32[2,1024]{1,0:T(2,128)S(1)} %get-tuple-element.85), channel_id=1, source_target_pairs={{0,1},{1,0},{2,3},{3,2},{4,5},{5,4},{6,7},{7,6},{8,9},{9,8},{10,11... | collective-permute-start | bytes 24584 | tf_op jit(solution)/shard_map/ppermute | solution.py:591
  65.6 3.7 %collective-permute-start.22 = (f32[2,1024]{1,0:T(2,128)S(1)}, f32[2,1024]{1,0:T(2,128)S(1)}, u32[]{:S(2)}, u32[]{:S(2)}) collective-permute-start(f32[2,1024]{1,0:T(2,128)S(1)} %get-tuple-element.86), channel_id=1, source_target_pairs={{0,2},{1,3},{2,0},{3,1},{4,6},{5,7},{6,4},{7,5},{8,10},{9,11},{10,... | collective-permute-start | bytes 24584 | tf_op jit(solution)/shard_map/ppermute | solution.py:591
  67.1 3.1 %collective-permute-start.23 = (f32[2,1024]{1,0:T(2,128)S(1)}, f32[2,1024]{1,0:T(2,128)S(1)}, u32[]{:S(2)}, u32[]{:S(2)}) collective-permute-start(f32[2,1024]{1,0:T(2,128)S(1)} %get-tuple-element.87), channel_id=1, source_target_pairs={{0,3},{1,2},{2,1},{3,0},{4,7},{5,6},{6,5},{7,4},{8,11},{9,10},{10,... | collective-permute-start | bytes 24584 | tf_op jit(solution)/shard_map/ppermute | solution.py:591
where the time goes:
time: 71.1 us; the launch traced here: 70.9 us
  Pallas kernels  25.2 us (35%)
  starting transfers between devices  21.9 us (31%)
  waiting for transfers between devices  16 us (23%)
  local copies, waits for them, and re-layouts  6.11 us (9%)
  between operations  0.89 us (1%)
  other arithmetic  0.74 us (1%)
    pallas_call x9, Pallas kernels, call(): pl.pallas_call(kernel, out_shape=tuple((jax.ShapeDtypeStruct(shape, f32)...  25.2 us
    ppermute x24, starting transfers between devices, trade(): result[m] = lax.ppermute(parts[m], axes, [(i, i ^ m) for i in range(count)])  21.9 us
    ppermute x24, waiting for transfers between devices, trade(): result[m] = lax.ppermute(parts[m], axes, [(i, i ^ m) for i in range(count)])  16 us
    unnamed x34, local copies, waits for them, and re-layouts  6.1 us
  transfers between devices with their start and end apart: 24, of which 9 were waited for; matrix products, arithmetic and copies ran while one was open for 0% of the time, Pallas kernels for 24%

commit v1 on v0

--- a/solution.py
+++ b/solution.py
@@ -12,6 +12,7 @@
 reg_floor = 0.01
 vmem_limit = 40 * 1024 * 1024
 bf16, f32 = jnp.bfloat16, jnp.float32
+hbm_rate = 3.69e6
 edge_rows = 16
 
 
@@ -97,17 +98,21 @@
         self.spread = np.concatenate([high, high, low, np.zeros_like(high)], 0)
 
 
-def call(kernel, outs, ins, scratch=(), aliases=None):
+def call(kernel, outs, ins, scratch=(), aliases=None, micros=0.0):
     space = {"s": pltpu.SMEM, "v": pltpu.VMEM, "h": pl.ANY, "m": pltpu.HBM}
+    ins = [
+        (kind, pltpu.with_memory_space_constraint(jnp.asarray(a), pltpu.HBM) if kind == "m" else a)
+        for kind, a in ins
+    ]
     return pl.pallas_call(
         kernel,
-        out_shape=tuple(jax.ShapeDtypeStruct(shape, f32) for _, shape in outs),
+        out_shape=tuple(jax.ShapeDtypeStruct(shape, (*kind, f32)[0]) for _, shape, *kind in outs),
         in_specs=[pl.BlockSpec(memory_space=space[kind]) for kind, _ in ins],
-        out_specs=tuple(pl.BlockSpec(memory_space=space[kind]) for kind, _ in outs),
+        out_specs=tuple(pl.BlockSpec(memory_space=space[out[0]]) for out in outs),
         scratch_shapes=list(scratch),
         input_output_aliases=aliases or {},
         compiler_params=pltpu.CompilerParams(vmem_limit_bytes=vmem_limit),
-        cost_estimate=pl.CostEstimate(flops=0, bytes_accessed=0, transcendentals=0),
+        cost_estimate=pl.CostEstimate(flops=0, bytes_accessed=int(micros * hbm_rate), transcendentals=0),
     )(*[a for _, a in ins])
 
 
@@ -132,80 +137,128 @@
     return jnp.concatenate([value[:, plan.cols :], value[:, : plan.cols]], 1)
 
 
-def row_transform(plan, place, index, flux, noise, images, bank):
-    epochs, rows, side = images.shape
-    width = epochs * rows
-    half, slabs, pairs, lanes, tall, stamp = (
-        plan.half, plan.slabs, plan.pairs, plan.lanes, plan.tall, plan.stamp,
-    )
+def owners_of(plan, q, group):
+    return [q ^ (group * plan.pairs + m) for m in range(plan.pairs)]
+
+
+def row_operands(plan, q, group, x_ref, table_ref):
+    half = plan.half
+    x = x_ref[...].reshape(-1, 2 * half)
+    first, second = x[:, :half], x[:, half:]
+    sign = jnp.where((q >= plan.pairs) != (group == 1), -1.0, 1.0).astype(f32)
+    data = split(first + sign * second)
+    table = [
+        jnp.concatenate([table_ref[n, d] for d in owners_of(plan, q, group)], 0) for n in range(2)
+    ]
+    return data, table
+
+
+def coadd_rows(plan, q, group, x_ref, table_ref, taps_ref, padded, gathered, outs):
+    rows, lanes, tall, stamp, pairs = plan.rows, plan.lanes, plan.tall, plan.stamp, plan.pairs
+    epochs = x_ref.shape[0]
     step = tall // 2
-
-    def kernel(place_ref, index_ref, flux_ref, noise_ref, bank_ref, coef_ref, image_ref, table_ref, *rest):
-        outs, numers = rest[:slabs], rest[slabs : 2 * slabs]
-        x_ref, both_ref, taps_ref, padded, gathered, sems = rest[2 * slabs :]
-        copies = [
-            pltpu.make_async_copy(image_ref, x_ref, sems.at[0]),
-            pltpu.make_async_copy(table_ref, both_ref, sems.at[1]),
-        ]
+    padded[:, :, :stamp] = jnp.zeros((pairs, epochs, stamp, lanes), f32)
+    padded[:, :, stamp + rows :] = jnp.zeros((pairs, epochs, stamp, lanes), f32)
+    data, table = row_operands(plan, q, group, x_ref, table_ref)
+    upright = mul3(data, table, True)
+    for m in range(pairs):
+        for e in range(epochs):
+            padded[m, e, stamp : stamp + rows] = upright[
+                e * rows : (e + 1) * rows, m * lanes : (m + 1) * lanes
+            ]
+
+    @pl.loop(0, pairs)
+    def _(m):
+        d = q ^ (group * pairs + m)
+        for start in range(0, tall, step):
+            straight = jnp.zeros((step, lanes), f32)
+            crossed = jnp.zeros((step, lanes), f32)
+            for e in range(epochs):
+                for a in range(stamp):
+                    value = padded[m, e, start + a : start + a + step, :]
+                    at = e * stamp + a
+                    straight += taps_ref[0, d, at : at + 1] * value
+                    crossed += taps_ref[1, d, at : at + 1] * value
+            gathered[m, start : start + step] = straight + swap_halves(plan, crossed)
+
+    for m in range(pairs):
+        outs[m][...] = gathered[m]
+
+
+def coadd_scratch(plan, epochs):
+    return [
+        pltpu.VMEM((plan.pairs, epochs, plan.rows + 2 * plan.stamp, plan.lanes), f32),
+        pltpu.VMEM((plan.pairs, plan.tall, plan.lanes), f32),
+    ]
+
+
+def row_transform_far(plan, place, index, flux, noise, images, bank):
+    epochs = images.shape[0]
+    slabs, pairs, lanes, tall, stamp = plan.slabs, plan.pairs, plan.lanes, plan.tall, plan.stamp
+
+    def kernel(place_ref, *rest):
+        sources, outs, rest = rest[:7], rest[7 : 7 + pairs], rest[7 + pairs :]
+        taps_ref, x_ref, table_ref, index_ref, flux_ref, noise_ref, bank_ref, coef_ref = rest[:8]
+        padded, gathered, sems = rest[8:]
+        targets = [index_ref, flux_ref, noise_ref, bank_ref, coef_ref, x_ref, table_ref]
+        copies = [pltpu.make_async_copy(sources[i], targets[i], sems.at[i]) for i in range(7)]
         for copy in copies:
             copy.start()
+        for copy in copies[:5]:
+            copy.wait()
         filter_taps(
             plan, bank_ref, coef_ref, index_ref, epochs,
             lambda e, own: own * (flux_ref[e] / (noise_ref[e] * noise_ref[e])), taps_ref,
         )
-        padded[:, :, :stamp] = jnp.zeros((slabs, epochs, stamp, lanes), f32)
-        padded[:, :, stamp + rows :] = jnp.zeros((slabs, epochs, stamp, lanes), f32)
-        for copy in copies:
+        for copy in copies[5:]:
             copy.wait()
-        q = place_ref[0]
-        x = x_ref[...].reshape(width, side)
-        first, second = x[:, :half], x[:, half:]
-        total = first + second
-        change = first - second
-        flag = jnp.broadcast_to((q >= pairs).astype(jnp.int32), (1, 1)) > 0
+        coadd_rows(plan, place_ref[0], 1, x_ref, table_ref, taps_ref, padded, gathered, outs)
+
+    flat = call(
+        kernel,
+        [("v", (tall, lanes))] * pairs
+        + [("v", (2, slabs, epochs * stamp, lanes)), ("v", images.shape), ("v", plan.ahead.shape, bf16)],
+        [("s", place), ("m", index), ("m", flux), ("m", noise), ("m", bank), ("m", plan.coef),
+         ("m", images), ("m", plan.ahead)],
+        [pltpu.SMEM(index.shape, jnp.int32), pltpu.SMEM(flux.shape, f32), pltpu.SMEM(noise.shape, f32),
+         pltpu.VMEM(bank.shape, f32), pltpu.VMEM(plan.coef.shape, f32)]
+        + coadd_scratch(plan, epochs) + [pltpu.SemaphoreType.DMA((7,))],
+        micros=4.5,
+    )
+    return list(flat[:pairs]), *flat[pairs:]
+
+
+def row_transform_near(plan, place, taps, images, table):
+    pairs = plan.pairs
+
+    def kernel(place_ref, taps_ref, x_ref, table_ref, *rest):
+        coadd_rows(plan, place_ref[0], 0, x_ref, table_ref, taps_ref, *rest[pairs:], rest[:pairs])
+
+    return list(call(
+        kernel,
+        [("v", (plan.tall, plan.lanes))] * pairs,
+        [("s", place), ("v", taps), ("v", images), ("v", table)],
+        coadd_scratch(plan, images.shape[0]),
+        micros=3.2,
+    ))
+
+
+def row_transform(plan, place, images, table):
+    slabs, pairs, lanes = plan.slabs, plan.pairs, plan.lanes
+
+    def kernel(place_ref, x_ref, table_ref, *outs):
         for group in range(2):
-            pick = flag if group == 0 else jnp.logical_not(flag)
-            data = split(jnp.where(pick, change, total))
-            owners = [q ^ (group * pairs + m) for m in range(pairs)]
-            table = [jnp.concatenate([both_ref[n, d] for d in owners], 0) for n in range(2)]
-            upright = mul3(data, table, True)
+            data, table = row_operands(plan, place_ref[0], group, x_ref, table_ref)
             result = mul3(table, data, True)
             for m in range(pairs):
-                here = slice(m * lanes, (m + 1) * lanes)
-                outs[group * pairs + m][...] = result[here]
-                for e in range(epochs):
-                    padded[group * pairs + m, e, stamp : stamp + rows] = upright[
-                        e * rows : (e + 1) * rows, here
-                    ]
-
-        @pl.loop(0, slabs)
-        def _(m):
-            d = q ^ m
-            for start in range(0, tall, step):
-                straight = jnp.zeros((step, lanes), f32)
-                crossed = jnp.zeros((step, lanes), f32)
-                for e in range(epochs):
-                    for a in range(stamp):
-                        value = padded[m, e, start + a : start + a + step, :]
-                        at = e * stamp + a
-                        straight += taps_ref[0, d, at : at + 1] * value
-                        crossed += taps_ref[1, d, at : at + 1] * value
-                gathered[m, start : start + step] = straight + swap_halves(plan, crossed)
-
-        for m in range(slabs):
-            numers[m][...] = gathered[m]
-
-    flat = call(
-        kernel,
-        [("v", (lanes, width))] * slabs + [("v", (tall, lanes))] * slabs,
-        [("s", place), ("s", index), ("s", flux), ("s", noise), ("v", bank), ("v", plan.coef),
-         ("m", images), ("m", plan.ahead)],
-        [pltpu.VMEM(images.shape, f32), pltpu.VMEM(plan.ahead.shape, bf16),
-         pltpu.VMEM((2, slabs, epochs * stamp, lanes), f32),
-         pltpu.VMEM((slabs, epochs, rows + 2 * stamp, lanes), f32),
-         pltpu.VMEM((slabs, tall, lanes), f32), pltpu.SemaphoreType.DMA((2,))],
-    )
-    return list(flat[:slabs]), list(flat[slabs:])
+                outs[group * pairs + m][...] = result[m * lanes : (m + 1) * lanes]
+
+    return list(call(
+        kernel,
+        [("v", (lanes, images.shape[0] * plan.rows))] * slabs,
+        [("s", place), ("v", images), ("v", table)],
+        micros=1.3,
+    ))
 
 
 def numerator(plan, place, index, flux, noise, blocks, pieces):
@@ -223,7 +276,7 @@
         whole[...] = jnp.zeros((side + 2 * halo, lanes), f32)
         for m in range(slabs):
             at = pl.multiple_of((q ^ m) * rows, rows)
-            whole[pl.ds(at, tall)] += ins[m][...]
+            whole[pl.ds(at, tall)] += ins[slabs - 1 - m][...]
         whole[side : side + halo] += whole[:halo]
         whole[halo : 2 * halo] += whole[side + halo :]
         top, bottom = whole[halo : halo + half], whole[halo + half : halo + side]
@@ -265,9 +318,10 @@
     return call(
         kernel,
         [("v", (lanes + 8, piece))] * pieces,
-        [("s", place), ("s", index), ("s", flux), ("s", noise)] + [("v", b) for b in blocks]
+        [("s", place), ("s", index), ("s", flux), ("s", noise)] + [("v", b) for b in reversed(blocks)]
         + [("v", plan.down)],
         [pltpu.VMEM((side + 2 * halo, lanes), f32), pltpu.VMEM((pieces, lanes + 8, piece), f32)],
+        micros=1.15,
     )
 
 
@@ -323,6 +377,7 @@
         [("v", (2 * size, side)), ("v", (count, band, side)), ("v", (2, slabs, epochs * stamp, lanes))],
         [("s", place), ("s", index), ("v", bank), ("v", plan.shift), ("v", plan.spread), ("v", plan.coef)],
         [pltpu.VMEM((count * pitch, 2 * stamp), f32), pltpu.VMEM((count, 2 * band, side), f32)],
+        micros=2.35,
     )
 
 
@@ -366,6 +421,7 @@
         kernel,
         [("v", (size, side)), ("v", (2 * size, side))],
         [("s", flux), ("s", noise), ("v", share), ("v", spectrum), ("v", power)],
+        micros=1.15,
     )
 
 
@@ -419,6 +475,7 @@
         [("v", (2 * size, side))],
         [("s", place)] + [("v", b) for b in blocks] + [("v", plan.down)],
         [pltpu.VMEM((2 * size, side), bf16), pltpu.VMEM((2 * size, side), bf16)],
+        micros=1.85,
     )
     return plane
 
@@ -495,10 +552,11 @@
         [pltpu.VMEM((pieces, lanes + 8, piece), f32),
          pltpu.VMEM((epochs * lanes, side), bf16), pltpu.VMEM((epochs * lanes, side), bf16),
          pltpu.VMEM((side + 2 * halo, epochs * lanes), f32)],
-    )
-
-
-def row_inverse(plan, place, blocks, taps, begin, epochs, difference, src_row, src_col):
+        micros=1.35,
+    )
+
+
+def row_inverse(plan, place, blocks, taps, begin, epochs, difference, earlier, src_row, src_col):
     slabs, pairs, rows, half, side, lanes, halo, stamp = (
         plan.slabs, plan.pairs, plan.rows, plan.half, plan.side, plan.lanes, plan.halo, plan.stamp,
     )
@@ -507,12 +565,17 @@
     each = groups // slabs
     total = mine * rows
     step = min(64, rows)
+    last = begin + mine == epochs
+    count = slabs if last else 1
+    flux_shapes = [("v", (epochs, each * group))] * slabs if last else [("v", (slabs, begin + mine, each * group))]
 
     def kernel(place_ref, row_ref, col_ref, taps_ref, *rest):
         ins, table_ref = rest[:slabs], rest[slabs]
-        rest = rest[slabs + 1 + (difference is not None) :]
-        diff_ref, outs = rest[0], rest[1 : 1 + slabs]
-        left_high, left_low, image_ref, flux_ref, picked, sem = rest[1 + slabs :]
+        rest = rest[slabs + 1 :]
+        if difference is not None:
+            earlier_ref, rest = rest[1], rest[2:]
+        diff_ref, outs = rest[0], rest[1 : 1 + count]
+        left_high, left_low, image_ref, flux_ref, picked, sem = rest[1 + count :]
         q = place_ref[0]
         for m in range(slabs):
             d = q ^ m
@@ -565,7 +628,11 @@
             where = (g % each) * group
             picked[g // each, :, where : where + group] = jnp.concatenate(found, 0)
         for m in range(slabs):
-            outs[m][...] = picked[q ^ m]
+            out = outs[m] if last else outs[0].at[m]
+            owner = q ^ m if last else m
+            if begin:
+                out[:begin] = earlier_ref[owner]
+            out[begin:] = picked[owner]
         copy.wait()
 
     ins = [("s", place), ("v", src_row), ("v", src_col), ("v", taps)]
@@ -573,15 +640,16 @@
     aliases = {}
     if difference is not None:
         aliases = {len(ins): 0}
-        ins.append(("h", difference))
+        ins += [("h", difference), ("v", earlier)]
     left = pltpu.VMEM((2 * total, side), bf16)
     return call(
         kernel,
-        [("h", (epochs, rows, side))] + [("v", (mine, each * group))] * slabs,
+        [("h", (epochs, rows, side))] + flux_shapes,
         ins,
         [left, left, pltpu.VMEM((mine, rows, side), f32), left,
          pltpu.VMEM((slabs, mine, each * group), f32), pltpu.SemaphoreType.DMA(())],
         aliases=aliases,
+        micros=5.4,
     )
 
 
@@ -603,16 +671,17 @@
         place = jnp.stack([lax.axis_index(slab_axes), lax.axis_index("epoch")]).astype(jnp.int32)
         direct = ranks & (ranks - 1) == 0 and side // ranks % 128 == 0
         pieces = ranks if direct else 1
-        parties = 2 if epochs % 2 == 0 else 1
         group = math.gcd(512, src_row.shape[0] // slabs)
         scalars = (psf_index, flux_scale, noise_level)
 
-        blocks, numer = row_transform(plan, place, *scalars, epoch_images, psf_bank)
-        numer = trade(numer, slab_axes, slabs)
+        far, weighted, images, table = row_transform_far(plan, place, *scalars, epoch_images, psf_bank)
+        near = row_transform_near(plan, place, weighted, images, table)
+        blocks = row_transform(plan, place, images, table)
+        numer = trade(near + far, slab_axes, slabs)
         numer = numerator(plan, place, *scalars, numer, pieces)
-        blocks, numer = lax.optimization_barrier((blocks, numer))
+        bank, numer = lax.optimization_barrier((psf_bank, numer))
+        spectrum, power, taps = psf_planes(plan, place, bank, psf_index)
         blocks = trade(blocks, slab_axes, slabs)
-        spectrum, power, taps = psf_planes(plan, place, psf_bank, psf_index)
         if direct:
             own = sum(trade(numer, "epoch", ranks))
             numer = trade([own] * ranks, "epoch", ranks)
@@ -622,22 +691,23 @@
         images = column_transform(plan, place, blocks)
         gain, cross = filter_gains(plan, flux_scale, noise_level, own, spectrum, power)
 
-        difference, fluxes = None, []
-        each = epochs // parties
+        parties = [0]
+        while parties[-1] < epochs:
+            parties.append(min(parties[-1] + 2, epochs))
+        parties = list(zip(parties, parties[1:]))
         returned = [
             trade(
-                column_inverse(plan, place, images, gain, cross, numer, i * each, (i + 1) * each),
-                slab_axes, slabs,
+                column_inverse(plan, place, images, gain, cross, numer, begin, end), slab_axes, slabs
             )
-            for i in range(parties)
+            for begin, end in parties
         ]
-        for i in range(parties):
+        difference, picked = None, [None]
+        for i, (begin, _) in enumerate(parties):
             difference, *picked = row_inverse(
-                plan, place, returned[i], taps, i * each, epochs, difference,
+                plan, place, returned[i], taps, begin, epochs, difference, picked[0],
                 src_row.reshape(-1, group), src_col.reshape(-1, group),
             )
-            fluxes.append(sum(trade(picked, slab_axes, slabs)))
-        return difference, jnp.concatenate(fluxes, 0)
+        return difference, sum(trade(picked, slab_axes, slabs))
 
     return shards
 

time: 71.1 us -> 63.9 us (0.90)
  local copies, waits for them, and re-layouts: 6.11 us -> 0.08 us
  Pallas kernels: 25.2 us -> 28.9 us
  waiting for transfers between devices: 16 us -> 12.7 us
  starting transfers between devices: 21.9 us -> 20.4 us
    unnamed x34 -> x24, local copies, waits for them, and re-layouts: 6.1 us -> 0.07 us
    pallas_call x9 -> x11, Pallas kernels: 25.2 us -> 28.9 us  [call(): pl.pallas_call(kernel, out_shape=tuple((jax.ShapeDtypeStruct(shape, (*kin...]
    ppermute x24 -> x21, waiting for transfers between devices: 16 us -> 12.7 us  [trade(): result[m] = lax.ppermute(parts[m], axes, [(i, i ^ m) for i in range(count)])]
    ppermute x24 -> x21, starting transfers between devices: 21.9 us -> 20.4 us  [trade(): result[m] = lax.ppermute(parts[m], axes, [(i, i ^ m) for i in range(count)])]
  transfers between devices with their start and end apart: 24 -> 21, of which waited for: 9 -> 9; matrix products, arithmetic and copies ran while one was open for 0% -> 0% of each run, Pallas kernels for 24% -> 26%
where the time goes in v1:
time: 63.9 us; the launch traced here: 63.7 us
  Pallas kernels  28.9 us (45%)
  starting transfers between devices  20.4 us (32%)
  waiting for transfers between devices  12.7 us (20%)
  between operations  0.91 us (1%)
  other arithmetic  0.71 us (1%)
    pallas_call x11, Pallas kernels, call(): pl.pallas_call(kernel, out_shape=tuple((jax.ShapeDtypeStruct(shape, (*kin...  28.9 us
    ppermute x21, starting transfers between devices, trade(): result[m] = lax.ppermute(parts[m], axes, [(i, i ^ m) for i in range(count)])  20.4 us
    ppermute x21, waiting for transfers between devices, trade(): result[m] = lax.ppermute(parts[m], axes, [(i, i ^ m) for i in range(count)])  12.7 us
  transfers between devices with their start and end apart: 21, of which 9 were waited for; matrix products, arithmetic and copies ran while one was open for 0% of the time, Pallas kernels for 26%

profile of v1, /device:TPU:0, one launch (start us, length us, event | category | flops | bytes accessed | tf_op | source)
XLA Modules:
  0.0 63.7 jit_solution(2234722159652451505)
XLA Ops:
  0.6 0.1 pad_add_fusion.place_ref
  0.7 4.5 %shard_map.149 = (f32[144,128]{1,0:T(8,128)S(1)}, f32[144,128]{1,0:T(8,128)S(1)}, f32[2,4,64,128]{3,2,1,0:T(8,128)S(1)}, f32[4,128,512]{2,1,0:T(8,128)S(1)}, bf16[2,4,128,256]{3,2,1,0:T(8,128)(2,1)S(1)}) custom-call(s32[2]{0:T(128)S(1)} %pad_add_fusion.place_ref, s32[4]{0:T(128)} %index_ref.3, f32[4]{0:T(128)} %flux_ref.3, f32[4]{0:T(128)} %noise_ref.3, ...), custom_call_target="tpu_custom_call" | custom-call | bytes 16605000 | tf_op jit(solution)/shard_map/pallas_call | solution.py:107
  5.2 0.0 copy-start
  5.2 0.0 copy-start.7
  5.2 0.0 copy-start.8
  5.3 0.0 copy-start.9
  5.3 2.4 %collective-permute-start = (f32[144,128]{1,0:T(8,128)S(1)}, f32[144,128]{1,0:T(8,128)S(1)}, u32[]{:S(2)}, u32[]{:S(2)}) collective-permute-start(f32[144,128]{1,0:T(8,128)S(1)} %get-tuple-element.42), channel_id=1, source_target_pairs={{0,3},{1,2},{2,1},{3,0},{4,7},{5,6},{6,5},{7,4},{8,11},{9,10},{10,... | collective-permute-start | bytes 221192 | tf_op jit(solution)/shard_map/ppermute | solution.py:659
  7.7 0.6 collective-permute-start.1
  8.4 3.2 %shard_map.150 = (f32[144,128]{1,0:T(8,128)S(1)}, f32[144,128]{1,0:T(8,128)S(1)}) custom-call(s32[2]{0:T(128)S(1)} %pad_add_fusion.place_ref, f32[2,4,64,128]{3,2,1,0:T(8,128)S(1)} %get-tuple-element.44.taps_ref, f32[4,128,512]{2,1,0:T(8,128)S(1)} %get-tuple-element.45.x_ref, bf16[2,4,128,256]{3,2,1,0:T(8,128)(2,1)S(1)} %get-tuple-element.46.table_ref), custom_call_target="tpu_custom_call" | custom-call | bytes 11808000 | tf_op jit(solution)/shard_map/pallas_call | solution.py:107
  11.5 0.1 collective-permute-start.2
  11.6 0.9 %collective-permute-done.1.rest_1_ = f32[144,128]{1,0:T(8,128)S(1)} collective-permute-done((f32[144,128]{1,0:T(8,128)S(1)}, f32[144,128]{1,0:T(8,128)S(1)}, u32[]{:S(2)}, u32[]{:S(2)}) %collective-permute-start.1) | collective-permute-done | bytes 73760 | tf_op jit(solution)/shard_map/ppermute | solution.py:659
  12.6 0.3 collective-permute-done.2.rest_2_
  12.9 1.1 %shard_map.151 = (f32[136,128]{1,0:T(8,128)S(1)}, f32[136,128]{1,0:T(8,128)S(1)}, f32[136,128]{1,0:T(8,128)S(1)}, f32[136,128]{1,0:T(8,128)S(1)}) custom-call(s32[2]{0:T(128)S(1)} %pad_add_fusion.place_ref, s32[4]{0:T(128)S(1)} %copy-done.7, f32[4]{0:T(128)S(1)} %copy-done.8, f32[4]{0:T(128)S(1)} %copy-done.9, f32[144,128]{1,0:T(8,128)S(1)} %collective-permute-done.rest_0_, ...), custom_call_target="tpu_custom_call" | custom-call | bytes 4243500 | tf_op jit(solution)/shard_map/pallas_call | solution.py:107
  14.0 0.0 copy-start.3
  14.0 0.0 copy-start.4
  14.0 0.0 copy-start.5
  14.1 0.0 copy-start.6
  14.1 3.8 %collective-permute-start.8 = (f32[136,128]{1,0:T(8,128)S(1)}, f32[136,128]{1,0:T(8,128)S(1)}, u32[]{:S(2)}, u32[]{:S(2)}) collective-permute-start(f32[136,128]{1,0:T(8,128)S(1)} %get-tuple-element.62), channel_id=1, source_target_pairs={{0,12},{4,8},{8,4},{12,0},{1,13},{5,9},{9,5},{13,1},{2,14},{6,10},... | collective-permute-start | bytes 208904 | tf_op jit(solution)/shard_map/ppermute | solution.py:659
  17.8 0.7 %collective-permute-start.6 = (f32[136,128]{1,0:T(8,128)S(1)}, f32[136,128]{1,0:T(8,128)S(1)}, u32[]{:S(2)}, u32[]{:S(2)}) collective-permute-start(f32[136,128]{1,0:T(8,128)S(1)} %get-tuple-element.60), channel_id=1, source_target_pairs={{0,4},{4,0},{8,12},{12,8},{1,5},{5,1},{9,13},{13,9},{2,6},{6,2},{1... | collective-permute-start | bytes 208904 | tf_op jit(solution)/shard_map/ppermute | solution.py:659
  18.5 1.2 %shard_map.153 = (f32[128,512]{1,0:T(8,128)S(1)}, f32[128,512]{1,0:T(8,128)S(1)}, f32[128,512]{1,0:T(8,128)S(1)}, f32[128,512]{1,0:T(8,128)S(1)}) custom-call(s32[2]{0:T(128)S(1)} %pad_add_fusion.place_ref, f32[4,128,512]{2,1,0:T(8,128)S(1)} %get-tuple-element.45.x_ref, bf16[2,4,128,256]{3,2,1,0:T(8,128)(2,1)S(1)} %get-tuple-element.46.table_ref), custom_call_target="tpu_custom_call" | custom-call | bytes 4797000 | tf_op jit(solution)/shard_map/pallas_call | solution.py:107
  19.7 0.1 collective-permute-start.3
  19.8 1.6 %collective-permute-start.4 = (f32[128,512]{1,0:T(8,128)S(1)}, f32[128,512]{1,0:T(8,128)S(1)}, u32[]{:S(2)}, u32[]{:S(2)}) collective-permute-start(f32[128,512]{1,0:T(8,128)S(1)} %get-tuple-element.57), channel_id=1, source_target_pairs={{0,2},{1,3},{2,0},{3,1},{4,6},{5,7},{6,4},{7,5},{8,10},{9,11},{10,... | collective-permute-start | bytes 786440 | tf_op jit(solution)/shard_map/ppermute | solution.py:659
  21.4 0.2 collective-permute-start.5
  21.6 2.4 %collective-permute-done.7 = f32[136,128]{1,0:T(8,128)S(1)} collective-permute-done((f32[136,128]{1,0:T(8,128)S(1)}, f32[136,128]{1,0:T(8,128)S(1)}, u32[]{:S(2)}, u32[]{:S(2)}) %collective-permute-start.7) | collective-permute-done | bytes 69664 | tf_op jit(solution)/shard_map/ppermute | solution.py:659
  24.1 1.2 %collective-permute-start.9 = (f32[136,128]{1,0:T(8,128)S(1)}, f32[136,128]{1,0:T(8,128)S(1)}, u32[]{:S(2)}, u32[]{:S(2)}) collective-permute-start(f32[136,128]{1,0:T(8,128)S(1)} %add_add_fusion.share_ref.rest_0_), channel_id=1, source_target_pairs={{0,4},{4,0},{8,12},{12,8},{1,5},{5,1},{9,13},{13,9},{2,6},{6,2},{1... | collective-permute-start | bytes 208904 | tf_op jit(solution)/shard_map/ppermute | solution.py:659
  25.2 1.9 %collective-permute-start.10 = (f32[136,128]{1,0:T(8,128)S(1)}, f32[136,128]{1,0:T(8,128)S(1)}, u32[]{:S(2)}, u32[]{:S(2)}) collective-permute-start(f32[136,128]{1,0:T(8,128)S(1)} %add_add_fusion.share_ref.rest_0_), channel_id=1, source_target_pairs={{0,8},{4,12},{8,0},{12,4},{1,9},{5,13},{9,1},{13,5},{2,10},{6,14},... | collective-permute-start | bytes 208904 | tf_op jit(solution)/shard_map/ppermute | solution.py:659
  27.2 1.3 %collective-permute-start.11 = (f32[136,128]{1,0:T(8,128)S(1)}, f32[136,128]{1,0:T(8,128)S(1)}, u32[]{:S(2)}, u32[]{:S(2)}) collective-permute-start(f32[136,128]{1,0:T(8,128)S(1)} %add_add_fusion.share_ref.rest_0_), channel_id=1, source_target_pairs={{0,12},{4,8},{8,4},{12,0},{1,13},{5,9},{9,5},{13,1},{2,14},{6,10},... | collective-permute-start | bytes 208904 | tf_op jit(solution)/shard_map/ppermute | solution.py:659
  28.5 2.3 %shard_map.152 = (f32[544,512]{1,0:T(8,128)S(1)}, f32[16,72,512]{2,1,0:T(8,128)S(1)}, f32[2,4,64,128]{3,2,1,0:T(8,128)S(1)}) custom-call(s32[2]{0:T(128)S(1)} %pad_add_fusion.place_ref, s32[4]{0:T(128)S(1)} %copy-done.7, f32[16,16,16]{2,1,0:T(8,128)S(1)} %copy-done.3, bf16[2,4,144,32]{3,2,1,0:T(8,128)(2,1)S(1)} %copy-done.4, bf16[128,512]{1,0:T(8,128)(2,1)S(1)} %copy-done.6, ...), custom_call_target="tpu_custom_call" | custom-call | bytes 8671500 | tf_op jit(solution)/shard_map/pallas_call | solution.py:107
  30.9 1.1 %shard_map.155 = (f32[272,512]{1,0:T(8,128)S(1)}, f32[544,512]{1,0:T(8,128)S(1)}) custom-call(f32[4]{0:T(128)S(1)} %copy-done.8, f32[4]{0:T(128)S(1)} %copy-done.9, f32[136,128]{1,0:T(8,128)S(1)} %add_add_fusion.share_ref.rest_0_, f32[544,512]{1,0:T(8,128)S(1)} %get-tuple-element.63.spectrum_ref, f32[16,72,512]{2,1,0:T(8,128)S(1)} %get-tuple-element.64.power_ref), custom_call_target="tpu_custom_call" | custom-call | bytes 4243500 | tf_op jit(solution)/shard_map/pallas_call | solution.py:107
  32.0 1.6 %collective-permute-done.5.rest_3_ = f32[128,512]{1,0:T(8,128)S(1)} collective-permute-done((f32[128,512]{1,0:T(8,128)S(1)}, f32[128,512]{1,0:T(8,128)S(1)}, u32[]{:S(2)}, u32[]{:S(2)}) %collective-permute-start.5) | collective-permute-done | bytes 262176 | tf_op jit(solution)/shard_map/ppermute | solution.py:659
  33.7 1.8 %shard_map.154.spectrum_ref = f32[544,512]{1,0:T(8,128)S(1)} custom-call(s32[2]{0:T(128)S(1)} %pad_add_fusion.place_ref, f32[128,512]{1,0:T(8,128)S(1)} %get-tuple-element.55.rest_0_, f32[128,512]{1,0:T(8,128)S(1)} %collective-permute-done.3.rest_1_, f32[128,512]{1,0:T(8,128)S(1)} %collective-permute-done.4.rest_2_, ...), custom_call_target="tpu_custom_call" | custom-call | bytes 6826500 | tf_op jit(solution)/shard_map/pallas_call | solution.py:107
  35.6 1.4 %shard_map.157 = (f32[2,144,128]{2,1,0:T(8,128)S(1)}, f32[2,144,128]{2,1,0:T(8,128)S(1)}, f32[2,144,128]{2,1,0:T(8,128)S(1)}, f32[2,144,128]{2,1,0:T(8,128)S(1)}) custom-call(s32[2]{0:T(128)S(1)} %pad_add_fusion.place_ref, f32[544,512]{1,0:T(8,128)S(1)} %shard_map.154.spectrum_ref, f32[272,512]{1,0:T(8,128)S(1)} %get-tuple-element.65.gain_ref, ...), custom_call_target="tpu_custom_call" | custom-call | bytes 4981500 | tf_op jit(solution)/shard_map/pallas_call | solution.py:107
  36.9 0.3 collective-permute-start.15
  37.3 1.6 %collective-permute-start.16 = (f32[2,144,128]{2,1,0:T(8,128)S(1)}, f32[2,144,128]{2,1,0:T(8,128)S(1)}, u32[]{:S(2)}, u32[]{:S(2)}) collective-permute-start(f32[2,144,128]{2,1,0:T(8,128)S(1)} %get-tuple-element.73), channel_id=1, source_target_pairs={{0,2},{1,3},{2,0},{3,1},{4,6},{5,7},{6,4},{7,5},{8,10},{9,11},{10,... | collective-permute-start | bytes 442376 | tf_op jit(solution)/shard_map/ppermute | solution.py:659
  38.8 0.0 collective-permute-start.17
  38.9 1.4 %shard_map.156 = (f32[2,144,128]{2,1,0:T(8,128)S(1)}, f32[2,144,128]{2,1,0:T(8,128)S(1)}, f32[2,144,128]{2,1,0:T(8,128)S(1)}, f32[2,144,128]{2,1,0:T(8,128)S(1)}) custom-call(s32[2]{0:T(128)S(1)} %pad_add_fusion.place_ref, f32[544,512]{1,0:T(8,128)S(1)} %shard_map.154.spectrum_ref, f32[272,512]{1,0:T(8,128)S(1)} %get-tuple-element.65.gain_ref, ...), custom_call_target="tpu_custom_call" | custom-call | bytes 4981500 | tf_op jit(solution)/shard_map/pallas_call | solution.py:107
  40.2 0.6 collective-permute-start.12
  40.8 1.6 %collective-permute-start.13 = (f32[2,144,128]{2,1,0:T(8,128)S(1)}, f32[2,144,128]{2,1,0:T(8,128)S(1)}, u32[]{:S(2)}, u32[]{:S(2)}) collective-permute-start(f32[2,144,128]{2,1,0:T(8,128)S(1)} %get-tuple-element.69), channel_id=1, source_target_pairs={{0,2},{1,3},{2,0},{3,1},{4,6},{5,7},{6,4},{7,5},{8,10},{9,11},{10,... | collective-permute-start | bytes 442376 | tf_op jit(solution)/shard_map/ppermute | solution.py:659
  42.4 1.5 %collective-permute-done.16.rest_2_ = f32[2,144,128]{2,1,0:T(8,128)S(1)} collective-permute-done((f32[2,144,128]{2,1,0:T(8,128)S(1)}, f32[2,144,128]{2,1,0:T(8,128)S(1)}, u32[]{:S(2)}, u32[]{:S(2)}) %collective-permute-start.16) | collective-permute-done | bytes 147488 | tf_op jit(solution)/shard_map/ppermute | solution.py:659
  43.9 2.3 %collective-permute-done.17.rest_3_ = f32[2,144,128]{2,1,0:T(8,128)S(1)} collective-permute-done((f32[2,144,128]{2,1,0:T(8,128)S(1)}, f32[2,144,128]{2,1,0:T(8,128)S(1)}, u32[]{:S(2)}, u32[]{:S(2)}) %collective-permute-start.17) | collective-permute-done | bytes 147488 | tf_op jit(solution)/shard_map/ppermute | solution.py:659
  46.2 5.4 %shard_map.158 = (f32[4,128,512]{2,1,0:T(8,128)}, f32[4,2,1024]{2,1,0:T(2,128)S(1)}) custom-call(s32[2]{0:T(128)S(1)} %pad_add_fusion.place_ref, s32[8,512]{1,0:T(8,128)S(1)} %reshape.12.row_ref, s32[8,512]{1,0:T(8,128)S(1)} %reshape.13.col_ref, f32[2,4,64,128]{3,2,1,0:T(8,128)S(1)} %get-tuple-element.54.taps_ref, ...), custom_call_target="tpu_custom_call" | custom-call | bytes 19926000 | tf_op jit(solution)/shard_map/pallas_call | solution.py:107
  51.6 0.4 collective-permute-done.14.rest_3_
  52.0 5.6 %shard_map.159 = (f32[4,128,512]{2,1,0:T(8,128)}, f32[4,1024]{1,0:T(4,128)S(1)}, f32[4,1024]{1,0:T(4,128)S(1)}, f32[4,1024]{1,0:T(4,128)S(1)}, f32[4,1024]{1,0:T(4,128)S(1)}) custom-call(s32[2]{0:T(128)S(1)} %pad_add_fusion.place_ref, s32[8,512]{1,0:T(8,128)S(1)} %reshape.12.row_ref, s32[8,512]{1,0:T(8,128)S(1)} %reshape.13.col_ref, ...), custom_call_target="tpu_custom_call", output_to_operand_aliasing={{0}: (9, {})} | custom-call | bytes 19926000 | tf_op jit(solution)/shard_map/pallas_call | solution.py:107
  57.6 1.8 %collective-permute-start.20 = (f32[4,1024]{1,0:T(4,128)S(1)}, f32[4,1024]{1,0:T(4,128)S(1)}, u32[]{:S(2)}, u32[]{:S(2)}) collective-permute-start(f32[4,1024]{1,0:T(4,128)S(1)} %get-tuple-element.81), channel_id=1, source_target_pairs={{0,3},{1,2},{2,1},{3,0},{4,7},{5,6},{6,5},{7,4},{8,11},{9,10},{10,... | collective-permute-start | bytes 49160 | tf_op jit(solution)/shard_map/ppermute | solution.py:659
  59.4 0.5 collective-permute-start.19
  59.8 1.0 %collective-permute-done.20 = f32[4,1024]{1,0:T(4,128)S(1)} collective-permute-done((f32[4,1024]{1,0:T(4,128)S(1)}, f32[4,1024]{1,0:T(4,128)S(1)}, u32[]{:S(2)}, u32[]{:S(2)}) %collective-permute-start.20) | collective-permute-done | bytes 16416 | tf_op jit(solution)/shard_map/ppermute | solution.py:659
  60.8 2.3 %collective-permute-done.19 = f32[4,1024]{1,0:T(4,128)S(1)} collective-permute-done((f32[4,1024]{1,0:T(4,128)S(1)}, f32[4,1024]{1,0:T(4,128)S(1)}, u32[]{:S(2)}, u32[]{:S(2)}) %collective-permute-start.19) | collective-permute-done | bytes 16416 | tf_op jit(solution)/shard_map/ppermute | solution.py:659
  63.1 0.6 add_add_fusion.1
  (34 shorter events, 0.1 us)
Async XLA Ops:
  5.2 7.6 %copy-start = (bf16[2,2,2,2,128,256]{5,4,3,2,1,0:T(8,128)(2,1)S(1)}, bf16[2,2,2,2,128,256]{5,4,3,2,1,0:T(8,128)(2,1)}, u32[]{:S(2)}) copy-start(bf16[2,2,2,2,128,256]{5,4,3,2,1,0:T(8,128)(2,1)} %constant.29.clone.rest_4_) | copy-start | bytes 3145732
  5.2 7.6 %copy-start.7 = (s32[4]{0:T(128)S(1)}, s32[4]{0:T(128)}, u32[]{:S(2)}) copy-start(s32[4]{0:T(128)} %index_ref.3) | copy-start | bytes 52
  5.2 7.6 %copy-start.8 = (f32[4]{0:T(128)S(1)}, f32[4]{0:T(128)}, u32[]{:S(2)}) copy-start(f32[4]{0:T(128)} %flux_ref.3) | copy-start | bytes 52
  5.3 7.6 %copy-start.9 = (f32[4]{0:T(128)S(1)}, f32[4]{0:T(128)}, u32[]{:S(2)}) copy-start(f32[4]{0:T(128)} %noise_ref.3) | copy-start | bytes 52
  5.3 6.3 %collective-permute-start = (f32[144,128]{1,0:T(8,128)S(1)}, f32[144,128]{1,0:T(8,128)S(1)}, u32[]{:S(2)}, u32[]{:S(2)}) collective-permute-start(f32[144,128]{1,0:T(8,128)S(1)} %get-tuple-element.42), channel_id=1, source_target_pairs={{0,3},{1,2},{2,1},{3,0},{4,7},{5,6},{6,5},{7,4},{8,11},{9,10},{10,... | collective-permute-start | bytes 221192 | tf_op jit(solution)/shard_map/ppermute | solution.py:659
  7.7 4.8 %collective-permute-start.1 = (f32[144,128]{1,0:T(8,128)S(1)}, f32[144,128]{1,0:T(8,128)S(1)}, u32[]{:S(2)}, u32[]{:S(2)}) collective-permute-start(f32[144,128]{1,0:T(8,128)S(1)} %get-tuple-element.43), channel_id=1, source_target_pairs={{0,2},{1,3},{2,0},{3,1},{4,6},{5,7},{6,4},{7,5},{8,10},{9,11},{10,... | collective-permute-start | bytes 221192 | tf_op jit(solution)/shard_map/ppermute | solution.py:659
  11.5 1.3 %collective-permute-start.2 = (f32[144,128]{1,0:T(8,128)S(1)}, f32[144,128]{1,0:T(8,128)S(1)}, u32[]{:S(2)}, u32[]{:S(2)}) collective-permute-start(f32[144,128]{1,0:T(8,128)S(1)} %get-tuple-element.47), channel_id=1, source_target_pairs={{0,1},{1,0},{2,3},{3,2},{4,5},{5,4},{6,7},{7,6},{8,9},{9,8},{10,11... | collective-permute-start | bytes 221192 | tf_op jit(solution)/shard_map/ppermute | solution.py:659
  14.0 14.5 %copy-start.3 = (f32[16,16,16]{2,1,0:T(8,128)S(1)}, f32[16,16,16]{2,1,0:T(8,128)}, u32[]{:S(2)}) copy-start(f32[16,16,16]{2,1,0:T(8,128)} %bank_ref) | copy-start | bytes 49156
  14.0 14.5 %copy-start.4 = (bf16[2,4,144,32]{3,2,1,0:T(8,128)(2,1)S(1)}, bf16[2,4,144,32]{3,2,1,0:T(8,128)(2,1)}, u32[]{:S(2)}) copy-start(bf16[2,4,144,32]{3,2,1,0:T(8,128)(2,1)} %constant.30.clone.shift_ref) | copy-start | bytes 221188
  14.0 14.5 %copy-start.5 = (f32[16,1024]{1,0:T(8,128)S(1)}, f32[16,1024]{1,0:T(8,128)}, u32[]{:S(2)}) copy-start(f32[16,1024]{1,0:T(8,128)} %constant.27.clone.rest_4_.coef_ref) | copy-start | bytes 196612
  14.1 14.5 %copy-start.6 = (bf16[128,512]{1,0:T(8,128)(2,1)S(1)}, bf16[128,512]{1,0:T(8,128)(2,1)}, u32[]{:S(2)}) copy-start(bf16[128,512]{1,0:T(8,128)(2,1)} %constant.31.clone.spread_ref) | copy-start | bytes 393220
  14.1 7.4 %collective-permute-start.8 = (f32[136,128]{1,0:T(8,128)S(1)}, f32[136,128]{1,0:T(8,128)S(1)}, u32[]{:S(2)}, u32[]{:S(2)}) collective-permute-start(f32[136,128]{1,0:T(8,128)S(1)} %get-tuple-element.62), channel_id=1, source_target_pairs={{0,12},{4,8},{8,4},{12,0},{1,13},{5,9},{9,5},{13,1},{2,14},{6,10},... | collective-permute-start | bytes 208904 | tf_op jit(solution)/shard_map/ppermute | solution.py:659
  17.8 6.2 %collective-permute-start.7 = (f32[136,128]{1,0:T(8,128)S(1)}, f32[136,128]{1,0:T(8,128)S(1)}, u32[]{:S(2)}, u32[]{:S(2)}) collective-permute-start(f32[136,128]{1,0:T(8,128)S(1)} %get-tuple-element.61), channel_id=1, source_target_pairs={{0,8},{4,12},{8,0},{12,4},{1,9},{5,13},{9,1},{13,5},{2,10},{6,14},... | collective-permute-start | bytes 208904 | tf_op jit(solution)/shard_map/ppermute | solution.py:659
  17.8 6.2 %collective-permute-start.6 = (f32[136,128]{1,0:T(8,128)S(1)}, f32[136,128]{1,0:T(8,128)S(1)}, u32[]{:S(2)}, u32[]{:S(2)}) collective-permute-start(f32[136,128]{1,0:T(8,128)S(1)} %get-tuple-element.60), channel_id=1, source_target_pairs={{0,4},{4,0},{8,12},{12,8},{1,5},{5,1},{9,13},{13,9},{2,6},{6,2},{1... | collective-permute-start | bytes 208904 | tf_op jit(solution)/shard_map/ppermute | solution.py:659
  19.7 7.5 %collective-permute-start.3 = (f32[128,512]{1,0:T(8,128)S(1)}, f32[128,512]{1,0:T(8,128)S(1)}, u32[]{:S(2)}, u32[]{:S(2)}) collective-permute-start(f32[128,512]{1,0:T(8,128)S(1)} %get-tuple-element.56), channel_id=1, source_target_pairs={{0,1},{1,0},{2,3},{3,2},{4,5},{5,4},{6,7},{7,6},{8,9},{9,8},{10,11... | collective-permute-start | bytes 786440 | tf_op jit(solution)/shard_map/ppermute | solution.py:659
  19.8 12.2 %collective-permute-start.4 = (f32[128,512]{1,0:T(8,128)S(1)}, f32[128,512]{1,0:T(8,128)S(1)}, u32[]{:S(2)}, u32[]{:S(2)}) collective-permute-start(f32[128,512]{1,0:T(8,128)S(1)} %get-tuple-element.57), channel_id=1, source_target_pairs={{0,2},{1,3},{2,0},{3,1},{4,6},{5,7},{6,4},{7,5},{8,10},{9,11},{10,... | collective-permute-start | bytes 786440 | tf_op jit(solution)/shard_map/ppermute | solution.py:659
  21.4 12.2 %collective-permute-start.5 = (f32[128,512]{1,0:T(8,128)S(1)}, f32[128,512]{1,0:T(8,128)S(1)}, u32[]{:S(2)}, u32[]{:S(2)}) collective-permute-start(f32[128,512]{1,0:T(8,128)S(1)} %get-tuple-element.58), channel_id=1, source_target_pairs={{0,3},{1,2},{2,1},{3,0},{4,7},{5,6},{6,5},{7,4},{8,11},{9,10},{10,... | collective-permute-start | bytes 786440 | tf_op jit(solution)/shard_map/ppermute | solution.py:659
  24.1 11.5 %collective-permute-start.9 = (f32[136,128]{1,0:T(8,128)S(1)}, f32[136,128]{1,0:T(8,128)S(1)}, u32[]{:S(2)}, u32[]{:S(2)}) collective-permute-start(f32[136,128]{1,0:T(8,128)S(1)} %add_add_fusion.share_ref.rest_0_), channel_id=1, source_target_pairs={{0,4},{4,0},{8,12},{12,8},{1,5},{5,1},{9,13},{13,9},{2,6},{6,2},{1... | collective-permute-start | bytes 208904 | tf_op jit(solution)/shard_map/ppermute | solution.py:659
  25.2 10.3 %collective-permute-start.10 = (f32[136,128]{1,0:T(8,128)S(1)}, f32[136,128]{1,0:T(8,128)S(1)}, u32[]{:S(2)}, u32[]{:S(2)}) collective-permute-start(f32[136,128]{1,0:T(8,128)S(1)} %add_add_fusion.share_ref.rest_0_), channel_id=1, source_target_pairs={{0,8},{4,12},{8,0},{12,4},{1,9},{5,13},{9,1},{13,5},{2,10},{6,14},... | collective-permute-start | bytes 208904 | tf_op jit(solution)/shard_map/ppermute | solution.py:659
  27.2 8.4 %collective-permute-start.11 = (f32[136,128]{1,0:T(8,128)S(1)}, f32[136,128]{1,0:T(8,128)S(1)}, u32[]{:S(2)}, u32[]{:S(2)}) collective-permute-start(f32[136,128]{1,0:T(8,128)S(1)} %add_add_fusion.share_ref.rest_0_), channel_id=1, source_target_pairs={{0,12},{4,8},{8,4},{12,0},{1,13},{5,9},{9,5},{13,1},{2,14},{6,10},... | collective-permute-start | bytes 208904 | tf_op jit(solution)/shard_map/ppermute | solution.py:659
  33.7 1.9 %copy-start.1 = (bf16[2,2,256,512]{3,2,1,0:T(8,128)(2,1)S(1)}, bf16[2,2,256,512]{3,2,1,0:T(8,128)(2,1)}, u32[]{:S(2)}) copy-start(bf16[2,2,256,512]{3,2,1,0:T(8,128)(2,1)} %constant.32.clone.rest_4_) | copy-start | bytes 3145732
  36.9 5.5 %collective-permute-start.15 = (f32[2,144,128]{2,1,0:T(8,128)S(1)}, f32[2,144,128]{2,1,0:T(8,128)S(1)}, u32[]{:S(2)}, u32[]{:S(2)}) collective-permute-start(f32[2,144,128]{2,1,0:T(8,128)S(1)} %get-tuple-element.72), channel_id=1, source_target_pairs={{0,1},{1,0},{2,3},{3,2},{4,5},{5,4},{6,7},{7,6},{8,9},{9,8},{10,11... | collective-permute-start | bytes 442376 | tf_op jit(solution)/shard_map/ppermute | solution.py:659
  37.3 6.7 %collective-permute-start.16 = (f32[2,144,128]{2,1,0:T(8,128)S(1)}, f32[2,144,128]{2,1,0:T(8,128)S(1)}, u32[]{:S(2)}, u32[]{:S(2)}) collective-permute-start(f32[2,144,128]{2,1,0:T(8,128)S(1)} %get-tuple-element.73), channel_id=1, source_target_pairs={{0,2},{1,3},{2,0},{3,1},{4,6},{5,7},{6,4},{7,5},{8,10},{9,11},{10,... | collective-permute-start | bytes 442376 | tf_op jit(solution)/shard_map/ppermute | solution.py:659
  38.8 3.6 %copy-start.10 = (s32[4096]{0:T(1024)S(1)}, s32[4096]{0:T(1024)}, u32[]{:S(2)}) copy-start(s32[4096]{0:T(1024)} %param.19) | copy-start | bytes 49156
  38.8 3.6 %copy-start.11 = (s32[4096]{0:T(1024)S(1)}, s32[4096]{0:T(1024)}, u32[]{:S(2)}) copy-start(s32[4096]{0:T(1024)} %param.20) | copy-start | bytes 49156
  38.8 7.4 %copy-start.2 = (bf16[2,4,128,256]{3,2,1,0:T(8,128)(2,1)S(1)}, bf16[2,4,128,256]{3,2,1,0:T(8,128)(2,1)}, u32[]{:S(2)}) copy-start(bf16[2,4,128,256]{3,2,1,0:T(8,128)(2,1)} %constant.33.clone.rest_4_) | copy-start | bytes 1572868
  38.8 7.4 %collective-permute-start.17 = (f32[2,144,128]{2,1,0:T(8,128)S(1)}, f32[2,144,128]{2,1,0:T(8,128)S(1)}, u32[]{:S(2)}, u32[]{:S(2)}) collective-permute-start(f32[2,144,128]{2,1,0:T(8,128)S(1)} %get-tuple-element.74), channel_id=1, source_target_pairs={{0,3},{1,2},{2,1},{3,0},{4,7},{5,6},{6,5},{7,4},{8,11},{9,10},{10,... | collective-permute-start | bytes 442376 | tf_op jit(solution)/shard_map/ppermute | solution.py:659
  40.2 11.3 %collective-permute-start.12 = (f32[2,144,128]{2,1,0:T(8,128)S(1)}, f32[2,144,128]{2,1,0:T(8,128)S(1)}, u32[]{:S(2)}, u32[]{:S(2)}) collective-permute-start(f32[2,144,128]{2,1,0:T(8,128)S(1)} %get-tuple-element.68), channel_id=1, source_target_pairs={{0,1},{1,0},{2,3},{3,2},{4,5},{5,4},{6,7},{7,6},{8,9},{9,8},{10,11... | collective-permute-start | bytes 442376 | tf_op jit(solution)/shard_map/ppermute | solution.py:659
  40.8 10.8 %collective-permute-start.13 = (f32[2,144,128]{2,1,0:T(8,128)S(1)}, f32[2,144,128]{2,1,0:T(8,128)S(1)}, u32[]{:S(2)}, u32[]{:S(2)}) collective-permute-start(f32[2,144,128]{2,1,0:T(8,128)S(1)} %get-tuple-element.69), channel_id=1, source_target_pairs={{0,2},{1,3},{2,0},{3,1},{4,6},{5,7},{6,4},{7,5},{8,10},{9,11},{10,... | collective-permute-start | bytes 442376 | tf_op jit(solution)/shard_map/ppermute | solution.py:659
  42.4 9.6 %collective-permute-start.14 = (f32[2,144,128]{2,1,0:T(8,128)S(1)}, f32[2,144,128]{2,1,0:T(8,128)S(1)}, u32[]{:S(2)}, u32[]{:S(2)}) collective-permute-start(f32[2,144,128]{2,1,0:T(8,128)S(1)} %get-tuple-element.70), channel_id=1, source_target_pairs={{0,3},{1,2},{2,1},{3,0},{4,7},{5,6},{6,5},{7,4},{8,11},{9,10},{10,... | collective-permute-start | bytes 442376 | tf_op jit(solution)/shard_map/ppermute | solution.py:659
  57.6 3.2 %collective-permute-start.20 = (f32[4,1024]{1,0:T(4,128)S(1)}, f32[4,1024]{1,0:T(4,128)S(1)}, u32[]{:S(2)}, u32[]{:S(2)}) collective-permute-start(f32[4,1024]{1,0:T(4,128)S(1)} %get-tuple-element.81), channel_id=1, source_target_pairs={{0,3},{1,2},{2,1},{3,0},{4,7},{5,6},{6,5},{7,4},{8,11},{9,10},{10,... | collective-permute-start | bytes 49160 | tf_op jit(solution)/shard_map/ppermute | solution.py:659
  59.4 3.7 %collective-permute-start.19 = (f32[4,1024]{1,0:T(4,128)S(1)}, f32[4,1024]{1,0:T(4,128)S(1)}, u32[]{:S(2)}, u32[]{:S(2)}) collective-permute-start(f32[4,1024]{1,0:T(4,128)S(1)} %get-tuple-element.80), channel_id=1, source_target_pairs={{0,2},{1,3},{2,0},{3,1},{4,6},{5,7},{6,4},{7,5},{8,10},{9,11},{10,... | collective-permute-start | bytes 49160 | tf_op jit(solution)/shard_map/ppermute | solution.py:659
  59.8 3.3 %collective-permute-start.18 = (f32[4,1024]{1,0:T(4,128)S(1)}, f32[4,1024]{1,0:T(4,128)S(1)}, u32[]{:S(2)}, u32[]{:S(2)}) collective-permute-start(f32[4,1024]{1,0:T(4,128)S(1)} %get-tuple-element.79), channel_id=1, source_target_pairs={{0,1},{1,0},{2,3},{3,2},{4,5},{5,4},{6,7},{7,6},{8,9},{9,8},{10,11... | collective-permute-start | bytes 49160 | tf_op jit(solution)/shard_map/ppermute | solution.py:659

commit v2 on v1

--- a/solution.py
+++ b/solution.py
@@ -174,11 +174,13 @@
             straight = jnp.zeros((step, lanes), f32)
             crossed = jnp.zeros((step, lanes), f32)
             for e in range(epochs):
-                for a in range(stamp):
-                    value = padded[m, e, start + a : start + a + step, :]
-                    at = e * stamp + a
-                    straight += taps_ref[0, d, at : at + 1] * value
-                    crossed += taps_ref[1, d, at : at + 1] * value
+                for shift in range(8):
+                    shifted = padded[m, e, start + shift : start + shift + step + stamp - 8, :]
+                    for base in range(0, stamp, 8):
+                        value = shifted[base : base + step]
+                        at = e * stamp + base + shift
+                        straight += taps_ref[0, d, at : at + 1] * value
+                        crossed += taps_ref[1, d, at : at + 1] * value
             gathered[m, start : start + step] = straight + swap_halves(plan, crossed)
 
     for m in range(pairs):
@@ -243,22 +245,26 @@
     ))
 
 
-def row_transform(plan, place, images, table):
-    slabs, pairs, lanes = plan.slabs, plan.pairs, plan.lanes
+def row_transform(plan, place, images, table, parties):
+    slabs, pairs, lanes, rows = plan.slabs, plan.pairs, plan.lanes, plan.rows
 
     def kernel(place_ref, x_ref, table_ref, *outs):
         for group in range(2):
             data, table = row_operands(plan, place_ref[0], group, x_ref, table_ref)
             result = mul3(table, data, True)
-            for m in range(pairs):
-                outs[group * pairs + m][...] = result[m * lanes : (m + 1) * lanes]
-
-    return list(call(
-        kernel,
-        [("v", (lanes, images.shape[0] * plan.rows))] * slabs,
+            for i, (begin, end) in enumerate(parties):
+                for m in range(pairs):
+                    outs[i * slabs + group * pairs + m][...] = result[
+                        m * lanes : (m + 1) * lanes, begin * rows : end * rows
+                    ]
+
+    flat = call(
+        kernel,
+        [("v", (lanes, (end - begin) * rows)) for begin, end in parties for _ in range(slabs)],
         [("s", place), ("v", images), ("v", table)],
         micros=1.3,
-    ))
+    )
+    return [list(flat[i * slabs : (i + 1) * slabs]) for i in range(len(parties))]
 
 
 def numerator(plan, place, index, flux, noise, blocks, pieces):
@@ -432,7 +438,7 @@
     size = body + edge_rows
 
     def kernel(place_ref, *rest):
-        ins = rest[:slabs]
+        ins = rest[:slabs][::-1]
         table_ref, plane_ref, left_high, left_low = rest[slabs:]
         q = place_ref[0]
         first = (q == 0).astype(f32)
@@ -473,7 +479,7 @@
     (plane,) = call(
         kernel,
         [("v", (2 * size, side))],
-        [("s", place)] + [("v", b) for b in blocks] + [("v", plan.down)],
+        [("s", place)] + [("v", b) for b in reversed(blocks)] + [("v", plan.down)],
         [pltpu.VMEM((2 * size, side), bf16), pltpu.VMEM((2 * size, side), bf16)],
         micros=1.85,
     )
@@ -509,21 +515,22 @@
             ]
             numer_all = parts[0] if len(parts) == 1 else jnp.concatenate(parts, 1)
 
-            def difference(start, stop, nre, nim):
-                gain_, cre = gain_ref[start:stop, here], cross_ref[start:stop, here]
-                cim = cross_ref[size + start : size + stop, here]
-                re = gain_ * spectrum_ref[start:stop, here] - (cre * nre - cim * nim)
-                im = gain_ * spectrum_ref[size + start : size + stop, here] - (cre * nim + cim * nre)
-                return re, im
-
-            edge_re, edge_im = difference(
-                body, size, numer_all[lanes : lanes + 1], numer_all[lanes + 1 : lanes + 2]
-            )
+            def difference(at, lines, nre, nim):
+                gain_, cre = gain_ref[at : at + lines, here], cross_ref[at : at + lines, here]
+                cim = cross_ref[size + at : size + at + lines, here]
+                mre = spectrum_ref[at : at + lines, here]
+                mim = spectrum_ref[size + at : size + at + lines, here]
+                return gain_ * mre - (cre * nre - cim * nim), gain_ * mim - (cre * nim + cim * nre)
+
             for i in range(epochs):
                 e = begin + i
-                re, im = difference(e * cols, (e + 1) * cols, numer_all[:cols], numer_all[cols:lanes])
-                im_left = jnp.where(packed, edge_re[e : e + 1], im)
-                im_right = jnp.where(packed, -edge_im[e : e + 1], re)
+                edge_re, edge_im = difference(
+                    body + e, 1,
+                    numer_all[lanes : lanes + 1], numer_all[lanes + 1 : lanes + 2],
+                )
+                re, im = difference(e * cols, cols, numer_all[:cols], numer_all[cols:lanes])
+                im_left = jnp.where(packed, edge_re, im)
+                im_right = jnp.where(packed, -edge_im, re)
                 for base, start, entry in (
                     (0, 0, re), (0, half, -im), (cols, 0, im_left), (cols, half, im_right),
                 ):
@@ -556,9 +563,80 @@
     )
 
 
-def row_inverse(plan, place, blocks, taps, begin, epochs, difference, earlier, src_row, src_col):
-    slabs, pairs, rows, half, side, lanes, halo, stamp = (
-        plan.slabs, plan.pairs, plan.rows, plan.half, plan.side, plan.lanes, plan.halo, plan.stamp,
+def column_choice(side, src_col):
+    groups, group = src_col.shape
+
+    def kernel(col_ref, out_ref):
+        column = lax.broadcasted_iota(jnp.int32, (side, group), 0)
+
+        @pl.loop(0, groups)
+        def _(g):
+            out_ref[g] = (column == col_ref[pl.ds(g, 1)]).astype(f32).astype(bf16)
+
+    (chosen,) = call(
+        kernel, [("v", (groups, side, group), bf16)], [("v", src_col)], micros=2.0
+    )
+    return chosen
+
+
+def inverse_rows(plan, q, left, table_ref):
+    pairs, lanes = plan.pairs, plan.lanes
+    sums = []
+    for group in range(2):
+        table = [
+            jnp.concatenate([table_ref[n, d] for d in owners_of(plan, q, group)], 0) for n in range(2)
+        ]
+        here = slice(group * pairs * lanes, (group + 1) * pairs * lanes)
+        sums.append(mul3((left[0][:, here], left[1][:, here]), table))
+    sign = jnp.where(q < pairs, 1.0, -1.0).astype(f32)
+    return sums[0] + sums[1], sign * (sums[0] - sums[1])
+
+
+def row_images(plan, place, returned):
+    slabs, rows, half, side, lanes, halo = (
+        plan.slabs, plan.rows, plan.half, plan.side, plan.lanes, plan.halo,
+    )
+    counts = [blocks[0].shape[0] for blocks in returned]
+    epochs = sum(counts)
+
+    def kernel(place_ref, *rest):
+        ins, table_ref, diff_ref = rest[: -6], rest[-6], rest[-5]
+        left_high, left_low, image_ref, sems = rest[-4:]
+        q = place_ref[0]
+        copies = []
+        begin = 0
+        for i, count in enumerate(counts):
+            total = count * rows
+            for m in range(slabs):
+                here = slice(m * lanes, (m + 1) * lanes)
+                value = ins[i * slabs + m][:, halo : halo + rows, :].reshape(total, lanes)
+                left_high[:total, here], left_low[:total, here] = split(value)
+            left = (left_high[:total], left_low[:total])
+            for part, value in enumerate(inverse_rows(plan, q, left, table_ref)):
+                image_ref[begin : begin + count, :, part * half : (part + 1) * half] = value.reshape(
+                    count, rows, half
+                )
+            where = pl.ds(begin, count)
+            copies.append(pltpu.make_async_copy(image_ref.at[where], diff_ref.at[where], sems.at[i]))
+            copies[-1].start()
+            begin += count
+        for copy in copies:
+            copy.wait()
+
+    left = pltpu.VMEM((max(counts) * rows, side), bf16)
+    (difference,) = call(
+        kernel,
+        [("h", (epochs, rows, side))],
+        [("s", place)] + [("v", b) for blocks in returned for b in blocks] + [("v", plan.back)],
+        [left, left, pltpu.VMEM((epochs, rows, side), f32), pltpu.SemaphoreType.DMA((len(counts),))],
+        micros=2.2,
+    )
+    return difference
+
+
+def row_fluxes(plan, place, blocks, taps, begin, epochs, earlier, src_row, chosen):
+    slabs, rows, half, side, lanes, stamp = (
+        plan.slabs, plan.rows, plan.half, plan.side, plan.lanes, plan.stamp,
     )
     mine = blocks[0].shape[0]
     groups, group = src_row.shape
@@ -566,57 +644,41 @@
     total = mine * rows
     step = min(64, rows)
     last = begin + mine == epochs
-    count = slabs if last else 1
-    flux_shapes = [("v", (epochs, each * group))] * slabs if last else [("v", (slabs, begin + mine, each * group))]
-
-    def kernel(place_ref, row_ref, col_ref, taps_ref, *rest):
-        ins, table_ref = rest[:slabs], rest[slabs]
+
+    def kernel(place_ref, row_ref, chosen_ref, taps_ref, *rest):
+        ins, table_ref = rest[:slabs][::-1], rest[slabs]
         rest = rest[slabs + 1 :]
-        if difference is not None:
-            earlier_ref, rest = rest[1], rest[2:]
-        diff_ref, outs = rest[0], rest[1 : 1 + count]
-        left_high, left_low, image_ref, flux_ref, picked, sem = rest[1 + count :]
+        if begin:
+            earlier_ref, rest = rest[0], rest[1:]
+        outs = rest[:-4]
+        left_high, left_low, flux_ref, picked = rest[-4:]
         q = place_ref[0]
         for m in range(slabs):
             d = q ^ m
             here = slice(m * lanes, (m + 1) * lanes)
             for i in range(mine):
-                base = i * rows
-                left_high[base : base + rows, here], left_low[base : base + rows, here] = split(
-                    ins[m][i, halo : halo + rows, :]
-                )
                 for start in range(0, rows, step):
                     straight = jnp.zeros((step, lanes), f32)
                     crossed = jnp.zeros((step, lanes), f32)
-                    for a in range(stamp):
-                        value = ins[m][i, start + a : start + a + step, :]
-                        at = (begin + i) * stamp + a
-                        straight += taps_ref[0, d, at : at + 1] * value
-                        crossed += taps_ref[1, d, at : at + 1] * value
-                    at = total + base + start
+                    for shift in range(8):
+                        shifted = ins[m][i, start + shift : start + shift + step + stamp - 8, :]
+                        for base in range(0, stamp, 8):
+                            value = shifted[base : base + step]
+                            at = (begin + i) * stamp + base + shift
+                            straight += taps_ref[0, d, at : at + 1] * value
+                            crossed += taps_ref[1, d, at : at + 1] * value
+                    at = i * rows + start
                     left_high[at : at + step, here], left_low[at : at + step, here] = split(
                         straight + swap_halves(plan, crossed)
                     )
-
-        sums = []
-        for side_ in range(2):
-            members = [side_ * pairs + m for m in range(pairs)]
-            table = [jnp.concatenate([table_ref[n, q ^ m] for m in members], 0) for n in range(2)]
-            here = slice(side_ * pairs * lanes, (side_ + 1) * pairs * lanes)
-            sums.append(mul3((left_high[:, here], left_low[:, here]), table))
-        sign = jnp.where(q < pairs, 1.0, -1.0).astype(f32)
-        for lane_half in range(2):
-            value = sums[0] + sums[1] if lane_half == 0 else sign * (sums[0] - sums[1])
-            here = slice(lane_half * half, (lane_half + 1) * half)
-            image_ref[:, :, here] = value[:total].reshape(mine, rows, half)
-            flux_ref[:total, here], flux_ref[total:, here] = split(value[total:])
-        copy = pltpu.make_async_copy(image_ref, diff_ref.at[pl.ds(begin, mine)], sem)
-        copy.start()
-        column = lax.broadcasted_iota(jnp.int32, (side, group), 0)
+        for part, value in enumerate(
+            inverse_rows(plan, q, (left_high[...], left_low[...]), table_ref)
+        ):
+            here = slice(part * half, (part + 1) * half)
+            flux_ref[:total, here], flux_ref[total:, here] = split(value)
         line = lax.broadcasted_iota(jnp.int32, (rows, group), 0)
         for g in range(groups):
-            chosen = (column == col_ref[g : g + 1]).astype(f32).astype(bf16)
-            values = mul(flux_ref[...], chosen)
+            values = mul(flux_ref[...], chosen_ref[g])
             values = values[:total] + values[total:]
             inside = line == row_ref[g : g + 1] - q * rows
             found = [
@@ -633,23 +695,18 @@
             if begin:
                 out[:begin] = earlier_ref[owner]
             out[begin:] = picked[owner]
-        copy.wait()
-
-    ins = [("s", place), ("v", src_row), ("v", src_col), ("v", taps)]
-    ins += [("v", b) for b in blocks] + [("v", plan.back)]
-    aliases = {}
-    if difference is not None:
-        aliases = {len(ins): 0}
-        ins += [("h", difference), ("v", earlier)]
-    left = pltpu.VMEM((2 * total, side), bf16)
+
+    ins = [("s", place), ("v", src_row), ("v", chosen), ("v", taps)]
+    ins += [("v", b) for b in reversed(blocks)] + [("v", plan.back)]
+    if begin:
+        ins.append(("v", earlier))
+    left = pltpu.VMEM((total, side), bf16)
     return call(
         kernel,
-        [("h", (epochs, rows, side))] + flux_shapes,
+        [("v", (epochs, each * group))] * slabs if last else [("v", (slabs, begin + mine, each * group))],
         ins,
-        [left, left, pltpu.VMEM((mine, rows, side), f32), left,
-         pltpu.VMEM((slabs, mine, each * group), f32), pltpu.SemaphoreType.DMA(())],
-        aliases=aliases,
-        micros=5.4,
+        [left, left, pltpu.VMEM((2 * total, side), bf16), pltpu.VMEM((slabs, mine, each * group), f32)],
+        micros=4.0,
     )
 
 
@@ -674,40 +731,39 @@
         group = math.gcd(512, src_row.shape[0] // slabs)
         scalars = (psf_index, flux_scale, noise_level)
 
+        edges = list(range(0, epochs, 2)) + [epochs]
+        parties = list(zip(edges, edges[1:]))
+
         far, weighted, images, table = row_transform_far(plan, place, *scalars, epoch_images, psf_bank)
         near = row_transform_near(plan, place, weighted, images, table)
-        blocks = row_transform(plan, place, images, table)
+        (blocks,) = row_transform(plan, place, images, table, [(0, epochs)])
         numer = trade(near + far, slab_axes, slabs)
-        numer = numerator(plan, place, *scalars, numer, pieces)
+        numer, blocks = lax.optimization_barrier((numer[::-1], blocks))
+        numer = numerator(plan, place, *scalars, numer[::-1], pieces)
         bank, numer = lax.optimization_barrier((psf_bank, numer))
         spectrum, power, taps = psf_planes(plan, place, bank, psf_index)
         blocks = trade(blocks, slab_axes, slabs)
         if direct:
-            own = sum(trade(numer, "epoch", ranks))
+            own = sum(trade(numer, "epoch", ranks)[::-1])
+            own, spectrum = lax.optimization_barrier((own, spectrum))
             numer = trade([own] * ranks, "epoch", ranks)
         else:
             own = lax.psum(numer[0], "epoch")
             numer = [own]
-        images = column_transform(plan, place, blocks)
         gain, cross = filter_gains(plan, flux_scale, noise_level, own, spectrum, power)
-
-        parties = [0]
-        while parties[-1] < epochs:
-            parties.append(min(parties[-1] + 2, epochs))
-        parties = list(zip(parties, parties[1:]))
-        returned = [
-            trade(
-                column_inverse(plan, place, images, gain, cross, numer, begin, end), slab_axes, slabs
+        image = column_transform(plan, place, blocks)
+        returned = []
+        for begin, end in parties:
+            rows_back = column_inverse(plan, place, image, gain, cross, numer, begin, end)
+            returned.append(trade(rows_back, slab_axes, slabs))
+        chosen = column_choice(side, src_col.reshape(-1, group))
+        picked = [None]
+        for (begin, _), block in zip(parties, returned):
+            picked = row_fluxes(
+                plan, place, block, taps, begin, epochs, picked[0], src_row.reshape(-1, group), chosen
             )
-            for begin, end in parties
-        ]
-        difference, picked = None, [None]
-        for i, (begin, _) in enumerate(parties):
-            difference, *picked = row_inverse(
-                plan, place, returned[i], taps, begin, epochs, difference, picked[0],
-                src_row.reshape(-1, group), src_col.reshape(-1, group),
-            )
-        return difference, sum(trade(picked, slab_axes, slabs))
+        difference = row_images(plan, place, returned)
+        return difference, sum(trade(picked, slab_axes, slabs)[::-1])
 
     return shards
 

time: 63.9 us -> 61 us (0.955)
  waiting for transfers between devices: 12.7 us -> 9.71 us
  Pallas kernels: 28.9 us -> 29.6 us
    ppermute x21, waiting for transfers between devices: 12.7 us -> 9.71 us  [trade(): result[m] = lax.ppermute(parts[m], axes, [(i, i ^ m) for i in range(count)])]
    pallas_call x11 -> x13, Pallas kernels: 28.9 us -> 29.6 us  [call(): pl.pallas_call(kernel, out_shape=tuple((jax.ShapeDtypeStruct(shape, (*kin...]
  transfers between devices with their start and end apart: 21 -> 21, of which waited for: 9 -> 7; matrix products, arithmetic and copies ran while one was open for 0% -> 0% of each run, Pallas kernels for 26% -> 30%
where the time goes in v2:
time: 61 us; the launch traced here: 60.8 us
  Pallas kernels  29.6 us (49%)
  starting transfers between devices  19.8 us (32%)
  waiting for transfers between devices  9.71 us (16%)
  between operations  0.93 us (2%)
  other arithmetic  0.71 us (1%)
    pallas_call x13, Pallas kernels, call(): pl.pallas_call(kernel, out_shape=tuple((jax.ShapeDtypeStruct(shape, (*kin...  29.6 us
    ppermute x21, starting transfers between devices, trade(): result[m] = lax.ppermute(parts[m], axes, [(i, i ^ m) for i in range(count)])  19.8 us
    ppermute x21, waiting for transfers between devices, trade(): result[m] = lax.ppermute(parts[m], axes, [(i, i ^ m) for i in range(count)])  9.71 us
  transfers between devices with their start and end apart: 21, of which 7 were waited for; matrix products, arithmetic and copies ran while one was open for 0% of the time, Pallas kernels for 30%

profile of v2, /device:TPU:0, one launch (start us, length us, event | category | flops | bytes accessed | tf_op | source)
XLA Modules:
  0.0 60.8 jit_solution(12613772309860505567)
XLA Ops:
  0.6 0.1 pad_add_fusion.place_ref
  0.7 4.4 %shard_map.149 = (f32[144,128]{1,0:T(8,128)S(1)}, f32[144,128]{1,0:T(8,128)S(1)}, f32[2,4,64,128]{3,2,1,0:T(8,128)S(1)}, f32[4,128,512]{2,1,0:T(8,128)S(1)}, bf16[2,4,128,256]{3,2,1,0:T(8,128)(2,1)S(1)}) custom-call(s32[2]{0:T(128)S(1)} %pad_add_fusion.place_ref, s32[4]{0:T(128)} %index_ref.3, f32[4]{0:T(128)} %flux_ref.3, f32[4]{0:T(128)} %noise_ref.3, ...), custom_call_target="tpu_custom_call" | custom-call | bytes 16605000 | tf_op jit(solution)/shard_map/pallas_call | solution.py:107
  5.2 2.4 %collective-permute-start = (f32[144,128]{1,0:T(8,128)S(1)}, f32[144,128]{1,0:T(8,128)S(1)}, u32[]{:S(2)}, u32[]{:S(2)}) collective-permute-start(f32[144,128]{1,0:T(8,128)S(1)} %get-tuple-element.49), channel_id=1, source_target_pairs={{0,3},{1,2},{2,1},{3,0},{4,7},{5,6},{6,5},{7,4},{8,11},{9,10},{10,... | collective-permute-start | bytes 221192 | tf_op jit(solution)/shard_map/ppermute | solution.py:716
  7.6 0.6 %collective-permute-start.1 = (f32[144,128]{1,0:T(8,128)S(1)}, f32[144,128]{1,0:T(8,128)S(1)}, u32[]{:S(2)}, u32[]{:S(2)}) collective-permute-start(f32[144,128]{1,0:T(8,128)S(1)} %get-tuple-element.50), channel_id=1, source_target_pairs={{0,2},{1,3},{2,0},{3,1},{4,6},{5,7},{6,4},{7,5},{8,10},{9,11},{10,... | collective-permute-start | bytes 221192 | tf_op jit(solution)/shard_map/ppermute | solution.py:716
  8.2 2.9 %shard_map.150 = (f32[144,128]{1,0:T(8,128)S(1)}, f32[144,128]{1,0:T(8,128)S(1)}) custom-call(s32[2]{0:T(128)S(1)} %pad_add_fusion.place_ref, f32[2,4,64,128]{3,2,1,0:T(8,128)S(1)} %get-tuple-element.51.taps_ref, f32[4,128,512]{2,1,0:T(8,128)S(1)} %get-tuple-element.52.x_ref, bf16[2,4,128,256]{3,2,1,0:T(8,128)(2,1)S(1)} %get-tuple-element.53.table_ref), custom_call_target="tpu_custom_call" | custom-call | bytes 11808000 | tf_op jit(solution)/shard_map/pallas_call | solution.py:107
  11.2 0.0 copy-start.1
  11.2 0.0 copy-start.4
  11.2 0.0 copy-start.5
  11.2 0.0 copy-start.6
  11.3 0.1 collective-permute-start.2
  11.4 1.2 %shard_map.151 = (f32[128,512]{1,0:T(8,128)S(1)}, f32[128,512]{1,0:T(8,128)S(1)}, f32[128,512]{1,0:T(8,128)S(1)}, f32[128,512]{1,0:T(8,128)S(1)}) custom-call(s32[2]{0:T(128)S(1)} %pad_add_fusion.place_ref, f32[4,128,512]{2,1,0:T(8,128)S(1)} %get-tuple-element.52.x_ref, bf16[2,4,128,256]{3,2,1,0:T(8,128)(2,1)S(1)} %get-tuple-element.53.table_ref), custom_call_target="tpu_custom_call" | custom-call | bytes 4797000 | tf_op jit(solution)/shard_map/pallas_call | solution.py:107
  12.5 0.0 collective-permute-done.2.rest_2_
  12.6 1.1 %shard_map.153 = (f32[136,128]{1,0:T(8,128)S(1)}, f32[136,128]{1,0:T(8,128)S(1)}, f32[136,128]{1,0:T(8,128)S(1)}, f32[136,128]{1,0:T(8,128)S(1)}) custom-call(s32[2]{0:T(128)S(1)} %pad_add_fusion.place_ref, s32[4]{0:T(128)S(1)} %copy-done.7, f32[4]{0:T(128)S(1)} %copy-done.8, f32[4]{0:T(128)S(1)} %copy-done.9, f32[144,128]{1,0:T(8,128)S(1)} %collective-permute-done.rest_0_, ...), custom_call_target="tpu_custom_call" | custom-call | bytes 4243500 | tf_op jit(solution)/shard_map/pallas_call | solution.py:107
  13.8 3.9 %collective-permute-start.6 = (f32[136,128]{1,0:T(8,128)S(1)}, f32[136,128]{1,0:T(8,128)S(1)}, u32[]{:S(2)}, u32[]{:S(2)}) collective-permute-start(f32[136,128]{1,0:T(8,128)S(1)} %get-tuple-element.72), channel_id=1, source_target_pairs={{0,12},{4,8},{8,4},{12,0},{1,13},{5,9},{9,5},{13,1},{2,14},{6,10},... | collective-permute-start | bytes 208904 | tf_op jit(solution)/shard_map/ppermute | solution.py:716
  17.7 0.6 %collective-permute-start.8 = (f32[136,128]{1,0:T(8,128)S(1)}, f32[136,128]{1,0:T(8,128)S(1)}, u32[]{:S(2)}, u32[]{:S(2)}) collective-permute-start(f32[136,128]{1,0:T(8,128)S(1)} %get-tuple-element.74), channel_id=1, source_target_pairs={{0,4},{4,0},{8,12},{12,8},{1,5},{5,1},{9,13},{13,9},{2,6},{6,2},{1... | collective-permute-start | bytes 208904 | tf_op jit(solution)/shard_map/ppermute | solution.py:716
  18.3 0.6 %collective-permute-start.3 = (f32[128,512]{1,0:T(8,128)S(1)}, f32[128,512]{1,0:T(8,128)S(1)}, u32[]{:S(2)}, u32[]{:S(2)}) collective-permute-start(f32[128,512]{1,0:T(8,128)S(1)} %get-tuple-element.60), channel_id=1, source_target_pairs={{0,3},{1,2},{2,1},{3,0},{4,7},{5,6},{6,5},{7,4},{8,11},{9,10},{10,... | collective-permute-start | bytes 786440 | tf_op jit(solution)/shard_map/ppermute | solution.py:716
  19.0 1.0 %collective-permute-start.4 = (f32[128,512]{1,0:T(8,128)S(1)}, f32[128,512]{1,0:T(8,128)S(1)}, u32[]{:S(2)}, u32[]{:S(2)}) collective-permute-start(f32[128,512]{1,0:T(8,128)S(1)} %get-tuple-element.61), channel_id=1, source_target_pairs={{0,2},{1,3},{2,0},{3,1},{4,6},{5,7},{6,4},{7,5},{8,10},{9,11},{10,... | collective-permute-start | bytes 786440 | tf_op jit(solution)/shard_map/ppermute | solution.py:716
  20.0 2.3 %shard_map.154 = (f32[544,512]{1,0:T(8,128)S(1)}, f32[16,72,512]{2,1,0:T(8,128)S(1)}, f32[2,4,64,128]{3,2,1,0:T(8,128)S(1)}) custom-call(s32[2]{0:T(128)S(1)} %pad_add_fusion.place_ref, s32[4]{0:T(128)S(1)} %copy-done.7, f32[16,16,16]{2,1,0:T(8,128)S(1)} %copy-done.3, bf16[2,4,144,32]{3,2,1,0:T(8,128)(2,1)S(1)} %copy-done.4, bf16[128,512]{1,0:T(8,128)(2,1)S(1)} %copy-done.6, ...), custom_call_target="tpu_custom_call" | custom-call | bytes 8671500 | tf_op jit(solution)/shard_map/pallas_call | solution.py:107
  22.3 0.3 collective-permute-start.5
  22.6 1.2 %collective-permute-done.7 = f32[136,128]{1,0:T(8,128)S(1)} collective-permute-done((f32[136,128]{1,0:T(8,128)S(1)}, f32[136,128]{1,0:T(8,128)S(1)}, u32[]{:S(2)}, u32[]{:S(2)}) %collective-permute-start.7) | collective-permute-done | bytes 69664 | tf_op jit(solution)/shard_map/ppermute | solution.py:716
  23.9 2.6 %collective-permute-start.11 = (f32[136,128]{1,0:T(8,128)S(1)}, f32[136,128]{1,0:T(8,128)S(1)}, u32[]{:S(2)}, u32[]{:S(2)}) collective-permute-start(f32[136,128]{1,0:T(8,128)S(1)} %add_add_fusion.share_ref.rest_0_), channel_id=1, source_target_pairs={{0,12},{4,8},{8,4},{12,0},{1,13},{5,9},{9,5},{13,1},{2,14},{6,10},... | collective-permute-start | bytes 208904 | tf_op jit(solution)/shard_map/ppermute | solution.py:716
  26.5 0.1 collective-permute-start.10
  26.5 0.2 collective-permute-done.3.rest_0_
  26.8 1.6 %collective-permute-start.9 = (f32[136,128]{1,0:T(8,128)S(1)}, f32[136,128]{1,0:T(8,128)S(1)}, u32[]{:S(2)}, u32[]{:S(2)}) collective-permute-start(f32[136,128]{1,0:T(8,128)S(1)} %add_add_fusion.share_ref.rest_0_), channel_id=1, source_target_pairs={{0,4},{4,0},{8,12},{12,8},{1,5},{5,1},{9,13},{13,9},{2,6},{6,2},{1... | collective-permute-start | bytes 208904 | tf_op jit(solution)/shard_map/ppermute | solution.py:716
  28.4 1.1 %shard_map.155 = (f32[272,512]{1,0:T(8,128)S(1)}, f32[544,512]{1,0:T(8,128)S(1)}) custom-call(f32[4]{0:T(128)S(1)} %copy-done.8, f32[4]{0:T(128)S(1)} %copy-done.9, f32[136,128]{1,0:T(8,128)S(1)} %add_add_fusion.share_ref.rest_0_, f32[544,512]{1,0:T(8,128)S(1)} %get-tuple-element.79.spectrum_ref, f32[16,72,512]{2,1,0:T(8,128)S(1)} %get-tuple-element.80.power_ref), custom_call_target="tpu_custom_call" | custom-call | bytes 4243500 | tf_op jit(solution)/shard_map/pallas_call | solution.py:107
  29.5 0.0 copy-start.2
  29.5 3.0 %collective-permute-done.4.rest_1_ = f32[128,512]{1,0:T(8,128)S(1)} collective-permute-done((f32[128,512]{1,0:T(8,128)S(1)}, f32[128,512]{1,0:T(8,128)S(1)}, u32[]{:S(2)}, u32[]{:S(2)}) %collective-permute-start.4) | collective-permute-done | bytes 262176 | tf_op jit(solution)/shard_map/ppermute | solution.py:716
  32.5 1.8 %shard_map.152.spectrum_ref = f32[544,512]{1,0:T(8,128)S(1)} custom-call(s32[2]{0:T(128)S(1)} %pad_add_fusion.place_ref, f32[128,512]{1,0:T(8,128)S(1)} %collective-permute-done.3.rest_0_, f32[128,512]{1,0:T(8,128)S(1)} %collective-permute-done.4.rest_1_, f32[128,512]{1,0:T(8,128)S(1)} %collective-permute-done.5.rest_2_, ...), custom_call_target="tpu_custom_call" | custom-call | bytes 6826500 | tf_op jit(solution)/shard_map/pallas_call | solution.py:107
  34.4 1.4 %shard_map.156 = (f32[2,144,128]{2,1,0:T(8,128)S(1)}, f32[2,144,128]{2,1,0:T(8,128)S(1)}, f32[2,144,128]{2,1,0:T(8,128)S(1)}, f32[2,144,128]{2,1,0:T(8,128)S(1)}) custom-call(s32[2]{0:T(128)S(1)} %pad_add_fusion.place_ref, f32[544,512]{1,0:T(8,128)S(1)} %shard_map.152.spectrum_ref, f32[272,512]{1,0:T(8,128)S(1)} %get-tuple-element.81.gain_ref, ...), custom_call_target="tpu_custom_call" | custom-call | bytes 4981500 | tf_op jit(solution)/shard_map/pallas_call | solution.py:107
  35.8 0.1 collective-permute-start.12
  35.9 1.3 %collective-permute-start.13 = (f32[2,144,128]{2,1,0:T(8,128)S(1)}, f32[2,144,128]{2,1,0:T(8,128)S(1)}, u32[]{:S(2)}, u32[]{:S(2)}) collective-permute-start(f32[2,144,128]{2,1,0:T(8,128)S(1)} %get-tuple-element.85), channel_id=1, source_target_pairs={{0,2},{1,3},{2,0},{3,1},{4,6},{5,7},{6,4},{7,5},{8,10},{9,11},{10,... | collective-permute-start | bytes 442376 | tf_op jit(solution)/shard_map/ppermute | solution.py:716
  37.2 0.6 collective-permute-start.14
  37.7 1.4 %shard_map.157 = (f32[2,144,128]{2,1,0:T(8,128)S(1)}, f32[2,144,128]{2,1,0:T(8,128)S(1)}, f32[2,144,128]{2,1,0:T(8,128)S(1)}, f32[2,144,128]{2,1,0:T(8,128)S(1)}) custom-call(s32[2]{0:T(128)S(1)} %pad_add_fusion.place_ref, f32[544,512]{1,0:T(8,128)S(1)} %shard_map.152.spectrum_ref, f32[272,512]{1,0:T(8,128)S(1)} %get-tuple-element.81.gain_ref, ...), custom_call_target="tpu_custom_call" | custom-call | bytes 4981500 | tf_op jit(solution)/shard_map/pallas_call | solution.py:107
  39.1 0.4 collective-permute-start.15
  39.5 1.2 %collective-permute-start.16 = (f32[2,144,128]{2,1,0:T(8,128)S(1)}, f32[2,144,128]{2,1,0:T(8,128)S(1)}, u32[]{:S(2)}, u32[]{:S(2)}) collective-permute-start(f32[2,144,128]{2,1,0:T(8,128)S(1)} %get-tuple-element.89), channel_id=1, source_target_pairs={{0,2},{1,3},{2,0},{3,1},{4,6},{5,7},{6,4},{7,5},{8,10},{9,11},{10,... | collective-permute-start | bytes 442376 | tf_op jit(solution)/shard_map/ppermute | solution.py:716
  40.8 0.3 collective-permute-start.17
  41.1 0.0 copy-start
  41.1 1.0 %shard_map.159.chosen_ref = bf16[8,512,512]{2,1,0:T(8,128)(2,1)S(1)} custom-call(s32[8,512]{1,0:T(8,128)S(1)} %reshape.12.col_ref), custom_call_target="tpu_custom_call" | custom-call | bytes 7380000 | tf_op jit(solution)/shard_map/pallas_call | solution.py:107
  42.1 0.5 collective-permute-done.13.rest_2_.rest_1_
  42.6 2.3 %collective-permute-done.14.rest_3_.rest_0_ = f32[2,144,128]{2,1,0:T(8,128)S(1)} collective-permute-done((f32[2,144,128]{2,1,0:T(8,128)S(1)}, f32[2,144,128]{2,1,0:T(8,128)S(1)}, u32[]{:S(2)}, u32[]{:S(2)}) %collective-permute-start.14) | collective-permute-done | bytes 147488 | tf_op jit(solution)/shard_map/ppermute | solution.py:716
  44.9 4.4 %shard_map.160.rest_5_ = f32[4,2,1024]{2,1,0:T(2,128)S(1)} custom-call(s32[2]{0:T(128)S(1)} %pad_add_fusion.place_ref, s32[8,512]{1,0:T(8,128)S(1)} %reshape.11.row_ref, bf16[8,512,512]{2,1,0:T(8,128)(2,1)S(1)} %shard_map.159.chosen_ref, f32[2,4,64,128]{3,2,1,0:T(8,128)S(1)} %get-tuple-element.91.taps_ref, ...), custom_call_target="tpu_custom_call" | custom-call | bytes 14760000 | tf_op jit(solution)/shard_map/pallas_call | solution.py:107
  49.3 1.9 %collective-permute-done.17.rest_7_.rest_0_ = f32[2,144,128]{2,1,0:T(8,128)S(1)} collective-permute-done((f32[2,144,128]{2,1,0:T(8,128)S(1)}, f32[2,144,128]{2,1,0:T(8,128)S(1)}, u32[]{:S(2)}, u32[]{:S(2)}) %collective-permute-start.17) | collective-permute-done | bytes 147488 | tf_op jit(solution)/shard_map/ppermute | solution.py:716
  51.2 4.4 %shard_map.161 = (f32[4,1024]{1,0:T(4,128)S(1)}, f32[4,1024]{1,0:T(4,128)S(1)}, f32[4,1024]{1,0:T(4,128)S(1)}, f32[4,1024]{1,0:T(4,128)S(1)}) custom-call(s32[2]{0:T(128)S(1)} %pad_add_fusion.place_ref, s32[8,512]{1,0:T(8,128)S(1)} %reshape.11.row_ref, bf16[8,512,512]{2,1,0:T(8,128)(2,1)S(1)} %shard_map.159.chosen_ref, ...), custom_call_target="tpu_custom_call" | custom-call | bytes 14760000 | tf_op jit(solution)/shard_map/pallas_call | solution.py:107
  55.6 0.8 %collective-permute-start.18 = (f32[4,1024]{1,0:T(4,128)S(1)}, f32[4,1024]{1,0:T(4,128)S(1)}, u32[]{:S(2)}, u32[]{:S(2)}) collective-permute-start(f32[4,1024]{1,0:T(4,128)S(1)} %get-tuple-element.92), channel_id=1, source_target_pairs={{0,3},{1,2},{2,1},{3,0},{4,7},{5,6},{6,5},{7,4},{8,11},{9,10},{10,... | collective-permute-start | bytes 49160 | tf_op jit(solution)/shard_map/ppermute | solution.py:716
  56.4 1.1 %collective-permute-start.19 = (f32[4,1024]{1,0:T(4,128)S(1)}, f32[4,1024]{1,0:T(4,128)S(1)}, u32[]{:S(2)}, u32[]{:S(2)}) collective-permute-start(f32[4,1024]{1,0:T(4,128)S(1)} %get-tuple-element.93), channel_id=1, source_target_pairs={{0,2},{1,3},{2,0},{3,1},{4,6},{5,7},{6,4},{7,5},{8,10},{9,11},{10,... | collective-permute-start | bytes 49160 | tf_op jit(solution)/shard_map/ppermute | solution.py:716
  57.6 2.1 %shard_map.158 = f32[4,128,512]{2,1,0:T(8,128)} custom-call(s32[2]{0:T(128)S(1)} %pad_add_fusion.place_ref, f32[2,144,128]{2,1,0:T(8,128)S(1)} %get-tuple-element.83.rest_0_.rest_3_, f32[2,144,128]{2,1,0:T(8,128)S(1)} %collective-permute-done.12.rest_1_.rest_2_, f32[2,144,128]{2,1,0:T(8,128)S(1)} %collective-permute-done.13.rest_2_.rest_1_, ...), custom_call_target="tpu_custom_call" | custom-call | bytes 8118000 | tf_op jit(solution)/shard_map/pallas_call | solution.py:107
  59.7 0.5 collective-permute-done.19
  60.2 0.6 %add_add_fusion.1 = f32[4,1024]{1,0:T(4,128)} fusion(f32[4,1024]{1,0:T(4,128)S(1)} %get-tuple-element.95, f32[4,1024]{1,0:T(4,128)S(1)} %collective-permute-done.20, f32[4,1024]{1,0:T(4,128)S(1)} %collective-permute-done.18, f32[4,1024]{1,0:T(4,128)S(1)} %collective-permute-done.19), kind=kLoop, calls=%fused_computation.1 | loop fusion | flops 12288 | bytes 81920 | tf_op jit(solution)/shard_map/add | solution.py:766
  (36 shorter events, 0.1 us)
Async XLA Ops:
  5.2 7.4 %collective-permute-start = (f32[144,128]{1,0:T(8,128)S(1)}, f32[144,128]{1,0:T(8,128)S(1)}, u32[]{:S(2)}, u32[]{:S(2)}) collective-permute-start(f32[144,128]{1,0:T(8,128)S(1)} %get-tuple-element.49), channel_id=1, source_target_pairs={{0,3},{1,2},{2,1},{3,0},{4,7},{5,6},{6,5},{7,4},{8,11},{9,10},{10,... | collective-permute-start | bytes 221192 | tf_op jit(solution)/shard_map/ppermute | solution.py:716
  7.6 4.9 %collective-permute-start.1 = (f32[144,128]{1,0:T(8,128)S(1)}, f32[144,128]{1,0:T(8,128)S(1)}, u32[]{:S(2)}, u32[]{:S(2)}) collective-permute-start(f32[144,128]{1,0:T(8,128)S(1)} %get-tuple-element.50), channel_id=1, source_target_pairs={{0,2},{1,3},{2,0},{3,1},{4,6},{5,7},{6,4},{7,5},{8,10},{9,11},{10,... | collective-permute-start | bytes 221192 | tf_op jit(solution)/shard_map/ppermute | solution.py:716
  11.2 1.4 %copy-start.1 = (bf16[2,2,2,2,128,256]{5,4,3,2,1,0:T(8,128)(2,1)S(1)}, bf16[2,2,2,2,128,256]{5,4,3,2,1,0:T(8,128)(2,1)}, u32[]{:S(2)}) copy-start(bf16[2,2,2,2,128,256]{5,4,3,2,1,0:T(8,128)(2,1)} %constant.29.clone.rest_4_) | copy-start | bytes 3145732
  11.2 1.4 %copy-start.7 = (s32[4]{0:T(128)S(1)}, s32[4]{0:T(128)}, u32[]{:S(2)}) copy-start(s32[4]{0:T(128)} %index_ref.3) | copy-start | bytes 52
  11.2 1.4 %copy-start.8 = (f32[4]{0:T(128)S(1)}, f32[4]{0:T(128)}, u32[]{:S(2)}) copy-start(f32[4]{0:T(128)} %flux_ref.3) | copy-start | bytes 52
  11.2 1.4 %copy-start.9 = (f32[4]{0:T(128)S(1)}, f32[4]{0:T(128)}, u32[]{:S(2)}) copy-start(f32[4]{0:T(128)} %noise_ref.3) | copy-start | bytes 52
  11.2 8.8 %copy-start.3 = (f32[16,16,16]{2,1,0:T(8,128)S(1)}, f32[16,16,16]{2,1,0:T(8,128)}, u32[]{:S(2)}) copy-start(f32[16,16,16]{2,1,0:T(8,128)} %bank_ref) | copy-start | bytes 49156
  11.2 8.8 %copy-start.4 = (bf16[2,4,144,32]{3,2,1,0:T(8,128)(2,1)S(1)}, bf16[2,4,144,32]{3,2,1,0:T(8,128)(2,1)}, u32[]{:S(2)}) copy-start(bf16[2,4,144,32]{3,2,1,0:T(8,128)(2,1)} %constant.30.clone.shift_ref) | copy-start | bytes 221188
  11.2 8.8 %copy-start.5 = (f32[16,1024]{1,0:T(8,128)S(1)}, f32[16,1024]{1,0:T(8,128)}, u32[]{:S(2)}) copy-start(f32[16,1024]{1,0:T(8,128)} %constant.27.clone.rest_4_.coef_ref) | copy-start | bytes 196612
  11.2 8.7 %copy-start.6 = (bf16[128,512]{1,0:T(8,128)(2,1)S(1)}, bf16[128,512]{1,0:T(8,128)(2,1)}, u32[]{:S(2)}) copy-start(bf16[128,512]{1,0:T(8,128)(2,1)} %constant.31.clone.spread_ref) | copy-start | bytes 393220
  11.3 1.3 %collective-permute-start.2 = (f32[144,128]{1,0:T(8,128)S(1)}, f32[144,128]{1,0:T(8,128)S(1)}, u32[]{:S(2)}, u32[]{:S(2)}) collective-permute-start(f32[144,128]{1,0:T(8,128)S(1)} %get-tuple-element.54), channel_id=1, source_target_pairs={{0,1},{1,0},{2,3},{3,2},{4,5},{5,4},{6,7},{7,6},{8,9},{9,8},{10,11... | collective-permute-start | bytes 221192 | tf_op jit(solution)/shard_map/ppermute | solution.py:716
  13.8 8.6 %collective-permute-start.6 = (f32[136,128]{1,0:T(8,128)S(1)}, f32[136,128]{1,0:T(8,128)S(1)}, u32[]{:S(2)}, u32[]{:S(2)}) collective-permute-start(f32[136,128]{1,0:T(8,128)S(1)} %get-tuple-element.72), channel_id=1, source_target_pairs={{0,12},{4,8},{8,4},{12,0},{1,13},{5,9},{9,5},{13,1},{2,14},{6,10},... | collective-permute-start | bytes 208904 | tf_op jit(solution)/shard_map/ppermute | solution.py:716
  17.7 6.2 %collective-permute-start.7 = (f32[136,128]{1,0:T(8,128)S(1)}, f32[136,128]{1,0:T(8,128)S(1)}, u32[]{:S(2)}, u32[]{:S(2)}) collective-permute-start(f32[136,128]{1,0:T(8,128)S(1)} %get-tuple-element.73), channel_id=1, source_target_pairs={{0,8},{4,12},{8,0},{12,4},{1,9},{5,13},{9,1},{13,5},{2,10},{6,14},... | collective-permute-start | bytes 208904 | tf_op jit(solution)/shard_map/ppermute | solution.py:716
  17.7 6.2 %collective-permute-start.8 = (f32[136,128]{1,0:T(8,128)S(1)}, f32[136,128]{1,0:T(8,128)S(1)}, u32[]{:S(2)}, u32[]{:S(2)}) collective-permute-start(f32[136,128]{1,0:T(8,128)S(1)} %get-tuple-element.74), channel_id=1, source_target_pairs={{0,4},{4,0},{8,12},{12,8},{1,5},{5,1},{9,13},{13,9},{2,6},{6,2},{1... | collective-permute-start | bytes 208904 | tf_op jit(solution)/shard_map/ppermute | solution.py:716
  18.3 8.4 %collective-permute-start.3 = (f32[128,512]{1,0:T(8,128)S(1)}, f32[128,512]{1,0:T(8,128)S(1)}, u32[]{:S(2)}, u32[]{:S(2)}) collective-permute-start(f32[128,512]{1,0:T(8,128)S(1)} %get-tuple-element.60), channel_id=1, source_target_pairs={{0,3},{1,2},{2,1},{3,0},{4,7},{5,6},{6,5},{7,4},{8,11},{9,10},{10,... | collective-permute-start | bytes 786440 | tf_op jit(solution)/shard_map/ppermute | solution.py:716
  19.0 13.6 %collective-permute-start.4 = (f32[128,512]{1,0:T(8,128)S(1)}, f32[128,512]{1,0:T(8,128)S(1)}, u32[]{:S(2)}, u32[]{:S(2)}) collective-permute-start(f32[128,512]{1,0:T(8,128)S(1)} %get-tuple-element.61), channel_id=1, source_target_pairs={{0,2},{1,3},{2,0},{3,1},{4,6},{5,7},{6,4},{7,5},{8,10},{9,11},{10,... | collective-permute-start | bytes 786440 | tf_op jit(solution)/shard_map/ppermute | solution.py:716
  22.3 10.2 %collective-permute-start.5 = (f32[128,512]{1,0:T(8,128)S(1)}, f32[128,512]{1,0:T(8,128)S(1)}, u32[]{:S(2)}, u32[]{:S(2)}) collective-permute-start(f32[128,512]{1,0:T(8,128)S(1)} %get-tuple-element.62), channel_id=1, source_target_pairs={{0,1},{1,0},{2,3},{3,2},{4,5},{5,4},{6,7},{7,6},{8,9},{9,8},{10,11... | collective-permute-start | bytes 786440 | tf_op jit(solution)/shard_map/ppermute | solution.py:716
  23.9 10.5 %collective-permute-start.11 = (f32[136,128]{1,0:T(8,128)S(1)}, f32[136,128]{1,0:T(8,128)S(1)}, u32[]{:S(2)}, u32[]{:S(2)}) collective-permute-start(f32[136,128]{1,0:T(8,128)S(1)} %add_add_fusion.share_ref.rest_0_), channel_id=1, source_target_pairs={{0,12},{4,8},{8,4},{12,0},{1,13},{5,9},{9,5},{13,1},{2,14},{6,10},... | collective-permute-start | bytes 208904 | tf_op jit(solution)/shard_map/ppermute | solution.py:716
  26.5 7.9 %collective-permute-start.10 = (f32[136,128]{1,0:T(8,128)S(1)}, f32[136,128]{1,0:T(8,128)S(1)}, u32[]{:S(2)}, u32[]{:S(2)}) collective-permute-start(f32[136,128]{1,0:T(8,128)S(1)} %add_add_fusion.share_ref.rest_0_), channel_id=1, source_target_pairs={{0,8},{4,12},{8,0},{12,4},{1,9},{5,13},{9,1},{13,5},{2,10},{6,14},... | collective-permute-start | bytes 208904 | tf_op jit(solution)/shard_map/ppermute | solution.py:716
  26.8 7.7 %collective-permute-start.9 = (f32[136,128]{1,0:T(8,128)S(1)}, f32[136,128]{1,0:T(8,128)S(1)}, u32[]{:S(2)}, u32[]{:S(2)}) collective-permute-start(f32[136,128]{1,0:T(8,128)S(1)} %add_add_fusion.share_ref.rest_0_), channel_id=1, source_target_pairs={{0,4},{4,0},{8,12},{12,8},{1,5},{5,1},{9,13},{13,9},{2,6},{6,2},{1... | collective-permute-start | bytes 208904 | tf_op jit(solution)/shard_map/ppermute | solution.py:716
  29.5 4.9 %copy-start.2 = (bf16[2,2,256,512]{3,2,1,0:T(8,128)(2,1)S(1)}, bf16[2,2,256,512]{3,2,1,0:T(8,128)(2,1)}, u32[]{:S(2)}) copy-start(bf16[2,2,256,512]{3,2,1,0:T(8,128)(2,1)} %constant.32.clone.rest_4_) | copy-start | bytes 3145732
  35.8 5.0 %collective-permute-start.12 = (f32[2,144,128]{2,1,0:T(8,128)S(1)}, f32[2,144,128]{2,1,0:T(8,128)S(1)}, u32[]{:S(2)}, u32[]{:S(2)}) collective-permute-start(f32[2,144,128]{2,1,0:T(8,128)S(1)} %get-tuple-element.84), channel_id=1, source_target_pairs={{0,1},{1,0},{2,3},{3,2},{4,5},{5,4},{6,7},{7,6},{8,9},{9,8},{10,11... | collective-permute-start | bytes 442376 | tf_op jit(solution)/shard_map/ppermute | solution.py:716
  35.9 6.7 %collective-permute-start.13 = (f32[2,144,128]{2,1,0:T(8,128)S(1)}, f32[2,144,128]{2,1,0:T(8,128)S(1)}, u32[]{:S(2)}, u32[]{:S(2)}) collective-permute-start(f32[2,144,128]{2,1,0:T(8,128)S(1)} %get-tuple-element.85), channel_id=1, source_target_pairs={{0,2},{1,3},{2,0},{3,1},{4,6},{5,7},{6,4},{7,5},{8,10},{9,11},{10,... | collective-permute-start | bytes 442376 | tf_op jit(solution)/shard_map/ppermute | solution.py:716
  37.2 3.9 %copy-start.10 = (s32[4096]{0:T(1024)S(1)}, s32[4096]{0:T(1024)}, u32[]{:S(2)}) copy-start(s32[4096]{0:T(1024)} %param.19) | copy-start | bytes 49156
  37.2 3.9 %copy-start.11 = (s32[4096]{0:T(1024)S(1)}, s32[4096]{0:T(1024)}, u32[]{:S(2)}) copy-start(s32[4096]{0:T(1024)} %param.20) | copy-start | bytes 49156
  37.2 7.7 %collective-permute-start.14 = (f32[2,144,128]{2,1,0:T(8,128)S(1)}, f32[2,144,128]{2,1,0:T(8,128)S(1)}, u32[]{:S(2)}, u32[]{:S(2)}) collective-permute-start(f32[2,144,128]{2,1,0:T(8,128)S(1)} %get-tuple-element.86), channel_id=1, source_target_pairs={{0,3},{1,2},{2,1},{3,0},{4,7},{5,6},{6,5},{7,4},{8,11},{9,10},{10,... | collective-permute-start | bytes 442376 | tf_op jit(solution)/shard_map/ppermute | solution.py:716
  39.1 10.2 %collective-permute-start.15 = (f32[2,144,128]{2,1,0:T(8,128)S(1)}, f32[2,144,128]{2,1,0:T(8,128)S(1)}, u32[]{:S(2)}, u32[]{:S(2)}) collective-permute-start(f32[2,144,128]{2,1,0:T(8,128)S(1)} %get-tuple-element.88), channel_id=1, source_target_pairs={{0,1},{1,0},{2,3},{3,2},{4,5},{5,4},{6,7},{7,6},{8,9},{9,8},{10,11... | collective-permute-start | bytes 442376 | tf_op jit(solution)/shard_map/ppermute | solution.py:716
  39.5 9.8 %collective-permute-start.16 = (f32[2,144,128]{2,1,0:T(8,128)S(1)}, f32[2,144,128]{2,1,0:T(8,128)S(1)}, u32[]{:S(2)}, u32[]{:S(2)}) collective-permute-start(f32[2,144,128]{2,1,0:T(8,128)S(1)} %get-tuple-element.89), channel_id=1, source_target_pairs={{0,2},{1,3},{2,0},{3,1},{4,6},{5,7},{6,4},{7,5},{8,10},{9,11},{10,... | collective-permute-start | bytes 442376 | tf_op jit(solution)/shard_map/ppermute | solution.py:716
  40.8 10.4 %collective-permute-start.17 = (f32[2,144,128]{2,1,0:T(8,128)S(1)}, f32[2,144,128]{2,1,0:T(8,128)S(1)}, u32[]{:S(2)}, u32[]{:S(2)}) collective-permute-start(f32[2,144,128]{2,1,0:T(8,128)S(1)} %get-tuple-element.90), channel_id=1, source_target_pairs={{0,3},{1,2},{2,1},{3,0},{4,7},{5,6},{6,5},{7,4},{8,11},{9,10},{10,... | collective-permute-start | bytes 442376 | tf_op jit(solution)/shard_map/ppermute | solution.py:716
  41.1 3.8 %copy-start = (bf16[2,4,128,256]{3,2,1,0:T(8,128)(2,1)S(1)}, bf16[2,4,128,256]{3,2,1,0:T(8,128)(2,1)}, u32[]{:S(2)}) copy-start(bf16[2,4,128,256]{3,2,1,0:T(8,128)(2,1)} %constant.33.clone.rest_8_.rest_4_) | copy-start | bytes 1572868
  55.6 4.1 %collective-permute-start.18 = (f32[4,1024]{1,0:T(4,128)S(1)}, f32[4,1024]{1,0:T(4,128)S(1)}, u32[]{:S(2)}, u32[]{:S(2)}) collective-permute-start(f32[4,1024]{1,0:T(4,128)S(1)} %get-tuple-element.92), channel_id=1, source_target_pairs={{0,3},{1,2},{2,1},{3,0},{4,7},{5,6},{6,5},{7,4},{8,11},{9,10},{10,... | collective-permute-start | bytes 49160 | tf_op jit(solution)/shard_map/ppermute | solution.py:716
  56.4 3.7 %collective-permute-start.19 = (f32[4,1024]{1,0:T(4,128)S(1)}, f32[4,1024]{1,0:T(4,128)S(1)}, u32[]{:S(2)}, u32[]{:S(2)}) collective-permute-start(f32[4,1024]{1,0:T(4,128)S(1)} %get-tuple-element.93), channel_id=1, source_target_pairs={{0,2},{1,3},{2,0},{3,1},{4,6},{5,7},{6,4},{7,5},{8,10},{9,11},{10,... | collective-permute-start | bytes 49160 | tf_op jit(solution)/shard_map/ppermute | solution.py:716
  57.6 2.6 %collective-permute-start.20 = (f32[4,1024]{1,0:T(4,128)S(1)}, f32[4,1024]{1,0:T(4,128)S(1)}, u32[]{:S(2)}, u32[]{:S(2)}) collective-permute-start(f32[4,1024]{1,0:T(4,128)S(1)} %get-tuple-element.94), channel_id=1, source_target_pairs={{0,1},{1,0},{2,3},{3,2},{4,5},{5,4},{6,7},{7,6},{8,9},{9,8},{10,11... | collective-permute-start | bytes 49160 | tf_op jit(solution)/shard_map/ppermute | solution.py:716

commit v3 on v2

--- a/solution.py
+++ b/solution.py
@@ -13,6 +13,7 @@
 vmem_limit = 40 * 1024 * 1024
 bf16, f32 = jnp.bfloat16, jnp.float32
 hbm_rate = 3.69e6
+slab_axes = ("tile", "sub")
 edge_rows = 16
 
 
@@ -25,6 +26,10 @@
 def split(value):
     high = value.astype(bf16)
     return high, (value - high.astype(f32)).astype(bf16)
+
+
+def slab_of():
+    return lax.axis_index(slab_axes)
 
 
 def angle(first, second, length):
@@ -194,14 +199,14 @@
     ]
 
 
-def row_transform_far(plan, place, index, flux, noise, images, bank):
+def row_transform_far(plan, index, flux, noise, images, bank, piece):
     epochs = images.shape[0]
     slabs, pairs, lanes, tall, stamp = plan.slabs, plan.pairs, plan.lanes, plan.tall, plan.stamp
 
-    def kernel(place_ref, *rest):
+    def kernel(*rest):
         sources, outs, rest = rest[:7], rest[7 : 7 + pairs], rest[7 + pairs :]
-        taps_ref, x_ref, table_ref, index_ref, flux_ref, noise_ref, bank_ref, coef_ref = rest[:8]
-        padded, gathered, sems = rest[8:]
+        shares_ref, taps_ref, x_ref, table_ref, index_ref, flux_ref, noise_ref, bank_ref, coef_ref = rest[:9]
+        padded, gathered, sems = rest[9:]
         targets = [index_ref, flux_ref, noise_ref, bank_ref, coef_ref, x_ref, table_ref]
         copies = [pltpu.make_async_copy(sources[i], targets[i], sems.at[i]) for i in range(7)]
         for copy in copies:
@@ -212,15 +217,21 @@
             plan, bank_ref, coef_ref, index_ref, epochs,
             lambda e, own: own * (flux_ref[e] / (noise_ref[e] * noise_ref[e])), taps_ref,
         )
+        lane = lax.broadcasted_iota(jnp.int32, (1, piece), 1)
+        shares = jnp.zeros((1, piece), f32)
+        for e in range(epochs):
+            ratio = flux_ref[e] / noise_ref[e]
+            shares += jnp.where(lane == index_ref[e], ratio * ratio, 0.0)
+        shares_ref[...] = shares
         for copy in copies[5:]:
             copy.wait()
-        coadd_rows(plan, place_ref[0], 1, x_ref, table_ref, taps_ref, padded, gathered, outs)
+        coadd_rows(plan, slab_of(), 1, x_ref, table_ref, taps_ref, padded, gathered, outs)
 
     flat = call(
         kernel,
         [("v", (tall, lanes))] * pairs
-        + [("v", (2, slabs, epochs * stamp, lanes)), ("v", images.shape), ("v", plan.ahead.shape, bf16)],
-        [("s", place), ("m", index), ("m", flux), ("m", noise), ("m", bank), ("m", plan.coef),
+        + [("v", (1, piece)), ("v", (2, slabs, epochs * stamp, lanes)), ("v", images.shape), ("v", plan.ahead.shape, bf16)],
+        [("m", index), ("m", flux), ("m", noise), ("m", bank), ("m", plan.coef),
          ("m", images), ("m", plan.ahead)],
         [pltpu.SMEM(index.shape, jnp.int32), pltpu.SMEM(flux.shape, f32), pltpu.SMEM(noise.shape, f32),
          pltpu.VMEM(bank.shape, f32), pltpu.VMEM(plan.coef.shape, f32)]
@@ -230,27 +241,27 @@
     return list(flat[:pairs]), *flat[pairs:]
 
 
-def row_transform_near(plan, place, taps, images, table):
+def row_transform_near(plan, taps, images, table):
     pairs = plan.pairs
 
-    def kernel(place_ref, taps_ref, x_ref, table_ref, *rest):
-        coadd_rows(plan, place_ref[0], 0, x_ref, table_ref, taps_ref, *rest[pairs:], rest[:pairs])
+    def kernel(taps_ref, x_ref, table_ref, *rest):
+        coadd_rows(plan, slab_of(), 0, x_ref, table_ref, taps_ref, *rest[pairs:], rest[:pairs])
 
     return list(call(
         kernel,
         [("v", (plan.tall, plan.lanes))] * pairs,
-        [("s", place), ("v", taps), ("v", images), ("v", table)],
+        [("v", taps), ("v", images), ("v", table)],
         coadd_scratch(plan, images.shape[0]),
         micros=3.2,
     ))
 
 
-def row_transform(plan, place, images, table, parties):
+def row_transform(plan, images, table, parties):
     slabs, pairs, lanes, rows = plan.slabs, plan.pairs, plan.lanes, plan.rows
 
-    def kernel(place_ref, x_ref, table_ref, *outs):
+    def kernel(x_ref, table_ref, *outs):
         for group in range(2):
-            data, table = row_operands(plan, place_ref[0], group, x_ref, table_ref)
+            data, table = row_operands(plan, slab_of(), group, x_ref, table_ref)
             result = mul3(table, data, True)
             for i, (begin, end) in enumerate(parties):
                 for m in range(pairs):
@@ -261,24 +272,23 @@
     flat = call(
         kernel,
         [("v", (lanes, (end - begin) * rows)) for begin, end in parties for _ in range(slabs)],
-        [("s", place), ("v", images), ("v", table)],
+        [("v", images), ("v", table)],
         micros=1.3,
     )
     return [list(flat[i * slabs : (i + 1) * slabs]) for i in range(len(parties))]
 
 
-def numerator(plan, place, index, flux, noise, blocks, pieces):
+def numerator(plan, shares, blocks, pieces):
     slabs, cols, rows, half, side, lanes, halo, tall = (
         plan.slabs, plan.cols, plan.rows, plan.half, plan.side, plan.lanes, plan.halo, plan.tall,
     )
-    epochs = index.shape[0]
     piece = side // pieces
 
-    def kernel(place_ref, index_ref, flux_ref, noise_ref, *rest):
+    def kernel(shares_ref, *rest):
         ins, table_ref = rest[:slabs], rest[slabs]
         outs = rest[slabs + 1 : slabs + 1 + pieces]
         whole, parts = rest[slabs + 1 + pieces :]
-        q, z = place_ref[0], place_ref[1] if pieces > 1 else 0
+        q, z = slab_of(), lax.axis_index("epoch") if pieces > 1 else 0
         whole[...] = jnp.zeros((side + 2 * halo, lanes), f32)
         for m in range(slabs):
             at = pl.multiple_of((q ^ m) * rows, rows)
@@ -311,27 +321,22 @@
             for i in range(half // step):
                 at = odd * half + i * step
                 parts[at // piece, :, at % piece : at % piece + step] = plane[:, i * step : (i + 1) * step]
-        lane = lax.broadcasted_iota(jnp.int32, (1, piece), 1)
-        shares = jnp.zeros((1, piece), f32)
-        for e in range(epochs):
-            ratio = flux_ref[e] / noise_ref[e]
-            shares += jnp.where(lane == index_ref[e], ratio * ratio, 0.0)
         for m in range(pieces):
-            parts[m, lanes + 2 : lanes + 3] = shares
+            parts[m, lanes + 2 : lanes + 3] = shares_ref[...]
         for m in range(pieces):
             outs[m][...] = parts[z ^ m]
 
     return call(
         kernel,
         [("v", (lanes + 8, piece))] * pieces,
-        [("s", place), ("s", index), ("s", flux), ("s", noise)] + [("v", b) for b in reversed(blocks)]
+        [("v", shares)] + [("v", b) for b in reversed(blocks)]
         + [("v", plan.down)],
         [pltpu.VMEM((side + 2 * halo, lanes), f32), pltpu.VMEM((pieces, lanes + 8, piece), f32)],
         micros=1.15,
     )
 
 
-def psf_planes(plan, place, bank, index):
+def psf_planes(plan, bank, index):
     epochs = index.shape[0]
     count, stamp = bank.shape[:2]
     side, cols, band, slabs, lanes = plan.side, plan.cols, plan.band, plan.slabs, plan.lanes
@@ -340,10 +345,10 @@
     pitch = 8 * stamp
 
     def kernel(
-        place_ref, index_ref, bank_ref, shift_ref, spread_ref, coef_ref,
+        index_ref, bank_ref, shift_ref, spread_ref, coef_ref,
         spectrum_ref, power_ref, taps_ref, right_ref, plane_ref,
     ):
-        q = place_ref[0]
+        q = slab_of()
         stamps = bank_ref[...]
         stamps = stamps / jnp.sum(jnp.sum(stamps, axis=2, keepdims=True), axis=1, keepdims=True)
         blank = jnp.zeros((stamp, stamp), f32)
@@ -381,7 +386,7 @@
     return call(
         kernel,
         [("v", (2 * size, side)), ("v", (count, band, side)), ("v", (2, slabs, epochs * stamp, lanes))],
-        [("s", place), ("s", index), ("v", bank), ("v", plan.shift), ("v", plan.spread), ("v", plan.coef)],
+        [("s", index), ("v", bank), ("v", plan.shift), ("v", plan.spread), ("v", plan.coef)],
         [pltpu.VMEM((count * pitch, 2 * stamp), f32), pltpu.VMEM((count, 2 * band, side), f32)],
         micros=2.35,
     )
@@ -431,16 +436,21 @@
     )
 
 
-def column_transform(plan, place, blocks):
-    slabs, pairs, cols, rows, half, side = plan.slabs, plan.pairs, plan.cols, plan.rows, plan.half, plan.side
+def column_transform(plan, members, blocks, partial):
+    pairs, cols, rows, half, side = plan.pairs, plan.cols, plan.rows, plan.half, plan.side
     epochs = blocks[0].shape[1] // rows
     body = epochs * cols
     size = body + edge_rows
-
-    def kernel(place_ref, *rest):
-        ins = rest[:slabs][::-1]
-        table_ref, plane_ref, left_high, left_low = rest[slabs:]
-        q = place_ref[0]
+    count = len(members)
+    depth = count * rows
+
+    def kernel(*rest):
+        far, near = rest[:count], rest[count : 2 * count]
+        table_ref, rest = rest[2 * count], rest[2 * count + 1 :]
+        if partial is not None:
+            partial_ref, rest = rest[0], rest[1:]
+        plane_ref, left_high, left_low = rest
+        q = slab_of()
         first = (q == 0).astype(f32)
         sign = jnp.where(q < pairs, 1.0, -1.0).astype(f32)
         row = lax.broadcasted_iota(jnp.int32, (cols, rows), 0)
@@ -451,42 +461,48 @@
             left_high[where], left_low[where] = split(entry)
 
         for odd in range(2):
-            for m in range(pairs):
-                near, far = ins[m][...], ins[m + pairs][...]
-                value = sign * (near - far) if odd else near + far
+            for n in range(count):
+                lower, upper = near[n][...], far[n][...]
+                value = sign * (lower - upper) if odd else lower + upper
                 edges = []
                 for e in range(epochs):
                     re = value[:cols, e * rows : (e + 1) * rows]
                     im = value[cols:, e * rows : (e + 1) * rows]
                     edges.append(im[:1] * first)
                     im = im * keep
-                    put(e * cols, m * rows, re)
-                    put(e * cols, half + m * rows, im)
-                    put(size + e * cols, m * rows, im)
-                    put(size + e * cols, half + m * rows, -re)
+                    put(e * cols, n * rows, re)
+                    put(e * cols, depth + n * rows, im)
+                    put(size + e * cols, n * rows, im)
+                    put(size + e * cols, depth + n * rows, -re)
                 edge = jnp.concatenate(edges + [jnp.zeros((edge_rows - epochs, rows), f32)], 0)
-                put(body, m * rows, edge)
-                put(body, half + m * rows, jnp.zeros_like(edge))
-                put(size + body, m * rows, jnp.zeros_like(edge))
-                put(size + body, half + m * rows, -edge)
-            order = [(q ^ m) % pairs for m in range(pairs)]
+                put(body, n * rows, edge)
+                put(body, depth + n * rows, jnp.zeros_like(edge))
+                put(size + body, n * rows, jnp.zeros_like(edge))
+                put(size + body, depth + n * rows, -edge)
+            order = [(q ^ m) % pairs for m in members]
             table = [
                 jnp.concatenate([table_ref[n, odd, kind, i] for kind in range(2) for i in order], 0)
                 for n in range(2)
             ]
-            plane_ref[:, odd * half : (odd + 1) * half] = mul3((left_high[...], left_low[...]), table)
-
+            here = slice(odd * half, (odd + 1) * half)
+            plane = mul3((left_high[...], left_low[...]), table)
+            plane_ref[:, here] = plane if partial is None else plane + partial_ref[:, here]
+
+    ins = [("v", blocks[m + pairs]) for m in members] + [("v", blocks[m]) for m in members]
+    ins.append(("v", plan.down))
+    if partial is not None:
+        ins.append(("v", partial))
     (plane,) = call(
         kernel,
         [("v", (2 * size, side))],
-        [("s", place)] + [("v", b) for b in reversed(blocks)] + [("v", plan.down)],
-        [pltpu.VMEM((2 * size, side), bf16), pltpu.VMEM((2 * size, side), bf16)],
-        micros=1.85,
+        ins,
+        [pltpu.VMEM((2 * size, 2 * depth), bf16), pltpu.VMEM((2 * size, 2 * depth), bf16)],
+        micros=1.0,
     )
     return plane
 
 
-def column_inverse(plan, place, spectrum, gain, cross, numer, begin, end):
+def column_inverse(plan, spectrum, gain, cross, numer, begin, end):
     slabs, cols, rows, half, side, lanes, halo, tall = (
         plan.slabs, plan.cols, plan.rows, plan.half, plan.side, plan.lanes, plan.halo, plan.tall,
     )
@@ -496,11 +512,11 @@
     pieces = len(numer)
     piece = side // pieces
 
-    def kernel(place_ref, spectrum_ref, gain_ref, cross_ref, *rest):
+    def kernel(spectrum_ref, gain_ref, cross_ref, *rest):
         numer_refs, table_ref = rest[:pieces], rest[pieces]
         outs = rest[pieces + 1 : pieces + 1 + slabs]
         whole, right_high, right_low, planes = rest[pieces + 1 + slabs :]
-        q, z = place_ref[0], place_ref[1] if pieces > 1 else 0
+        q, z = slab_of(), lax.axis_index("epoch") if pieces > 1 else 0
         for m in range(pieces):
             whole[z ^ m] = numer_refs[m][...]
         flag = jnp.broadcast_to(q, (cols, half)) == 0
@@ -554,7 +570,7 @@
     return call(
         kernel,
         [("v", (epochs, tall, lanes))] * slabs,
-        [("s", place), ("v", spectrum), ("v", gain), ("v", cross)] + [("v", n) for n in numer]
+        [("v", spectrum), ("v", gain), ("v", cross)] + [("v", n) for n in numer]
         + [("v", plan.up)],
         [pltpu.VMEM((pieces, lanes + 8, piece), f32),
          pltpu.VMEM((epochs * lanes, side), bf16), pltpu.VMEM((epochs * lanes, side), bf16),
@@ -592,17 +608,17 @@
     return sums[0] + sums[1], sign * (sums[0] - sums[1])
 
 
-def row_images(plan, place, returned):
+def row_images(plan, returned):
     slabs, rows, half, side, lanes, halo = (
         plan.slabs, plan.rows, plan.half, plan.side, plan.lanes, plan.halo,
     )
     counts = [blocks[0].shape[0] for blocks in returned]
     epochs = sum(counts)
 
-    def kernel(place_ref, *rest):
+    def kernel(*rest):
         ins, table_ref, diff_ref = rest[: -6], rest[-6], rest[-5]
         left_high, left_low, image_ref, sems = rest[-4:]
-        q = place_ref[0]
+        q = slab_of()
         copies = []
         begin = 0
         for i, count in enumerate(counts):
@@ -627,16 +643,33 @@
     (difference,) = call(
         kernel,
         [("h", (epochs, rows, side))],
-        [("s", place)] + [("v", b) for blocks in returned for b in blocks] + [("v", plan.back)],
+        [("v", b) for blocks in returned for b in blocks] + [("v", plan.back)],
         [left, left, pltpu.VMEM((epochs, rows, side), f32), pltpu.SemaphoreType.DMA((len(counts),))],
         micros=2.2,
     )
     return difference
 
 
-def row_fluxes(plan, place, blocks, taps, begin, epochs, earlier, src_row, chosen):
-    slabs, rows, half, side, lanes, stamp = (
-        plan.slabs, plan.rows, plan.half, plan.side, plan.lanes, plan.stamp,
+def pick(plan, q, flux_ref, chosen_ref, row_ref, groups):
+    rows = plan.rows
+    total = flux_ref.shape[0] // 2
+    line = lax.broadcasted_iota(jnp.int32, (rows, row_ref.shape[1]), 0)
+    parts = []
+    for g in groups:
+        values = mul(flux_ref[...], chosen_ref[g])
+        values = values[:total] + values[total:]
+        inside = line == row_ref[pl.ds(g, 1)] - q * rows
+        found = [
+            jnp.sum(jnp.where(inside, values[at : at + rows], 0.0), axis=0, keepdims=True)
+            for at in range(0, total, rows)
+        ]
+        parts.append(jnp.concatenate(found, 0))
+    return jnp.concatenate(parts, 1)
+
+
+def row_fluxes(plan, blocks, taps, begin, epochs, src_row, chosen, earlier):
+    slabs, pairs, rows, half, side, lanes, stamp = (
+        plan.slabs, plan.pairs, plan.rows, plan.half, plan.side, plan.lanes, plan.stamp,
     )
     mine = blocks[0].shape[0]
     groups, group = src_row.shape
@@ -645,14 +678,12 @@
     step = min(64, rows)
     last = begin + mine == epochs
 
-    def kernel(place_ref, row_ref, chosen_ref, taps_ref, *rest):
-        ins, table_ref = rest[:slabs][::-1], rest[slabs]
-        rest = rest[slabs + 1 :]
+    def kernel(row_ref, chosen_ref, taps_ref, *rest):
+        ins, table_ref, rest = rest[:slabs][::-1], rest[slabs], rest[slabs + 1 :]
         if begin:
             earlier_ref, rest = rest[0], rest[1:]
-        outs = rest[:-4]
-        left_high, left_low, flux_ref, picked = rest[-4:]
-        q = place_ref[0]
+        flux_ref, *outs, left_high, left_low = rest
+        q = slab_of()
         for m in range(slabs):
             d = q ^ m
             here = slice(m * lanes, (m + 1) * lanes)
@@ -676,37 +707,48 @@
         ):
             here = slice(part * half, (part + 1) * half)
             flux_ref[:total, here], flux_ref[total:, here] = split(value)
-        line = lax.broadcasted_iota(jnp.int32, (rows, group), 0)
-        for g in range(groups):
-            values = mul(flux_ref[...], chosen_ref[g])
-            values = values[:total] + values[total:]
-            inside = line == row_ref[g : g + 1] - q * rows
-            found = [
-                jnp.sum(
-                    jnp.where(inside, values[e * rows : (e + 1) * rows], 0.0), axis=0, keepdims=True
-                )
-                for e in range(mine)
-            ]
-            where = (g % each) * group
-            picked[g // each, :, where : where + group] = jnp.concatenate(found, 0)
-        for m in range(slabs):
-            out = outs[m] if last else outs[0].at[m]
+        for m in range(1 if last else 0, slabs):
             owner = q ^ m if last else m
+            out = outs[m - 1] if last else outs[0].at[m]
             if begin:
                 out[:begin] = earlier_ref[owner]
-            out[begin:] = picked[owner]
-
-    ins = [("s", place), ("v", src_row), ("v", chosen), ("v", taps)]
+            out[begin:] = pick(
+                plan, q, flux_ref, chosen_ref, row_ref, [owner * each + i for i in range(each)]
+            )
+
+    left = pltpu.VMEM((total, side), bf16)
+    shape = (begin + mine, each * group)
+    ins = [("v", src_row), ("v", chosen), ("v", taps)]
     ins += [("v", b) for b in reversed(blocks)] + [("v", plan.back)]
     if begin:
         ins.append(("v", earlier))
-    left = pltpu.VMEM((total, side), bf16)
+    flux, *picked = call(
+        kernel,
+        [("v", (2 * total, side), bf16)] + ([("v", shape)] * (slabs - 1) if last else [("v", (slabs, *shape))]),
+        ins,
+        [left, left],
+        micros=3.5,
+    )
+    return flux, picked
+
+
+def own_fluxes(plan, flux, begin, src_row, chosen, earlier):
+    groups, group = src_row.shape
+    each = groups // plan.slabs
+    epochs = begin + flux.shape[0] // 2 // plan.rows
+
+    def kernel(row_ref, chosen_ref, flux_ref, *rest):
+        out, q = rest[-1], slab_of()
+        if begin:
+            out[:begin] = rest[0][q]
+        out[begin:] = pick(plan, q, flux_ref, chosen_ref, row_ref, [q * each + i for i in range(each)])
+
+    ins = [("v", src_row), ("v", chosen), ("v", flux)]
     return call(
         kernel,
-        [("v", (epochs, each * group))] * slabs if last else [("v", (slabs, begin + mine, each * group))],
-        ins,
-        [left, left, pltpu.VMEM((2 * total, side), bf16), pltpu.VMEM((slabs, mine, each * group), f32)],
-        micros=4.0,
+        [("v", (epochs, each * group))],
+        ins + ([("v", earlier)] if begin else []),
+        micros=0.9,
     )
 
 
@@ -720,12 +762,10 @@
 def make_shards(mesh):
     slabs = mesh.shape["tile"] * mesh.shape["sub"]
     ranks = mesh.shape["epoch"]
-    slab_axes = ("tile", "sub")
 
     def shards(epoch_images, psf_bank, psf_index, flux_scale, noise_level, src_row, src_col):
         epochs, rows, side = epoch_images.shape
         plan = Plan(side, slabs, psf_bank.shape[1])
-        place = jnp.stack([lax.axis_index(slab_axes), lax.axis_index("epoch")]).astype(jnp.int32)
         direct = ranks & (ranks - 1) == 0 and side // ranks % 128 == 0
         pieces = ranks if direct else 1
         group = math.gcd(512, src_row.shape[0] // slabs)
@@ -734,14 +774,16 @@
         edges = list(range(0, epochs, 2)) + [epochs]
         parties = list(zip(edges, edges[1:]))
 
-        far, weighted, images, table = row_transform_far(plan, place, *scalars, epoch_images, psf_bank)
-        near = row_transform_near(plan, place, weighted, images, table)
-        (blocks,) = row_transform(plan, place, images, table, [(0, epochs)])
+        far, shares, weighted, images, table = row_transform_far(
+            plan, *scalars, epoch_images, psf_bank, side // pieces
+        )
+        near = row_transform_near(plan, weighted, images, table)
+        (blocks,) = row_transform(plan, images, table, [(0, epochs)])
         numer = trade(near + far, slab_axes, slabs)
         numer, blocks = lax.optimization_barrier((numer[::-1], blocks))
-        numer = numerator(plan, place, *scalars, numer[::-1], pieces)
+        numer = numerator(plan, shares, numer[::-1], pieces)
         bank, numer = lax.optimization_barrier((psf_bank, numer))
-        spectrum, power, taps = psf_planes(plan, place, bank, psf_index)
+        spectrum, power, taps = psf_planes(plan, bank, psf_index)
         blocks = trade(blocks, slab_axes, slabs)
         if direct:
             own = sum(trade(numer, "epoch", ranks)[::-1])
@@ -751,18 +793,23 @@
             own = lax.psum(numer[0], "epoch")
             numer = [own]
         gain, cross = filter_gains(plan, flux_scale, noise_level, own, spectrum, power)
-        image = column_transform(plan, place, blocks)
+        image = None
+        if plan.pairs > 1:
+            image = column_transform(plan, list(range(1, plan.pairs)), blocks, None)
+        image = column_transform(plan, [0], blocks, image)
         returned = []
         for begin, end in parties:
-            rows_back = column_inverse(plan, place, image, gain, cross, numer, begin, end)
+            rows_back = column_inverse(plan, image, gain, cross, numer, begin, end)
             returned.append(trade(rows_back, slab_axes, slabs))
         chosen = column_choice(side, src_col.reshape(-1, group))
-        picked = [None]
-        for (begin, _), block in zip(parties, returned):
-            picked = row_fluxes(
-                plan, place, block, taps, begin, epochs, picked[0], src_row.reshape(-1, group), chosen
-            )
-        difference = row_images(plan, place, returned)
+        src_row = src_row.reshape(-1, group)
+        earlier = None
+        for (begin, end), block in zip(parties, returned):
+            flux, picked = row_fluxes(plan, block, taps, begin, epochs, src_row, chosen, earlier)
+            if end < epochs:
+                (earlier,) = picked
+        picked = [*own_fluxes(plan, flux, begin, src_row, chosen, earlier), *picked]
+        difference = row_images(plan, returned)
         return difference, sum(trade(picked, slab_axes, slabs)[::-1])
 
     return shards

time: 61 us -> 57.3 us (0.939)
  Pallas kernels: 29.6 us -> 25 us
  waiting for transfers between devices: 9.71 us -> 10.7 us
    pallas_call x13 -> x15, Pallas kernels: 29.6 us -> 25 us  [call(): pl.pallas_call(kernel, out_shape=tuple((jax.ShapeDtypeStruct(shape, (*kin...]
    ppermute x21, waiting for transfers between devices: 9.71 us -> 10.7 us  [trade(): result[m] = lax.ppermute(parts[m], axes, [(i, i ^ m) for i in range(count)])]
  transfers between devices with their start and end apart: 21 -> 21, of which waited for: 7 -> 8; matrix products, arithmetic and copies ran while one was open for 0% -> 0% of each run, Pallas kernels for 30% -> 29%
where the time goes in v3:
time: 57.3 us; the launch traced here: 57.1 us
  Pallas kernels  25 us (44%)
  starting transfers between devices  19.8 us (35%)
  waiting for transfers between devices  10.7 us (19%)
  between operations  0.92 us (2%)
  other arithmetic  0.64 us (1%)
    pallas_call x15, Pallas kernels, call(): pl.pallas_call(kernel, out_shape=tuple((jax.ShapeDtypeStruct(shape, (*kin...  25 us
    ppermute x21, starting transfers between devices, trade(): result[m] = lax.ppermute(parts[m], axes, [(i, i ^ m) for i in range(count)])  19.8 us
    ppermute x21, waiting for transfers between devices, trade(): result[m] = lax.ppermute(parts[m], axes, [(i, i ^ m) for i in range(count)])  10.7 us
  transfers between devices with their start and end apart: 21, of which 8 were waited for; matrix products, arithmetic and copies ran while one was open for 0% of the time, Pallas kernels for 29%

profile of v3, /device:TPU:0, one launch (start us, length us, event | category | flops | bytes accessed | tf_op | source)
XLA Modules:
  0.0 57.1 jit_solution(10311746616353579958)
XLA Ops:
  0.6 3.9 %shard_map.149 = (f32[144,128]{1,0:T(8,128)S(1)}, f32[144,128]{1,0:T(8,128)S(1)}, f32[1,128]{1,0:T(1,128)S(1)}, f32[2,4,64,128]{3,2,1,0:T(8,128)S(1)}, f32[4,128...) custom-call(s32[4]{0:T(128)} %index_ref.1, f32[4]{0:T(128)} %flux_ref.1, f32[4]{0:T(128)} %noise_ref.1, ...), custom_call_target="tpu_custom_call" | custom-call | bytes 16605000 | tf_op jit(solution)/shard_map/pallas_call | solution.py:112
  4.5 2.4 %collective-permute-start = (f32[144,128]{1,0:T(8,128)S(1)}, f32[144,128]{1,0:T(8,128)S(1)}, u32[]{:S(2)}, u32[]{:S(2)}) collective-permute-start(f32[144,128]{1,0:T(8,128)S(1)} %get-tuple-element.51), channel_id=1, source_target_pairs={{0,3},{1,2},{2,1},{3,0},{4,7},{5,6},{6,5},{7,4},{8,11},{9,10},{10,... | collective-permute-start | bytes 221192 | tf_op jit(solution)/shard_map/ppermute | solution.py:758
  7.0 0.6 %collective-permute-start.1 = (f32[144,128]{1,0:T(8,128)S(1)}, f32[144,128]{1,0:T(8,128)S(1)}, u32[]{:S(2)}, u32[]{:S(2)}) collective-permute-start(f32[144,128]{1,0:T(8,128)S(1)} %get-tuple-element.52), channel_id=1, source_target_pairs={{0,2},{1,3},{2,0},{3,1},{4,6},{5,7},{6,4},{7,5},{8,10},{9,11},{10,... | collective-permute-start | bytes 221192 | tf_op jit(solution)/shard_map/ppermute | solution.py:758
  7.6 2.4 %shard_map.150 = (f32[144,128]{1,0:T(8,128)S(1)}, f32[144,128]{1,0:T(8,128)S(1)}) custom-call(f32[2,4,64,128]{3,2,1,0:T(8,128)S(1)} %get-tuple-element.53.taps_ref, f32[4,128,512]{2,1,0:T(8,128)S(1)} %get-tuple-element.54.x_ref, bf16[2,4,128,256]{3,2,1,0:T(8,128)(2,1)S(1)} %get-tuple-element.55.table_ref), custom_call_target="tpu_custom_call" | custom-call | bytes 11808000 | tf_op jit(solution)/shard_map/pallas_call | solution.py:112
  10.0 0.0 copy-start
  10.0 0.0 copy-start.4
  10.0 0.0 copy-start.5
  10.1 0.0 copy-start.6
  10.1 0.1 collective-permute-start.2
  10.2 0.6 %shard_map.151 = (f32[128,512]{1,0:T(8,128)S(1)}, f32[128,512]{1,0:T(8,128)S(1)}, f32[128,512]{1,0:T(8,128)S(1)}, f32[128,512]{1,0:T(8,128)S(1)}) custom-call(f32[4,128,512]{2,1,0:T(8,128)S(1)} %get-tuple-element.54.x_ref, bf16[2,4,128,256]{3,2,1,0:T(8,128)(2,1)S(1)} %get-tuple-element.55.table_ref), custom_call_target="tpu_custom_call" | custom-call | bytes 4797000 | tf_op jit(solution)/shard_map/pallas_call | solution.py:112
  10.8 1.0 %collective-permute-done.1.rest_1_ = f32[144,128]{1,0:T(8,128)S(1)} collective-permute-done((f32[144,128]{1,0:T(8,128)S(1)}, f32[144,128]{1,0:T(8,128)S(1)}, u32[]{:S(2)}, u32[]{:S(2)}) %collective-permute-start.1) | collective-permute-done | bytes 73760 | tf_op jit(solution)/shard_map/ppermute | solution.py:758
  11.9 0.6 %shard_map.154 = (f32[136,128]{1,0:T(8,128)S(1)}, f32[136,128]{1,0:T(8,128)S(1)}, f32[136,128]{1,0:T(8,128)S(1)}, f32[136,128]{1,0:T(8,128)S(1)}) custom-call(f32[1,128]{1,0:T(1,128)S(1)} %get-tuple-element.66.shares_ref, f32[144,128]{1,0:T(8,128)S(1)} %collective-permute-done.rest_0_, f32[144,128]{1,0:T(8,128)S(1)} %collective-permute-done.1.rest_1_, ...), custom_call_target="tpu_custom_call" | custom-call | bytes 4243500 | tf_op jit(solution)/shard_map/pallas_call | solution.py:112
  12.5 4.0 %collective-permute-start.6 = (f32[136,128]{1,0:T(8,128)S(1)}, f32[136,128]{1,0:T(8,128)S(1)}, u32[]{:S(2)}, u32[]{:S(2)}) collective-permute-start(f32[136,128]{1,0:T(8,128)S(1)} %get-tuple-element.75), channel_id=1, source_target_pairs={{0,12},{4,8},{8,4},{12,0},{1,13},{5,9},{9,5},{13,1},{2,14},{6,10},... | collective-permute-start | bytes 208904 | tf_op jit(solution)/shard_map/ppermute | solution.py:758
  16.5 0.6 %collective-permute-start.8 = (f32[136,128]{1,0:T(8,128)S(1)}, f32[136,128]{1,0:T(8,128)S(1)}, u32[]{:S(2)}, u32[]{:S(2)}) collective-permute-start(f32[136,128]{1,0:T(8,128)S(1)} %get-tuple-element.77), channel_id=1, source_target_pairs={{0,4},{4,0},{8,12},{12,8},{1,5},{5,1},{9,13},{13,9},{2,6},{6,2},{1... | collective-permute-start | bytes 208904 | tf_op jit(solution)/shard_map/ppermute | solution.py:758
  17.1 0.6 %collective-permute-start.4 = (f32[128,512]{1,0:T(8,128)S(1)}, f32[128,512]{1,0:T(8,128)S(1)}, u32[]{:S(2)}, u32[]{:S(2)}) collective-permute-start(f32[128,512]{1,0:T(8,128)S(1)} %get-tuple-element.64), channel_id=1, source_target_pairs={{0,3},{1,2},{2,1},{3,0},{4,7},{5,6},{6,5},{7,4},{8,11},{9,10},{10,... | collective-permute-start | bytes 786440 | tf_op jit(solution)/shard_map/ppermute | solution.py:758
  17.8 1.0 %collective-permute-start.3 = (f32[128,512]{1,0:T(8,128)S(1)}, f32[128,512]{1,0:T(8,128)S(1)}, u32[]{:S(2)}, u32[]{:S(2)}) collective-permute-start(f32[128,512]{1,0:T(8,128)S(1)} %get-tuple-element.62), channel_id=1, source_target_pairs={{0,2},{1,3},{2,0},{3,1},{4,6},{5,7},{6,4},{7,5},{8,10},{9,11},{10,... | collective-permute-start | bytes 786440 | tf_op jit(solution)/shard_map/ppermute | solution.py:758
  18.8 2.4 %shard_map.155 = (f32[544,512]{1,0:T(8,128)S(1)}, f32[16,72,512]{2,1,0:T(8,128)S(1)}, f32[2,4,64,128]{3,2,1,0:T(8,128)S(1)}) custom-call(s32[4]{0:T(128)S(1)} %copy-done.9, f32[16,16,16]{2,1,0:T(8,128)S(1)} %copy-done.3, bf16[2,4,144,32]{3,2,1,0:T(8,128)(2,1)S(1)} %copy-done.4, bf16[128,512]{1,0:T(8,128)(2,1)S(1)} %copy-done.6, f32[16,1024]{1,0:T(8,128)S(1)} %copy-done.5), custom_call_target="tpu_custom_call" | custom-call | bytes 8671500 | tf_op jit(solution)/shard_map/pallas_call | solution.py:112
  21.2 0.3 collective-permute-start.5
  21.5 1.2 %collective-permute-done.7 = f32[136,128]{1,0:T(8,128)S(1)} collective-permute-done((f32[136,128]{1,0:T(8,128)S(1)}, f32[136,128]{1,0:T(8,128)S(1)}, u32[]{:S(2)}, u32[]{:S(2)}) %collective-permute-start.7) | collective-permute-done | bytes 69664 | tf_op jit(solution)/shard_map/ppermute | solution.py:758
  22.7 2.6 %collective-permute-start.11 = (f32[136,128]{1,0:T(8,128)S(1)}, f32[136,128]{1,0:T(8,128)S(1)}, u32[]{:S(2)}, u32[]{:S(2)}) collective-permute-start(f32[136,128]{1,0:T(8,128)S(1)} %add_add_fusion.share_ref.rest_0_), channel_id=1, source_target_pairs={{0,12},{4,8},{8,4},{12,0},{1,13},{5,9},{9,5},{13,1},{2,14},{6,10},... | collective-permute-start | bytes 208904 | tf_op jit(solution)/shard_map/ppermute | solution.py:758
  25.3 0.3 collective-permute-done.4.rest_0_
  25.6 1.6 %collective-permute-start.9 = (f32[136,128]{1,0:T(8,128)S(1)}, f32[136,128]{1,0:T(8,128)S(1)}, u32[]{:S(2)}, u32[]{:S(2)}) collective-permute-start(f32[136,128]{1,0:T(8,128)S(1)} %add_add_fusion.share_ref.rest_0_), channel_id=1, source_target_pairs={{0,4},{4,0},{8,12},{12,8},{1,5},{5,1},{9,13},{13,9},{2,6},{6,2},{1... | collective-permute-start | bytes 208904 | tf_op jit(solution)/shard_map/ppermute | solution.py:758
  27.1 1.1 %shard_map.156 = (f32[272,512]{1,0:T(8,128)S(1)}, f32[544,512]{1,0:T(8,128)S(1)}) custom-call(f32[4]{0:T(128)S(1)} %copy-done.7, f32[4]{0:T(128)S(1)} %copy-done.8, f32[136,128]{1,0:T(8,128)S(1)} %add_add_fusion.share_ref.rest_0_, f32[544,512]{1,0:T(8,128)S(1)} %get-tuple-element.82.spectrum_ref, f32[16,72,512]{2,1,0:T(8,128)S(1)} %get-tuple-element.83.power_ref), custom_call_target="tpu_custom_call" | custom-call | bytes 4243500 | tf_op jit(solution)/shard_map/pallas_call | solution.py:112
  28.2 0.8 %shard_map.152.rest_3_ = f32[544,512]{1,0:T(8,128)S(1)} custom-call(f32[128,512]{1,0:T(8,128)S(1)} %collective-permute-done.4.rest_0_, f32[128,512]{1,0:T(8,128)S(1)} %collective-permute-done.5.rest_1_, bf16[2,2,2,2,128,256]{5,4,3,2,1,0:T(8,128)(2,1)S(1)} %copy-done), custom_call_target="tpu_custom_call" | custom-call | bytes 3690000 | tf_op jit(solution)/shard_map/pallas_call | solution.py:112
  29.0 0.0 copy-start.2
  29.0 2.4 %collective-permute-done.3.rest_0_ = f32[128,512]{1,0:T(8,128)S(1)} collective-permute-done((f32[128,512]{1,0:T(8,128)S(1)}, f32[128,512]{1,0:T(8,128)S(1)}, u32[]{:S(2)}, u32[]{:S(2)}) %collective-permute-start.3) | collective-permute-done | bytes 262176 | tf_op jit(solution)/shard_map/ppermute | solution.py:758
  31.4 0.7 %shard_map.153.spectrum_ref = f32[544,512]{1,0:T(8,128)S(1)} custom-call(f32[128,512]{1,0:T(8,128)S(1)} %collective-permute-done.3.rest_0_, f32[128,512]{1,0:T(8,128)S(1)} %get-tuple-element.63.rest_1_, bf16[2,2,2,2,128,256]{5,4,3,2,1,0:T(8,128)(2,1)S(1)} %copy-done, f32[544,512]{1,0:T(8,128)S(1)} %shard_map.152.rest_3_), custom_call_target="tpu_custom_call" | custom-call | bytes 3690000 | tf_op jit(solution)/shard_map/pallas_call | solution.py:112
  32.2 0.8 %shard_map.157 = (f32[2,144,128]{2,1,0:T(8,128)S(1)}, f32[2,144,128]{2,1,0:T(8,128)S(1)}, f32[2,144,128]{2,1,0:T(8,128)S(1)}, f32[2,144,128]{2,1,0:T(8,128)S(1)}) custom-call(f32[544,512]{1,0:T(8,128)S(1)} %shard_map.153.spectrum_ref, f32[272,512]{1,0:T(8,128)S(1)} %get-tuple-element.84.gain_ref, f32[544,512]{1,0:T(8,128)S(1)} %get-tuple-element.85.cross_ref, ...), custom_call_target="tpu_custom_call" | custom-call | bytes 4981500 | tf_op jit(solution)/shard_map/pallas_call | solution.py:112
  33.0 0.1 collective-permute-start.12
  33.0 1.3 %collective-permute-start.13 = (f32[2,144,128]{2,1,0:T(8,128)S(1)}, f32[2,144,128]{2,1,0:T(8,128)S(1)}, u32[]{:S(2)}, u32[]{:S(2)}) collective-permute-start(f32[2,144,128]{2,1,0:T(8,128)S(1)} %get-tuple-element.88), channel_id=1, source_target_pairs={{0,2},{1,3},{2,0},{3,1},{4,6},{5,7},{6,4},{7,5},{8,10},{9,11},{10,... | collective-permute-start | bytes 442376 | tf_op jit(solution)/shard_map/ppermute | solution.py:758
  34.4 0.5 collective-permute-start.14
  34.9 0.8 %shard_map.158 = (f32[2,144,128]{2,1,0:T(8,128)S(1)}, f32[2,144,128]{2,1,0:T(8,128)S(1)}, f32[2,144,128]{2,1,0:T(8,128)S(1)}, f32[2,144,128]{2,1,0:T(8,128)S(1)}) custom-call(f32[544,512]{1,0:T(8,128)S(1)} %shard_map.153.spectrum_ref, f32[272,512]{1,0:T(8,128)S(1)} %get-tuple-element.84.gain_ref, f32[544,512]{1,0:T(8,128)S(1)} %get-tuple-element.85.cross_ref, ...), custom_call_target="tpu_custom_call" | custom-call | bytes 4981500 | tf_op jit(solution)/shard_map/pallas_call | solution.py:112
  35.7 0.4 collective-permute-start.15
  36.1 1.3 %collective-permute-start.16 = (f32[2,144,128]{2,1,0:T(8,128)S(1)}, f32[2,144,128]{2,1,0:T(8,128)S(1)}, u32[]{:S(2)}, u32[]{:S(2)}) collective-permute-start(f32[2,144,128]{2,1,0:T(8,128)S(1)} %get-tuple-element.92), channel_id=1, source_target_pairs={{0,2},{1,3},{2,0},{3,1},{4,6},{5,7},{6,4},{7,5},{8,10},{9,11},{10,... | collective-permute-start | bytes 442376 | tf_op jit(solution)/shard_map/ppermute | solution.py:758
  37.4 0.2 collective-permute-start.17
  37.7 0.0 copy-start.1
  37.7 1.0 %shard_map.160.chosen_ref = bf16[8,512,512]{2,1,0:T(8,128)(2,1)S(1)} custom-call(s32[8,512]{1,0:T(8,128)S(1)} %reshape.11.col_ref), custom_call_target="tpu_custom_call" | custom-call | bytes 7380000 | tf_op jit(solution)/shard_map/pallas_call | solution.py:112
  38.7 1.1 %collective-permute-done.13.rest_2_.rest_1_ = f32[2,144,128]{2,1,0:T(8,128)S(1)} collective-permute-done((f32[2,144,128]{2,1,0:T(8,128)S(1)}, f32[2,144,128]{2,1,0:T(8,128)S(1)}, u32[]{:S(2)}, u32[]{:S(2)}) %collective-permute-start.13) | collective-permute-done | bytes 147488 | tf_op jit(solution)/shard_map/ppermute | solution.py:758
  39.8 2.3 %collective-permute-done.14.rest_3_.rest_0_ = f32[2,144,128]{2,1,0:T(8,128)S(1)} collective-permute-done((f32[2,144,128]{2,1,0:T(8,128)S(1)}, f32[2,144,128]{2,1,0:T(8,128)S(1)}, u32[]{:S(2)}, u32[]{:S(2)}) %collective-permute-start.14) | collective-permute-done | bytes 147488 | tf_op jit(solution)/shard_map/ppermute | solution.py:758
  42.0 4.4 %shard_map.161 = (bf16[512,512]{1,0:T(8,128)(2,1)}, f32[4,2,1024]{2,1,0:T(2,128)S(1)}) custom-call(s32[8,512]{1,0:T(8,128)S(1)} %reshape.10.row_ref, bf16[8,512,512]{2,1,0:T(8,128)(2,1)S(1)} %shard_map.160.chosen_ref, f32[2,4,64,128]{3,2,1,0:T(8,128)S(1)} %get-tuple-element.94.taps_ref, f32[2,144,128]{2,1,0:T(8,128)S(1)} %collective-permute-done.14.rest_3_.rest_0_, ...), custom_call_target="tpu_custom_call" | custom-call | bytes 12915000 | tf_op jit(solution)/shard_map/pallas_call | solution.py:112
  46.4 1.9 %collective-permute-done.17.rest_7_.rest_0_ = f32[2,144,128]{2,1,0:T(8,128)S(1)} collective-permute-done((f32[2,144,128]{2,1,0:T(8,128)S(1)}, f32[2,144,128]{2,1,0:T(8,128)S(1)}, u32[]{:S(2)}, u32[]{:S(2)}) %collective-permute-start.17) | collective-permute-done | bytes 147488 | tf_op jit(solution)/shard_map/ppermute | solution.py:758
  48.3 3.3 %shard_map.162 = (bf16[512,512]{1,0:T(8,128)(2,1)S(1)}, f32[4,1024]{1,0:T(4,128)S(1)}, f32[4,1024]{1,0:T(4,128)S(1)}, f32[4,1024]{1,0:T(4,128)S(1)}) custom-call(s32[8,512]{1,0:T(8,128)S(1)} %reshape.10.row_ref, bf16[8,512,512]{2,1,0:T(8,128)(2,1)S(1)} %shard_map.160.chosen_ref, f32[2,4,64,128]{3,2,1,0:T(8,128)S(1)} %get-tuple-element.94.taps_ref, ...), custom_call_target="tpu_custom_call" | custom-call | bytes 12915000 | tf_op jit(solution)/shard_map/pallas_call | solution.py:112
  51.7 1.1 %collective-permute-start.18 = (f32[4,1024]{1,0:T(4,128)S(1)}, f32[4,1024]{1,0:T(4,128)S(1)}, u32[]{:S(2)}, u32[]{:S(2)}) collective-permute-start(f32[4,1024]{1,0:T(4,128)S(1)} %get-tuple-element.96), channel_id=1, source_target_pairs={{0,3},{1,2},{2,1},{3,0},{4,7},{5,6},{6,5},{7,4},{8,11},{9,10},{10,... | collective-permute-start | bytes 49160 | tf_op jit(solution)/shard_map/ppermute | solution.py:758
  52.8 0.8 %collective-permute-start.19 = (f32[4,1024]{1,0:T(4,128)S(1)}, f32[4,1024]{1,0:T(4,128)S(1)}, u32[]{:S(2)}, u32[]{:S(2)}) collective-permute-start(f32[4,1024]{1,0:T(4,128)S(1)} %get-tuple-element.97), channel_id=1, source_target_pairs={{0,2},{1,3},{2,0},{3,1},{4,6},{5,7},{6,4},{7,5},{8,10},{9,11},{10,... | collective-permute-start | bytes 49160 | tf_op jit(solution)/shard_map/ppermute | solution.py:758
  53.6 0.7 %shard_map.163 = f32[4,1024]{1,0:T(4,128)S(1)} custom-call(s32[8,512]{1,0:T(8,128)S(1)} %reshape.10.row_ref, bf16[8,512,512]{2,1,0:T(8,128)(2,1)S(1)} %shard_map.160.chosen_ref, bf16[512,512]{1,0:T(8,128)(2,1)S(1)} %get-tuple-element.99.flux_ref, f32[4,2,1024]{2,1,0:T(2,128)S(1)} %get-tuple-element.95.rest_5_.rest_0_), custom_call_target="tpu_custom_call" | custom-call | bytes 3321000 | tf_op jit(solution)/shard_map/pallas_call | solution.py:112
  54.4 1.5 %shard_map.159 = f32[4,128,512]{2,1,0:T(8,128)} custom-call(f32[2,144,128]{2,1,0:T(8,128)S(1)} %get-tuple-element.86.rest_0_.rest_3_, f32[2,144,128]{2,1,0:T(8,128)S(1)} %collective-permute-done.12.rest_1_.rest_2_, f32[2,144,128]{2,1,0:T(8,128)S(1)} %collective-permute-done.13.rest_2_.rest_1_, f32[2,144,128]{2,1,0:T(8,128)S(1)} %collective-permute-done.14.rest_3_.rest_0_, ...), custom_call_target="tpu_custom_call" | custom-call | bytes 8118000 | tf_op jit(solution)/shard_map/pallas_call | solution.py:112
  55.9 0.6 %collective-permute-done.19 = f32[4,1024]{1,0:T(4,128)S(1)} collective-permute-done((f32[4,1024]{1,0:T(4,128)S(1)}, f32[4,1024]{1,0:T(4,128)S(1)}, u32[]{:S(2)}, u32[]{:S(2)}) %collective-permute-start.19) | collective-permute-done | bytes 16416 | tf_op jit(solution)/shard_map/ppermute | solution.py:758
  56.5 0.6 %add_add_fusion.1 = f32[4,1024]{1,0:T(4,128)} fusion(f32[4,1024]{1,0:T(4,128)S(1)} %shard_map.163, f32[4,1024]{1,0:T(4,128)S(1)} %collective-permute-done.20, f32[4,1024]{1,0:T(4,128)S(1)} %collective-permute-done.18, f32[4,1024]{1,0:T(4,128)S(1)} %collective-permute-done.19), kind=kLoop, calls=%fused_computation.1 | loop fusion | flops 12288 | bytes 81920 | tf_op jit(solution)/shard_map/add | solution.py:813
  (37 shorter events, 0.1 us)
Async XLA Ops:
  4.5 6.3 %collective-permute-start = (f32[144,128]{1,0:T(8,128)S(1)}, f32[144,128]{1,0:T(8,128)S(1)}, u32[]{:S(2)}, u32[]{:S(2)}) collective-permute-start(f32[144,128]{1,0:T(8,128)S(1)} %get-tuple-element.51), channel_id=1, source_target_pairs={{0,3},{1,2},{2,1},{3,0},{4,7},{5,6},{6,5},{7,4},{8,11},{9,10},{10,... | collective-permute-start | bytes 221192 | tf_op jit(solution)/shard_map/ppermute | solution.py:758
  7.0 4.8 %collective-permute-start.1 = (f32[144,128]{1,0:T(8,128)S(1)}, f32[144,128]{1,0:T(8,128)S(1)}, u32[]{:S(2)}, u32[]{:S(2)}) collective-permute-start(f32[144,128]{1,0:T(8,128)S(1)} %get-tuple-element.52), channel_id=1, source_target_pairs={{0,2},{1,3},{2,0},{3,1},{4,6},{5,7},{6,4},{7,5},{8,10},{9,11},{10,... | collective-permute-start | bytes 221192 | tf_op jit(solution)/shard_map/ppermute | solution.py:758
  10.0 1.8 %copy-start = (bf16[2,2,2,2,128,256]{5,4,3,2,1,0:T(8,128)(2,1)S(1)}, bf16[2,2,2,2,128,256]{5,4,3,2,1,0:T(8,128)(2,1)}, u32[]{:S(2)}) copy-start(bf16[2,2,2,2,128,256]{5,4,3,2,1,0:T(8,128)(2,1)} %constant.16.clone.rest_2_.rest_4_) | copy-start | bytes 3145732
  10.0 8.8 %copy-start.3 = (f32[16,16,16]{2,1,0:T(8,128)S(1)}, f32[16,16,16]{2,1,0:T(8,128)}, u32[]{:S(2)}) copy-start(f32[16,16,16]{2,1,0:T(8,128)} %bank_ref) | copy-start | bytes 49156
  10.0 8.8 %copy-start.4 = (bf16[2,4,144,32]{3,2,1,0:T(8,128)(2,1)S(1)}, bf16[2,4,144,32]{3,2,1,0:T(8,128)(2,1)}, u32[]{:S(2)}) copy-start(bf16[2,4,144,32]{3,2,1,0:T(8,128)(2,1)} %constant.17.clone.shift_ref) | copy-start | bytes 221188
  10.0 8.8 %copy-start.5 = (f32[16,1024]{1,0:T(8,128)S(1)}, f32[16,1024]{1,0:T(8,128)}, u32[]{:S(2)}) copy-start(f32[16,1024]{1,0:T(8,128)} %constant.14.clone.rest_4_.coef_ref) | copy-start | bytes 196612
  10.1 8.8 %copy-start.6 = (bf16[128,512]{1,0:T(8,128)(2,1)S(1)}, bf16[128,512]{1,0:T(8,128)(2,1)}, u32[]{:S(2)}) copy-start(bf16[128,512]{1,0:T(8,128)(2,1)} %constant.18.clone.spread_ref) | copy-start | bytes 393220
  10.1 8.8 %copy-start.9 = (s32[4]{0:T(128)S(1)}, s32[4]{0:T(128)}, u32[]{:S(2)}) copy-start(s32[4]{0:T(128)} %index_ref.1) | copy-start | bytes 52
  10.1 1.8 %collective-permute-start.2 = (f32[144,128]{1,0:T(8,128)S(1)}, f32[144,128]{1,0:T(8,128)S(1)}, u32[]{:S(2)}, u32[]{:S(2)}) collective-permute-start(f32[144,128]{1,0:T(8,128)S(1)} %get-tuple-element.56), channel_id=1, source_target_pairs={{0,1},{1,0},{2,3},{3,2},{4,5},{5,4},{6,7},{7,6},{8,9},{9,8},{10,11... | collective-permute-start | bytes 221192 | tf_op jit(solution)/shard_map/ppermute | solution.py:758
  11.8 15.3 %copy-start.7 = (f32[4]{0:T(128)S(1)}, f32[4]{0:T(128)}, u32[]{:S(2)}) copy-start(f32[4]{0:T(128)} %flux_ref.1) | copy-start | bytes 52
  11.8 15.3 %copy-start.8 = (f32[4]{0:T(128)S(1)}, f32[4]{0:T(128)}, u32[]{:S(2)}) copy-start(f32[4]{0:T(128)} %noise_ref.1) | copy-start | bytes 52
  12.5 8.7 %collective-permute-start.6 = (f32[136,128]{1,0:T(8,128)S(1)}, f32[136,128]{1,0:T(8,128)S(1)}, u32[]{:S(2)}, u32[]{:S(2)}) collective-permute-start(f32[136,128]{1,0:T(8,128)S(1)} %get-tuple-element.75), channel_id=1, source_target_pairs={{0,12},{4,8},{8,4},{12,0},{1,13},{5,9},{9,5},{13,1},{2,14},{6,10},... | collective-permute-start | bytes 208904 | tf_op jit(solution)/shard_map/ppermute | solution.py:758
  16.5 6.1 %collective-permute-start.7 = (f32[136,128]{1,0:T(8,128)S(1)}, f32[136,128]{1,0:T(8,128)S(1)}, u32[]{:S(2)}, u32[]{:S(2)}) collective-permute-start(f32[136,128]{1,0:T(8,128)S(1)} %get-tuple-element.76), channel_id=1, source_target_pairs={{0,8},{4,12},{8,0},{12,4},{1,9},{5,13},{9,1},{13,5},{2,10},{6,14},... | collective-permute-start | bytes 208904 | tf_op jit(solution)/shard_map/ppermute | solution.py:758
  16.5 6.1 %collective-permute-start.8 = (f32[136,128]{1,0:T(8,128)S(1)}, f32[136,128]{1,0:T(8,128)S(1)}, u32[]{:S(2)}, u32[]{:S(2)}) collective-permute-start(f32[136,128]{1,0:T(8,128)S(1)} %get-tuple-element.77), channel_id=1, source_target_pairs={{0,4},{4,0},{8,12},{12,8},{1,5},{5,1},{9,13},{13,9},{2,6},{6,2},{1... | collective-permute-start | bytes 208904 | tf_op jit(solution)/shard_map/ppermute | solution.py:758
  17.1 8.4 %collective-permute-start.4 = (f32[128,512]{1,0:T(8,128)S(1)}, f32[128,512]{1,0:T(8,128)S(1)}, u32[]{:S(2)}, u32[]{:S(2)}) collective-permute-start(f32[128,512]{1,0:T(8,128)S(1)} %get-tuple-element.64), channel_id=1, source_target_pairs={{0,3},{1,2},{2,1},{3,0},{4,7},{5,6},{6,5},{7,4},{8,11},{9,10},{10,... | collective-permute-start | bytes 786440 | tf_op jit(solution)/shard_map/ppermute | solution.py:758
  17.8 13.6 %collective-permute-start.3 = (f32[128,512]{1,0:T(8,128)S(1)}, f32[128,512]{1,0:T(8,128)S(1)}, u32[]{:S(2)}, u32[]{:S(2)}) collective-permute-start(f32[128,512]{1,0:T(8,128)S(1)} %get-tuple-element.62), channel_id=1, source_target_pairs={{0,2},{1,3},{2,0},{3,1},{4,6},{5,7},{6,4},{7,5},{8,10},{9,11},{10,... | collective-permute-start | bytes 786440 | tf_op jit(solution)/shard_map/ppermute | solution.py:758
  21.2 7.0 %collective-permute-start.5 = (f32[128,512]{1,0:T(8,128)S(1)}, f32[128,512]{1,0:T(8,128)S(1)}, u32[]{:S(2)}, u32[]{:S(2)}) collective-permute-start(f32[128,512]{1,0:T(8,128)S(1)} %get-tuple-element.65), channel_id=1, source_target_pairs={{0,1},{1,0},{2,3},{3,2},{4,5},{5,4},{6,7},{7,6},{8,9},{9,8},{10,11... | collective-permute-start | bytes 786440 | tf_op jit(solution)/shard_map/ppermute | solution.py:758
  22.7 9.5 %collective-permute-start.11 = (f32[136,128]{1,0:T(8,128)S(1)}, f32[136,128]{1,0:T(8,128)S(1)}, u32[]{:S(2)}, u32[]{:S(2)}) collective-permute-start(f32[136,128]{1,0:T(8,128)S(1)} %add_add_fusion.share_ref.rest_0_), channel_id=1, source_target_pairs={{0,12},{4,8},{8,4},{12,0},{1,13},{5,9},{9,5},{13,1},{2,14},{6,10},... | collective-permute-start | bytes 208904 | tf_op jit(solution)/shard_map/ppermute | solution.py:758
  25.3 6.8 %collective-permute-start.10 = (f32[136,128]{1,0:T(8,128)S(1)}, f32[136,128]{1,0:T(8,128)S(1)}, u32[]{:S(2)}, u32[]{:S(2)}) collective-permute-start(f32[136,128]{1,0:T(8,128)S(1)} %add_add_fusion.share_ref.rest_0_), channel_id=1, source_target_pairs={{0,8},{4,12},{8,0},{12,4},{1,9},{5,13},{9,1},{13,5},{2,10},{6,14},... | collective-permute-start | bytes 208904 | tf_op jit(solution)/shard_map/ppermute | solution.py:758
  25.6 6.6 %collective-permute-start.9 = (f32[136,128]{1,0:T(8,128)S(1)}, f32[136,128]{1,0:T(8,128)S(1)}, u32[]{:S(2)}, u32[]{:S(2)}) collective-permute-start(f32[136,128]{1,0:T(8,128)S(1)} %add_add_fusion.share_ref.rest_0_), channel_id=1, source_target_pairs={{0,4},{4,0},{8,12},{12,8},{1,5},{5,1},{9,13},{13,9},{2,6},{6,2},{1... | collective-permute-start | bytes 208904 | tf_op jit(solution)/shard_map/ppermute | solution.py:758
  29.0 3.1 %copy-start.2 = (bf16[2,2,256,512]{3,2,1,0:T(8,128)(2,1)S(1)}, bf16[2,2,256,512]{3,2,1,0:T(8,128)(2,1)}, u32[]{:S(2)}) copy-start(bf16[2,2,256,512]{3,2,1,0:T(8,128)(2,1)} %constant.19.clone.rest_4_) | copy-start | bytes 3145732
  33.0 4.4 %collective-permute-start.12 = (f32[2,144,128]{2,1,0:T(8,128)S(1)}, f32[2,144,128]{2,1,0:T(8,128)S(1)}, u32[]{:S(2)}, u32[]{:S(2)}) collective-permute-start(f32[2,144,128]{2,1,0:T(8,128)S(1)} %get-tuple-element.87), channel_id=1, source_target_pairs={{0,1},{1,0},{2,3},{3,2},{4,5},{5,4},{6,7},{7,6},{8,9},{9,8},{10,11... | collective-permute-start | bytes 442376 | tf_op jit(solution)/shard_map/ppermute | solution.py:758
  33.0 6.7 %collective-permute-start.13 = (f32[2,144,128]{2,1,0:T(8,128)S(1)}, f32[2,144,128]{2,1,0:T(8,128)S(1)}, u32[]{:S(2)}, u32[]{:S(2)}) collective-permute-start(f32[2,144,128]{2,1,0:T(8,128)S(1)} %get-tuple-element.88), channel_id=1, source_target_pairs={{0,2},{1,3},{2,0},{3,1},{4,6},{5,7},{6,4},{7,5},{8,10},{9,11},{10,... | collective-permute-start | bytes 442376 | tf_op jit(solution)/shard_map/ppermute | solution.py:758
  34.4 3.3 %copy-start.10 = (s32[4096]{0:T(1024)S(1)}, s32[4096]{0:T(1024)}, u32[]{:S(2)}) copy-start(s32[4096]{0:T(1024)} %param.19) | copy-start | bytes 49156
  34.4 3.3 %copy-start.11 = (s32[4096]{0:T(1024)S(1)}, s32[4096]{0:T(1024)}, u32[]{:S(2)}) copy-start(s32[4096]{0:T(1024)} %param.20) | copy-start | bytes 49156
  34.4 7.6 %collective-permute-start.14 = (f32[2,144,128]{2,1,0:T(8,128)S(1)}, f32[2,144,128]{2,1,0:T(8,128)S(1)}, u32[]{:S(2)}, u32[]{:S(2)}) collective-permute-start(f32[2,144,128]{2,1,0:T(8,128)S(1)} %get-tuple-element.89), channel_id=1, source_target_pairs={{0,3},{1,2},{2,1},{3,0},{4,7},{5,6},{6,5},{7,4},{8,11},{9,10},{10,... | collective-permute-start | bytes 442376 | tf_op jit(solution)/shard_map/ppermute | solution.py:758
  35.7 10.7 %collective-permute-start.15 = (f32[2,144,128]{2,1,0:T(8,128)S(1)}, f32[2,144,128]{2,1,0:T(8,128)S(1)}, u32[]{:S(2)}, u32[]{:S(2)}) collective-permute-start(f32[2,144,128]{2,1,0:T(8,128)S(1)} %get-tuple-element.91), channel_id=1, source_target_pairs={{0,1},{1,0},{2,3},{3,2},{4,5},{5,4},{6,7},{7,6},{8,9},{9,8},{10,11... | collective-permute-start | bytes 442376 | tf_op jit(solution)/shard_map/ppermute | solution.py:758
  36.1 10.3 %collective-permute-start.16 = (f32[2,144,128]{2,1,0:T(8,128)S(1)}, f32[2,144,128]{2,1,0:T(8,128)S(1)}, u32[]{:S(2)}, u32[]{:S(2)}) collective-permute-start(f32[2,144,128]{2,1,0:T(8,128)S(1)} %get-tuple-element.92), channel_id=1, source_target_pairs={{0,2},{1,3},{2,0},{3,1},{4,6},{5,7},{6,4},{7,5},{8,10},{9,11},{10,... | collective-permute-start | bytes 442376 | tf_op jit(solution)/shard_map/ppermute | solution.py:758
  37.4 10.9 %collective-permute-start.17 = (f32[2,144,128]{2,1,0:T(8,128)S(1)}, f32[2,144,128]{2,1,0:T(8,128)S(1)}, u32[]{:S(2)}, u32[]{:S(2)}) collective-permute-start(f32[2,144,128]{2,1,0:T(8,128)S(1)} %get-tuple-element.93), channel_id=1, source_target_pairs={{0,3},{1,2},{2,1},{3,0},{4,7},{5,6},{6,5},{7,4},{8,11},{9,10},{10,... | collective-permute-start | bytes 442376 | tf_op jit(solution)/shard_map/ppermute | solution.py:758
  37.7 4.3 %copy-start.1 = (bf16[2,4,128,256]{3,2,1,0:T(8,128)(2,1)S(1)}, bf16[2,4,128,256]{3,2,1,0:T(8,128)(2,1)}, u32[]{:S(2)}) copy-start(bf16[2,4,128,256]{3,2,1,0:T(8,128)(2,1)} %constant.20.clone.rest_8_.rest_4_) | copy-start | bytes 1572868
  51.7 4.2 %collective-permute-start.18 = (f32[4,1024]{1,0:T(4,128)S(1)}, f32[4,1024]{1,0:T(4,128)S(1)}, u32[]{:S(2)}, u32[]{:S(2)}) collective-permute-start(f32[4,1024]{1,0:T(4,128)S(1)} %get-tuple-element.96), channel_id=1, source_target_pairs={{0,3},{1,2},{2,1},{3,0},{4,7},{5,6},{6,5},{7,4},{8,11},{9,10},{10,... | collective-permute-start | bytes 49160 | tf_op jit(solution)/shard_map/ppermute | solution.py:758
  52.8 3.7 %collective-permute-start.19 = (f32[4,1024]{1,0:T(4,128)S(1)}, f32[4,1024]{1,0:T(4,128)S(1)}, u32[]{:S(2)}, u32[]{:S(2)}) collective-permute-start(f32[4,1024]{1,0:T(4,128)S(1)} %get-tuple-element.97), channel_id=1, source_target_pairs={{0,2},{1,3},{2,0},{3,1},{4,6},{5,7},{6,4},{7,5},{8,10},{9,11},{10,... | collective-permute-start | bytes 49160 | tf_op jit(solution)/shard_map/ppermute | solution.py:758
  53.6 2.9 %collective-permute-start.20 = (f32[4,1024]{1,0:T(4,128)S(1)}, f32[4,1024]{1,0:T(4,128)S(1)}, u32[]{:S(2)}, u32[]{:S(2)}) collective-permute-start(f32[4,1024]{1,0:T(4,128)S(1)} %get-tuple-element.98), channel_id=1, source_target_pairs={{0,1},{1,0},{2,3},{3,2},{4,5},{5,4},{6,7},{7,6},{8,9},{9,8},{10,11... | collective-permute-start | bytes 49160 | tf_op jit(solution)/shard_map/ppermute | solution.py:758

commit v4 on v3

--- a/solution.py
+++ b/solution.py
@@ -158,10 +158,9 @@
     return data, table
 
 
-def coadd_rows(plan, q, group, x_ref, table_ref, taps_ref, padded, gathered, outs):
-    rows, lanes, tall, stamp, pairs = plan.rows, plan.lanes, plan.tall, plan.stamp, plan.pairs
+def lay_rows(plan, q, group, x_ref, table_ref, padded):
+    rows, lanes, stamp, pairs = plan.rows, plan.lanes, plan.stamp, plan.pairs
     epochs = x_ref.shape[0]
-    step = tall // 2
     padded[:, :, :stamp] = jnp.zeros((pairs, epochs, stamp, lanes), f32)
     padded[:, :, stamp + rows :] = jnp.zeros((pairs, epochs, stamp, lanes), f32)
     data, table = row_operands(plan, q, group, x_ref, table_ref)
@@ -172,41 +171,37 @@
                 e * rows : (e + 1) * rows, m * lanes : (m + 1) * lanes
             ]
 
-    @pl.loop(0, pairs)
-    def _(m):
-        d = q ^ (group * pairs + m)
-        for start in range(0, tall, step):
-            straight = jnp.zeros((step, lanes), f32)
-            crossed = jnp.zeros((step, lanes), f32)
-            for e in range(epochs):
-                for shift in range(8):
-                    shifted = padded[m, e, start + shift : start + shift + step + stamp - 8, :]
-                    for base in range(0, stamp, 8):
-                        value = shifted[base : base + step]
-                        at = e * stamp + base + shift
-                        straight += taps_ref[0, d, at : at + 1] * value
-                        crossed += taps_ref[1, d, at : at + 1] * value
-            gathered[m, start : start + step] = straight + swap_halves(plan, crossed)
-
-    for m in range(pairs):
-        outs[m][...] = gathered[m]
-
-
-def coadd_scratch(plan, epochs):
-    return [
-        pltpu.VMEM((plan.pairs, epochs, plan.rows + 2 * plan.stamp, plan.lanes), f32),
-        pltpu.VMEM((plan.pairs, plan.tall, plan.lanes), f32),
-    ]
+
+def coadd_rows(plan, q, mask, padded, taps_ref, out):
+    lanes, tall, stamp = plan.lanes, plan.tall, plan.stamp
+    step = tall // 2
+    d, m = q ^ mask, mask % plan.pairs
+    for start in range(0, tall, step):
+        straight = jnp.zeros((step, lanes), f32)
+        crossed = jnp.zeros((step, lanes), f32)
+        for e in range(padded.shape[1]):
+            for shift in range(8):
+                shifted = padded[m, e, start + shift : start + shift + step + stamp - 8, :]
+                for base in range(0, stamp, 8):
+                    value = shifted[base : base + step]
+                    at = e * stamp + base + shift
+                    straight += taps_ref[0, d, at : at + 1] * value
+                    crossed += taps_ref[1, d, at : at + 1] * value
+        out[start : start + step] = straight + swap_halves(plan, crossed)
+
+
+def padded_shape(plan, epochs):
+    return plan.pairs, epochs, plan.rows + 2 * plan.stamp, plan.lanes
 
 
 def row_transform_far(plan, index, flux, noise, images, bank, piece):
     epochs = images.shape[0]
-    slabs, pairs, lanes, tall, stamp = plan.slabs, plan.pairs, plan.lanes, plan.tall, plan.stamp
+    slabs, pairs, lanes, stamp = plan.slabs, plan.pairs, plan.lanes, plan.stamp
 
     def kernel(*rest):
         sources, outs, rest = rest[:7], rest[7 : 7 + pairs], rest[7 + pairs :]
         shares_ref, taps_ref, x_ref, table_ref, index_ref, flux_ref, noise_ref, bank_ref, coef_ref = rest[:9]
-        padded, gathered, sems = rest[9:]
+        padded, sems = rest[9:]
         targets = [index_ref, flux_ref, noise_ref, bank_ref, coef_ref, x_ref, table_ref]
         copies = [pltpu.make_async_copy(sources[i], targets[i], sems.at[i]) for i in range(7)]
         for copy in copies:
@@ -225,18 +220,20 @@
         shares_ref[...] = shares
         for copy in copies[5:]:
             copy.wait()
-        coadd_rows(plan, slab_of(), 1, x_ref, table_ref, taps_ref, padded, gathered, outs)
+        lay_rows(plan, slab_of(), 1, x_ref, table_ref, padded)
+        for m in range(pairs):
+            coadd_rows(plan, slab_of(), pairs + m, padded, taps_ref, outs[m])
 
     flat = call(
         kernel,
-        [("v", (tall, lanes))] * pairs
+        [("v", (plan.tall, lanes))] * pairs
         + [("v", (1, piece)), ("v", (2, slabs, epochs * stamp, lanes)), ("v", images.shape), ("v", plan.ahead.shape, bf16)],
         [("m", index), ("m", flux), ("m", noise), ("m", bank), ("m", plan.coef),
          ("m", images), ("m", plan.ahead)],
         [pltpu.SMEM(index.shape, jnp.int32), pltpu.SMEM(flux.shape, f32), pltpu.SMEM(noise.shape, f32),
          pltpu.VMEM(bank.shape, f32), pltpu.VMEM(plan.coef.shape, f32)]
-        + coadd_scratch(plan, epochs) + [pltpu.SemaphoreType.DMA((7,))],
-        micros=4.5,
+        + [pltpu.VMEM(padded_shape(plan, epochs), f32), pltpu.SemaphoreType.DMA((7,))],
+        micros=3.2,
     )
     return list(flat[:pairs]), *flat[pairs:]
 
@@ -244,15 +241,28 @@
 def row_transform_near(plan, taps, images, table):
     pairs = plan.pairs
 
-    def kernel(taps_ref, x_ref, table_ref, *rest):
-        coadd_rows(plan, slab_of(), 0, x_ref, table_ref, taps_ref, *rest[pairs:], rest[:pairs])
+    def kernel(taps_ref, x_ref, table_ref, out, padded):
+        lay_rows(plan, slab_of(), 0, x_ref, table_ref, padded)
+        coadd_rows(plan, slab_of(), pairs - 1, padded, taps_ref, out)
+
+    return call(
+        kernel,
+        [("v", (plan.tall, plan.lanes)), ("v", padded_shape(plan, images.shape[0]))],
+        [("v", taps), ("v", images), ("v", table)],
+        micros=1.6,
+    )
+
+
+def coadd_rest(plan, taps, padded, masks):
+    def kernel(taps_ref, padded_ref, *outs):
+        for mask, out in zip(masks, outs):
+            coadd_rows(plan, slab_of(), mask, padded_ref, taps_ref, out)
 
     return list(call(
         kernel,
-        [("v", (plan.tall, plan.lanes))] * pairs,
-        [("v", taps), ("v", images), ("v", table)],
-        coadd_scratch(plan, images.shape[0]),
-        micros=3.2,
+        [("v", (plan.tall, plan.lanes))] * len(masks),
+        [("v", taps), ("v", padded)],
+        micros=1.0 * len(masks),
     ))
 
 
@@ -278,7 +288,7 @@
     return [list(flat[i * slabs : (i + 1) * slabs]) for i in range(len(parties))]
 
 
-def numerator(plan, shares, blocks, pieces):
+def numerator(plan, shares, order, blocks, pieces):
     slabs, cols, rows, half, side, lanes, halo, tall = (
         plan.slabs, plan.cols, plan.rows, plan.half, plan.side, plan.lanes, plan.halo, plan.tall,
     )
@@ -290,9 +300,9 @@
         whole, parts = rest[slabs + 1 + pieces :]
         q, z = slab_of(), lax.axis_index("epoch") if pieces > 1 else 0
         whole[...] = jnp.zeros((side + 2 * halo, lanes), f32)
-        for m in range(slabs):
+        for m, block in zip(order, ins):
             at = pl.multiple_of((q ^ m) * rows, rows)
-            whole[pl.ds(at, tall)] += ins[slabs - 1 - m][...]
+            whole[pl.ds(at, tall)] += block[...]
         whole[side : side + halo] += whole[:halo]
         whole[halo : 2 * halo] += whole[side + halo :]
         top, bottom = whole[halo : halo + half], whole[halo + half : halo + side]
@@ -329,7 +339,7 @@
     return call(
         kernel,
         [("v", (lanes + 8, piece))] * pieces,
-        [("v", shares)] + [("v", b) for b in reversed(blocks)]
+        [("v", shares)] + [("v", b) for b in blocks]
         + [("v", plan.down)],
         [pltpu.VMEM((side + 2 * halo, lanes), f32), pltpu.VMEM((pieces, lanes + 8, piece), f32)],
         micros=1.15,
@@ -667,7 +677,7 @@
     return jnp.concatenate(parts, 1)
 
 
-def row_fluxes(plan, blocks, taps, begin, epochs, src_row, chosen, earlier):
+def row_fluxes(plan, order, blocks, taps, begin, epochs, src_row, chosen, earlier):
     slabs, pairs, rows, half, side, lanes, stamp = (
         plan.slabs, plan.pairs, plan.rows, plan.half, plan.side, plan.lanes, plan.stamp,
     )
@@ -679,7 +689,8 @@
     last = begin + mine == epochs
 
     def kernel(row_ref, chosen_ref, taps_ref, *rest):
-        ins, table_ref, rest = rest[:slabs][::-1], rest[slabs], rest[slabs + 1 :]
+        ins, table_ref, rest = rest[:slabs], rest[slabs], rest[slabs + 1 :]
+        ins = [ins[order.index(m)] for m in range(slabs)]
         if begin:
             earlier_ref, rest = rest[0], rest[1:]
         flux_ref, *outs, left_high, left_low = rest
@@ -719,7 +730,7 @@
     left = pltpu.VMEM((total, side), bf16)
     shape = (begin + mine, each * group)
     ins = [("v", src_row), ("v", chosen), ("v", taps)]
-    ins += [("v", b) for b in reversed(blocks)] + [("v", plan.back)]
+    ins += [("v", blocks[m]) for m in order] + [("v", plan.back)]
     if begin:
         ins.append(("v", earlier))
     flux, *picked = call(
@@ -777,11 +788,14 @@
         far, shares, weighted, images, table = row_transform_far(
             plan, *scalars, epoch_images, psf_bank, side // pieces
         )
-        near = row_transform_near(plan, weighted, images, table)
+        half = slabs // 2
+        near, near_rows = row_transform_near(plan, weighted, images, table)
+        near = coadd_rest(plan, weighted, near_rows, list(range(half - 1))) + [near]
         (blocks,) = row_transform(plan, images, table, [(0, epochs)])
         numer = trade(near + far, slab_axes, slabs)
-        numer, blocks = lax.optimization_barrier((numer[::-1], blocks))
-        numer = numerator(plan, shares, numer[::-1], pieces)
+        order = list(range(half, slabs)) + list(range(half))[::-1]
+        numer, blocks = lax.optimization_barrier(([numer[m] for m in order], blocks))
+        numer = numerator(plan, shares, order, numer, pieces)
         bank, numer = lax.optimization_barrier((psf_bank, numer))
         spectrum, power, taps = psf_planes(plan, bank, psf_index)
         blocks = trade(blocks, slab_axes, slabs)
@@ -795,8 +809,8 @@
         gain, cross = filter_gains(plan, flux_scale, noise_level, own, spectrum, power)
         image = None
         if plan.pairs > 1:
-            image = column_transform(plan, list(range(1, plan.pairs)), blocks, None)
-        image = column_transform(plan, [0], blocks, image)
+            image = column_transform(plan, [0], blocks, None)
+        image = column_transform(plan, list(range(1, plan.pairs)), blocks, image)
         returned = []
         for begin, end in parties:
             rows_back = column_inverse(plan, image, gain, cross, numer, begin, end)
@@ -805,7 +819,7 @@
         src_row = src_row.reshape(-1, group)
         earlier = None
         for (begin, end), block in zip(parties, returned):
-            flux, picked = row_fluxes(plan, block, taps, begin, epochs, src_row, chosen, earlier)
+            flux, picked = row_fluxes(plan, order, block, taps, begin, epochs, src_row, chosen, earlier)
             if end < epochs:
                 (earlier,) = picked
         picked = [*own_fluxes(plan, flux, begin, src_row, chosen, earlier), *picked]

time: 57.3 us -> 56.4 us (0.984)
  Pallas kernels: 25 us -> 24.1 us
    pallas_call x15 -> x16, Pallas kernels: 25 us -> 24.1 us  [call(): pl.pallas_call(kernel, out_shape=tuple((jax.ShapeDtypeStruct(shape, (*kin...]
  transfers between devices with their start and end apart: 21 -> 21, of which waited for: 8 -> 9; matrix products, arithmetic and copies ran while one was open for 0% -> 0% of each run, Pallas kernels for 29% -> 28%
where the time goes in v4:
time: 56.4 us; the launch traced here: 56.3 us
  Pallas kernels  24.1 us (43%)
  starting transfers between devices  20.1 us (36%)
  waiting for transfers between devices  10.5 us (19%)
  between operations  0.91 us (2%)
  other arithmetic  0.64 us (1%)
    pallas_call x16, Pallas kernels, call(): pl.pallas_call(kernel, out_shape=tuple((jax.ShapeDtypeStruct(shape, (*kin...  24.1 us
    ppermute x21, starting transfers between devices, trade(): result[m] = lax.ppermute(parts[m], axes, [(i, i ^ m) for i in range(count)])  20.1 us
    ppermute x21, waiting for transfers between devices, trade(): result[m] = lax.ppermute(parts[m], axes, [(i, i ^ m) for i in range(count)])  10.5 us
  transfers between devices with their start and end apart: 21, of which 9 were waited for; matrix products, arithmetic and copies ran while one was open for 0% of the time, Pallas kernels for 28%

profile of v4, /device:TPU:0, one launch (start us, length us, event | category | flops | bytes accessed | tf_op | source)
XLA Modules:
  0.0 56.3 jit_solution(2852339561892587210)
XLA Ops:
  0.6 3.4 %shard_map.149 = (f32[144,128]{1,0:T(8,128)S(1)}, f32[144,128]{1,0:T(8,128)S(1)}, f32[1,128]{1,0:T(1,128)S(1)}, f32[2,4,64,128]{3,2,1,0:T(8,128)S(1)}, f32[4,128...) custom-call(s32[4]{0:T(128)} %index_ref.1, f32[4]{0:T(128)} %flux_ref.1, f32[4]{0:T(128)} %noise_ref.1, ...), custom_call_target="tpu_custom_call" | custom-call | bytes 11808000 | tf_op jit(solution)/shard_map/pallas_call | solution.py:112
  4.1 3.0 %collective-permute-start = (f32[144,128]{1,0:T(8,128)S(1)}, f32[144,128]{1,0:T(8,128)S(1)}, u32[]{:S(2)}, u32[]{:S(2)}) collective-permute-start(f32[144,128]{1,0:T(8,128)S(1)} %get-tuple-element.51), channel_id=1, source_target_pairs={{0,2},{1,3},{2,0},{3,1},{4,6},{5,7},{6,4},{7,5},{8,10},{9,11},{10,... | collective-permute-start | bytes 221192 | tf_op jit(solution)/shard_map/ppermute | solution.py:769
  7.1 1.0 %shard_map.150 = (f32[144,128]{1,0:T(8,128)S(1)}, f32[2,4,160,128]{3,2,1,0:T(8,128)S(1)}) custom-call(f32[2,4,64,128]{3,2,1,0:T(8,128)S(1)} %get-tuple-element.53.taps_ref, f32[4,128,512]{2,1,0:T(8,128)S(1)} %get-tuple-element.54.x_ref, bf16[2,4,128,256]{3,2,1,0:T(8,128)(2,1)S(1)} %get-tuple-element.55.table_ref), custom_call_target="tpu_custom_call" | custom-call | bytes 5904000 | tf_op jit(solution)/shard_map/pallas_call | solution.py:112
  8.1 0.0 copy-start
  8.1 0.3 collective-permute-start.2
  8.4 0.6 %shard_map.152 = (f32[128,512]{1,0:T(8,128)S(1)}, f32[128,512]{1,0:T(8,128)S(1)}, f32[128,512]{1,0:T(8,128)S(1)}, f32[128,512]{1,0:T(8,128)S(1)}) custom-call(f32[4,128,512]{2,1,0:T(8,128)S(1)} %get-tuple-element.54.x_ref, bf16[2,4,128,256]{3,2,1,0:T(8,128)(2,1)S(1)} %get-tuple-element.55.table_ref), custom_call_target="tpu_custom_call" | custom-call | bytes 4797000 | tf_op jit(solution)/shard_map/pallas_call | solution.py:112
  9.0 0.0 copy-start.4
  9.0 0.0 copy-start.5
  9.0 0.0 copy-start.6
  9.1 1.0 %shard_map.151.rest_3_ = f32[144,128]{1,0:T(8,128)S(1)} custom-call(f32[2,4,64,128]{3,2,1,0:T(8,128)S(1)} %get-tuple-element.53.taps_ref, f32[2,4,160,128]{3,2,1,0:T(8,128)S(1)} %get-tuple-element.57.padded_ref), custom_call_target="tpu_custom_call" | custom-call | bytes 3690000 | tf_op jit(solution)/shard_map/pallas_call | solution.py:112
  10.0 1.3 %collective-permute-done.1.rest_1_ = f32[144,128]{1,0:T(8,128)S(1)} collective-permute-done((f32[144,128]{1,0:T(8,128)S(1)}, f32[144,128]{1,0:T(8,128)S(1)}, u32[]{:S(2)}, u32[]{:S(2)}) %collective-permute-start.1) | collective-permute-done | bytes 73760 | tf_op jit(solution)/shard_map/ppermute | solution.py:769
  11.4 0.6 %shard_map.155 = (f32[136,128]{1,0:T(8,128)S(1)}, f32[136,128]{1,0:T(8,128)S(1)}, f32[136,128]{1,0:T(8,128)S(1)}, f32[136,128]{1,0:T(8,128)S(1)}) custom-call(f32[1,128]{1,0:T(1,128)S(1)} %get-tuple-element.66.shares_ref, f32[144,128]{1,0:T(8,128)S(1)} %collective-permute-done.rest_0_, f32[144,128]{1,0:T(8,128)S(1)} %collective-permute-done.1.rest_1_, ...), custom_call_target="tpu_custom_call" | custom-call | bytes 4243500 | tf_op jit(solution)/shard_map/pallas_call | solution.py:112
  12.0 3.8 %collective-permute-start.6 = (f32[136,128]{1,0:T(8,128)S(1)}, f32[136,128]{1,0:T(8,128)S(1)}, u32[]{:S(2)}, u32[]{:S(2)}) collective-permute-start(f32[136,128]{1,0:T(8,128)S(1)} %get-tuple-element.75), channel_id=1, source_target_pairs={{0,12},{4,8},{8,4},{12,0},{1,13},{5,9},{9,5},{13,1},{2,14},{6,10},... | collective-permute-start | bytes 208904 | tf_op jit(solution)/shard_map/ppermute | solution.py:769
  15.8 0.6 %collective-permute-start.8 = (f32[136,128]{1,0:T(8,128)S(1)}, f32[136,128]{1,0:T(8,128)S(1)}, u32[]{:S(2)}, u32[]{:S(2)}) collective-permute-start(f32[136,128]{1,0:T(8,128)S(1)} %get-tuple-element.77), channel_id=1, source_target_pairs={{0,4},{4,0},{8,12},{12,8},{1,5},{5,1},{9,13},{13,9},{2,6},{6,2},{1... | collective-permute-start | bytes 208904 | tf_op jit(solution)/shard_map/ppermute | solution.py:769
  16.4 0.7 %collective-permute-start.5 = (f32[128,512]{1,0:T(8,128)S(1)}, f32[128,512]{1,0:T(8,128)S(1)}, u32[]{:S(2)}, u32[]{:S(2)}) collective-permute-start(f32[128,512]{1,0:T(8,128)S(1)} %get-tuple-element.64), channel_id=1, source_target_pairs={{0,2},{1,3},{2,0},{3,1},{4,6},{5,7},{6,4},{7,5},{8,10},{9,11},{10,... | collective-permute-start | bytes 786440 | tf_op jit(solution)/shard_map/ppermute | solution.py:769
  17.1 0.1 collective-permute-start.3
  17.3 2.3 %shard_map.156 = (f32[544,512]{1,0:T(8,128)S(1)}, f32[16,72,512]{2,1,0:T(8,128)S(1)}, f32[2,4,64,128]{3,2,1,0:T(8,128)S(1)}) custom-call(s32[4]{0:T(128)S(1)} %copy-done.9, f32[16,16,16]{2,1,0:T(8,128)S(1)} %copy-done.3, bf16[2,4,144,32]{3,2,1,0:T(8,128)(2,1)S(1)} %copy-done.4, bf16[128,512]{1,0:T(8,128)(2,1)S(1)} %copy-done.6, f32[16,1024]{1,0:T(8,128)S(1)} %copy-done.5), custom_call_target="tpu_custom_call" | custom-call | bytes 8671500 | tf_op jit(solution)/shard_map/pallas_call | solution.py:112
  19.6 1.4 %collective-permute-start.4 = (f32[128,512]{1,0:T(8,128)S(1)}, f32[128,512]{1,0:T(8,128)S(1)}, u32[]{:S(2)}, u32[]{:S(2)}) collective-permute-start(f32[128,512]{1,0:T(8,128)S(1)} %get-tuple-element.63), channel_id=1, source_target_pairs={{0,1},{1,0},{2,3},{3,2},{4,5},{5,4},{6,7},{7,6},{8,9},{9,8},{10,11... | collective-permute-start | bytes 786440 | tf_op jit(solution)/shard_map/ppermute | solution.py:769
  21.0 0.8 %collective-permute-done.7 = f32[136,128]{1,0:T(8,128)S(1)} collective-permute-done((f32[136,128]{1,0:T(8,128)S(1)}, f32[136,128]{1,0:T(8,128)S(1)}, u32[]{:S(2)}, u32[]{:S(2)}) %collective-permute-start.7) | collective-permute-done | bytes 69664 | tf_op jit(solution)/shard_map/ppermute | solution.py:769
  21.9 3.0 %collective-permute-start.11 = (f32[136,128]{1,0:T(8,128)S(1)}, f32[136,128]{1,0:T(8,128)S(1)}, u32[]{:S(2)}, u32[]{:S(2)}) collective-permute-start(f32[136,128]{1,0:T(8,128)S(1)} %add_add_fusion.share_ref.rest_0_), channel_id=1, source_target_pairs={{0,12},{4,8},{8,4},{12,0},{1,13},{5,9},{9,5},{13,1},{2,14},{6,10},... | collective-permute-start | bytes 208904 | tf_op jit(solution)/shard_map/ppermute | solution.py:769
  24.9 0.8 %collective-permute-done.5.rest_0_ = f32[128,512]{1,0:T(8,128)S(1)} collective-permute-done((f32[128,512]{1,0:T(8,128)S(1)}, f32[128,512]{1,0:T(8,128)S(1)}, u32[]{:S(2)}, u32[]{:S(2)}) %collective-permute-start.5) | collective-permute-done | bytes 262176 | tf_op jit(solution)/shard_map/ppermute | solution.py:769
  25.7 1.4 %collective-permute-start.9 = (f32[136,128]{1,0:T(8,128)S(1)}, f32[136,128]{1,0:T(8,128)S(1)}, u32[]{:S(2)}, u32[]{:S(2)}) collective-permute-start(f32[136,128]{1,0:T(8,128)S(1)} %add_add_fusion.share_ref.rest_0_), channel_id=1, source_target_pairs={{0,4},{4,0},{8,12},{12,8},{1,5},{5,1},{9,13},{13,9},{2,6},{6,2},{1... | collective-permute-start | bytes 208904 | tf_op jit(solution)/shard_map/ppermute | solution.py:769
  27.1 1.1 %shard_map.157 = (f32[272,512]{1,0:T(8,128)S(1)}, f32[544,512]{1,0:T(8,128)S(1)}) custom-call(f32[4]{0:T(128)S(1)} %copy-done.7, f32[4]{0:T(128)S(1)} %copy-done.8, f32[136,128]{1,0:T(8,128)S(1)} %add_add_fusion.share_ref.rest_0_, f32[544,512]{1,0:T(8,128)S(1)} %get-tuple-element.82.spectrum_ref, f32[16,72,512]{2,1,0:T(8,128)S(1)} %get-tuple-element.83.power_ref), custom_call_target="tpu_custom_call" | custom-call | bytes 4243500 | tf_op jit(solution)/shard_map/pallas_call | solution.py:112
  28.2 0.7 %shard_map.153.rest_3_ = f32[544,512]{1,0:T(8,128)S(1)} custom-call(f32[128,512]{1,0:T(8,128)S(1)} %collective-permute-done.5.rest_0_, f32[128,512]{1,0:T(8,128)S(1)} %get-tuple-element.65.rest_1_, bf16[2,2,2,2,128,256]{5,4,3,2,1,0:T(8,128)(2,1)S(1)} %copy-done), custom_call_target="tpu_custom_call" | custom-call | bytes 3690000 | tf_op jit(solution)/shard_map/pallas_call | solution.py:112
  28.9 0.0 copy-start.2
  29.0 0.7 %shard_map.154.spectrum_ref = f32[544,512]{1,0:T(8,128)S(1)} custom-call(f32[128,512]{1,0:T(8,128)S(1)} %collective-permute-done.3.rest_0_, f32[128,512]{1,0:T(8,128)S(1)} %collective-permute-done.4.rest_1_, bf16[2,2,2,2,128,256]{5,4,3,2,1,0:T(8,128)(2,1)S(1)} %copy-done, f32[544,512]{1,0:T(8,128)S(1)} %shard_map.153.rest_3_), custom_call_target="tpu_custom_call" | custom-call | bytes 3690000 | tf_op jit(solution)/shard_map/pallas_call | solution.py:112
  29.7 1.4 %collective-permute-done.10.rest_2_ = f32[136,128]{1,0:T(8,128)S(1)} collective-permute-done((f32[136,128]{1,0:T(8,128)S(1)}, f32[136,128]{1,0:T(8,128)S(1)}, u32[]{:S(2)}, u32[]{:S(2)}) %collective-permute-start.10) | collective-permute-done | bytes 69664 | tf_op jit(solution)/shard_map/ppermute | solution.py:769
  31.2 0.2 collective-permute-done.9.rest_1_
  31.3 0.8 %shard_map.158 = (f32[2,144,128]{2,1,0:T(8,128)S(1)}, f32[2,144,128]{2,1,0:T(8,128)S(1)}, f32[2,144,128]{2,1,0:T(8,128)S(1)}, f32[2,144,128]{2,1,0:T(8,128)S(1)}) custom-call(f32[544,512]{1,0:T(8,128)S(1)} %shard_map.154.spectrum_ref, f32[272,512]{1,0:T(8,128)S(1)} %get-tuple-element.84.gain_ref, f32[544,512]{1,0:T(8,128)S(1)} %get-tuple-element.85.cross_ref, ...), custom_call_target="tpu_custom_call" | custom-call | bytes 4981500 | tf_op jit(solution)/shard_map/pallas_call | solution.py:112
  32.1 0.1 collective-permute-start.12
  32.2 1.2 %collective-permute-start.13 = (f32[2,144,128]{2,1,0:T(8,128)S(1)}, f32[2,144,128]{2,1,0:T(8,128)S(1)}, u32[]{:S(2)}, u32[]{:S(2)}) collective-permute-start(f32[2,144,128]{2,1,0:T(8,128)S(1)} %get-tuple-element.88), channel_id=1, source_target_pairs={{0,2},{1,3},{2,0},{3,1},{4,6},{5,7},{6,4},{7,5},{8,10},{9,11},{10,... | collective-permute-start | bytes 442376 | tf_op jit(solution)/shard_map/ppermute | solution.py:769
  33.4 0.6 %collective-permute-start.14 = (f32[2,144,128]{2,1,0:T(8,128)S(1)}, f32[2,144,128]{2,1,0:T(8,128)S(1)}, u32[]{:S(2)}, u32[]{:S(2)}) collective-permute-start(f32[2,144,128]{2,1,0:T(8,128)S(1)} %get-tuple-element.89), channel_id=1, source_target_pairs={{0,3},{1,2},{2,1},{3,0},{4,7},{5,6},{6,5},{7,4},{8,11},{9,10},{10,... | collective-permute-start | bytes 442376 | tf_op jit(solution)/shard_map/ppermute | solution.py:769
  34.1 0.8 %shard_map.159 = (f32[2,144,128]{2,1,0:T(8,128)S(1)}, f32[2,144,128]{2,1,0:T(8,128)S(1)}, f32[2,144,128]{2,1,0:T(8,128)S(1)}, f32[2,144,128]{2,1,0:T(8,128)S(1)}) custom-call(f32[544,512]{1,0:T(8,128)S(1)} %shard_map.154.spectrum_ref, f32[272,512]{1,0:T(8,128)S(1)} %get-tuple-element.84.gain_ref, f32[544,512]{1,0:T(8,128)S(1)} %get-tuple-element.85.cross_ref, ...), custom_call_target="tpu_custom_call" | custom-call | bytes 4981500 | tf_op jit(solution)/shard_map/pallas_call | solution.py:112
  34.9 0.4 collective-permute-start.15
  35.3 1.2 %collective-permute-start.16 = (f32[2,144,128]{2,1,0:T(8,128)S(1)}, f32[2,144,128]{2,1,0:T(8,128)S(1)}, u32[]{:S(2)}, u32[]{:S(2)}) collective-permute-start(f32[2,144,128]{2,1,0:T(8,128)S(1)} %get-tuple-element.92), channel_id=1, source_target_pairs={{0,2},{1,3},{2,0},{3,1},{4,6},{5,7},{6,4},{7,5},{8,10},{9,11},{10,... | collective-permute-start | bytes 442376 | tf_op jit(solution)/shard_map/ppermute | solution.py:769
  36.5 0.3 collective-permute-start.17
  36.8 1.0 %shard_map.161.chosen_ref = bf16[8,512,512]{2,1,0:T(8,128)(2,1)S(1)} custom-call(s32[8,512]{1,0:T(8,128)S(1)} %reshape.11.col_ref), custom_call_target="tpu_custom_call" | custom-call | bytes 7380000 | tf_op jit(solution)/shard_map/pallas_call | solution.py:112
  37.8 1.1 %collective-permute-done.13.rest_2_.rest_0_ = f32[2,144,128]{2,1,0:T(8,128)S(1)} collective-permute-done((f32[2,144,128]{2,1,0:T(8,128)S(1)}, f32[2,144,128]{2,1,0:T(8,128)S(1)}, u32[]{:S(2)}, u32[]{:S(2)}) %collective-permute-start.13) | collective-permute-done | bytes 147488 | tf_op jit(solution)/shard_map/ppermute | solution.py:769
  38.9 2.3 %collective-permute-done.14.rest_3_.rest_1_ = f32[2,144,128]{2,1,0:T(8,128)S(1)} collective-permute-done((f32[2,144,128]{2,1,0:T(8,128)S(1)}, f32[2,144,128]{2,1,0:T(8,128)S(1)}, u32[]{:S(2)}, u32[]{:S(2)}) %collective-permute-start.14) | collective-permute-done | bytes 147488 | tf_op jit(solution)/shard_map/ppermute | solution.py:769
  41.2 4.4 %shard_map.162 = (bf16[512,512]{1,0:T(8,128)(2,1)}, f32[4,2,1024]{2,1,0:T(2,128)S(1)}) custom-call(s32[8,512]{1,0:T(8,128)S(1)} %reshape.10.row_ref, bf16[8,512,512]{2,1,0:T(8,128)(2,1)S(1)} %shard_map.161.chosen_ref, f32[2,4,64,128]{3,2,1,0:T(8,128)S(1)} %get-tuple-element.94.taps_ref, f32[2,144,128]{2,1,0:T(8,128)S(1)} %collective-permute-done.13.rest_2_.rest_0_, ...), custom_call_target="tpu_custom_call" | custom-call | bytes 12915000 | tf_op jit(solution)/shard_map/pallas_call | solution.py:112
  45.6 1.9 %collective-permute-done.17.rest_7_.rest_1_ = f32[2,144,128]{2,1,0:T(8,128)S(1)} collective-permute-done((f32[2,144,128]{2,1,0:T(8,128)S(1)}, f32[2,144,128]{2,1,0:T(8,128)S(1)}, u32[]{:S(2)}, u32[]{:S(2)}) %collective-permute-start.17) | collective-permute-done | bytes 147488 | tf_op jit(solution)/shard_map/ppermute | solution.py:769
  47.5 3.3 %shard_map.163 = (bf16[512,512]{1,0:T(8,128)(2,1)S(1)}, f32[4,1024]{1,0:T(4,128)S(1)}, f32[4,1024]{1,0:T(4,128)S(1)}, f32[4,1024]{1,0:T(4,128)S(1)}) custom-call(s32[8,512]{1,0:T(8,128)S(1)} %reshape.10.row_ref, bf16[8,512,512]{2,1,0:T(8,128)(2,1)S(1)} %shard_map.161.chosen_ref, f32[2,4,64,128]{3,2,1,0:T(8,128)S(1)} %get-tuple-element.94.taps_ref, ...), custom_call_target="tpu_custom_call" | custom-call | bytes 12915000 | tf_op jit(solution)/shard_map/pallas_call | solution.py:112
  50.8 1.1 %collective-permute-start.18 = (f32[4,1024]{1,0:T(4,128)S(1)}, f32[4,1024]{1,0:T(4,128)S(1)}, u32[]{:S(2)}, u32[]{:S(2)}) collective-permute-start(f32[4,1024]{1,0:T(4,128)S(1)} %get-tuple-element.96), channel_id=1, source_target_pairs={{0,3},{1,2},{2,1},{3,0},{4,7},{5,6},{6,5},{7,4},{8,11},{9,10},{10,... | collective-permute-start | bytes 49160 | tf_op jit(solution)/shard_map/ppermute | solution.py:769
  51.9 0.9 %collective-permute-start.19 = (f32[4,1024]{1,0:T(4,128)S(1)}, f32[4,1024]{1,0:T(4,128)S(1)}, u32[]{:S(2)}, u32[]{:S(2)}) collective-permute-start(f32[4,1024]{1,0:T(4,128)S(1)} %get-tuple-element.97), channel_id=1, source_target_pairs={{0,2},{1,3},{2,0},{3,1},{4,6},{5,7},{6,4},{7,5},{8,10},{9,11},{10,... | collective-permute-start | bytes 49160 | tf_op jit(solution)/shard_map/ppermute | solution.py:769
  52.8 0.7 %shard_map.164 = f32[4,1024]{1,0:T(4,128)S(1)} custom-call(s32[8,512]{1,0:T(8,128)S(1)} %reshape.10.row_ref, bf16[8,512,512]{2,1,0:T(8,128)(2,1)S(1)} %shard_map.161.chosen_ref, bf16[512,512]{1,0:T(8,128)(2,1)S(1)} %get-tuple-element.99.flux_ref, f32[4,2,1024]{2,1,0:T(2,128)S(1)} %get-tuple-element.95.rest_5_.rest_0_), custom_call_target="tpu_custom_call" | custom-call | bytes 3321000 | tf_op jit(solution)/shard_map/pallas_call | solution.py:112
  53.5 1.5 %shard_map.160 = f32[4,128,512]{2,1,0:T(8,128)} custom-call(f32[2,144,128]{2,1,0:T(8,128)S(1)} %get-tuple-element.86.rest_0_.rest_3_, f32[2,144,128]{2,1,0:T(8,128)S(1)} %collective-permute-done.12.rest_1_.rest_2_, f32[2,144,128]{2,1,0:T(8,128)S(1)} %collective-permute-done.13.rest_2_.rest_0_, f32[2,144,128]{2,1,0:T(8,128)S(1)} %collective-permute-done.14.rest_3_.rest_1_, ...), custom_call_target="tpu_custom_call" | custom-call | bytes 8118000 | tf_op jit(solution)/shard_map/pallas_call | solution.py:112
  55.1 0.6 %collective-permute-done.19 = f32[4,1024]{1,0:T(4,128)S(1)} collective-permute-done((f32[4,1024]{1,0:T(4,128)S(1)}, f32[4,1024]{1,0:T(4,128)S(1)}, u32[]{:S(2)}, u32[]{:S(2)}) %collective-permute-start.19) | collective-permute-done | bytes 16416 | tf_op jit(solution)/shard_map/ppermute | solution.py:769
  55.7 0.6 %add_add_fusion.1 = f32[4,1024]{1,0:T(4,128)} fusion(f32[4,1024]{1,0:T(4,128)S(1)} %shard_map.164, f32[4,1024]{1,0:T(4,128)S(1)} %collective-permute-done.20, f32[4,1024]{1,0:T(4,128)S(1)} %collective-permute-done.18, f32[4,1024]{1,0:T(4,128)S(1)} %collective-permute-done.19), kind=kLoop, calls=%fused_computation.1 | loop fusion | flops 12288 | bytes 81920 | tf_op jit(solution)/shard_map/add | solution.py:827
  (38 shorter events, 0.1 us)
Async XLA Ops:
  4.1 6.0 %collective-permute-start = (f32[144,128]{1,0:T(8,128)S(1)}, f32[144,128]{1,0:T(8,128)S(1)}, u32[]{:S(2)}, u32[]{:S(2)}) collective-permute-start(f32[144,128]{1,0:T(8,128)S(1)} %get-tuple-element.51), channel_id=1, source_target_pairs={{0,2},{1,3},{2,0},{3,1},{4,6},{5,7},{6,4},{7,5},{8,10},{9,11},{10,... | collective-permute-start | bytes 221192 | tf_op jit(solution)/shard_map/ppermute | solution.py:769
  7.1 4.3 %collective-permute-start.1 = (f32[144,128]{1,0:T(8,128)S(1)}, f32[144,128]{1,0:T(8,128)S(1)}, u32[]{:S(2)}, u32[]{:S(2)}) collective-permute-start(f32[144,128]{1,0:T(8,128)S(1)} %get-tuple-element.52), channel_id=1, source_target_pairs={{0,3},{1,2},{2,1},{3,0},{4,7},{5,6},{6,5},{7,4},{8,11},{9,10},{10,... | collective-permute-start | bytes 221192 | tf_op jit(solution)/shard_map/ppermute | solution.py:769
  8.1 3.3 %copy-start = (bf16[2,2,2,2,128,256]{5,4,3,2,1,0:T(8,128)(2,1)S(1)}, bf16[2,2,2,2,128,256]{5,4,3,2,1,0:T(8,128)(2,1)}, u32[]{:S(2)}) copy-start(bf16[2,2,2,2,128,256]{5,4,3,2,1,0:T(8,128)(2,1)} %constant.16.clone.rest_2_.rest_4_) | copy-start | bytes 3145732
  8.1 3.3 %collective-permute-start.2 = (f32[144,128]{1,0:T(8,128)S(1)}, f32[144,128]{1,0:T(8,128)S(1)}, u32[]{:S(2)}, u32[]{:S(2)}) collective-permute-start(f32[144,128]{1,0:T(8,128)S(1)} %get-tuple-element.56), channel_id=1, source_target_pairs={{0,1},{1,0},{2,3},{3,2},{4,5},{5,4},{6,7},{7,6},{8,9},{9,8},{10,11... | collective-permute-start | bytes 221192 | tf_op jit(solution)/shard_map/ppermute | solution.py:769
  9.0 8.2 %copy-start.3 = (f32[16,16,16]{2,1,0:T(8,128)S(1)}, f32[16,16,16]{2,1,0:T(8,128)}, u32[]{:S(2)}) copy-start(f32[16,16,16]{2,1,0:T(8,128)} %bank_ref) | copy-start | bytes 49156
  9.0 8.2 %copy-start.4 = (bf16[2,4,144,32]{3,2,1,0:T(8,128)(2,1)S(1)}, bf16[2,4,144,32]{3,2,1,0:T(8,128)(2,1)}, u32[]{:S(2)}) copy-start(bf16[2,4,144,32]{3,2,1,0:T(8,128)(2,1)} %constant.17.clone.shift_ref) | copy-start | bytes 221188
  9.0 8.2 %copy-start.5 = (f32[16,1024]{1,0:T(8,128)S(1)}, f32[16,1024]{1,0:T(8,128)}, u32[]{:S(2)}) copy-start(f32[16,1024]{1,0:T(8,128)} %constant.14.clone.rest_4_.coef_ref) | copy-start | bytes 196612
  9.0 8.2 %copy-start.6 = (bf16[128,512]{1,0:T(8,128)(2,1)S(1)}, bf16[128,512]{1,0:T(8,128)(2,1)}, u32[]{:S(2)}) copy-start(bf16[128,512]{1,0:T(8,128)(2,1)} %constant.18.clone.spread_ref) | copy-start | bytes 393220
  9.1 8.2 %copy-start.9 = (s32[4]{0:T(128)S(1)}, s32[4]{0:T(128)}, u32[]{:S(2)}) copy-start(s32[4]{0:T(128)} %index_ref.1) | copy-start | bytes 52
  11.4 15.7 %copy-start.7 = (f32[4]{0:T(128)S(1)}, f32[4]{0:T(128)}, u32[]{:S(2)}) copy-start(f32[4]{0:T(128)} %flux_ref.1) | copy-start | bytes 52
  11.4 15.7 %copy-start.8 = (f32[4]{0:T(128)S(1)}, f32[4]{0:T(128)}, u32[]{:S(2)}) copy-start(f32[4]{0:T(128)} %noise_ref.1) | copy-start | bytes 52
  12.0 7.6 %collective-permute-start.6 = (f32[136,128]{1,0:T(8,128)S(1)}, f32[136,128]{1,0:T(8,128)S(1)}, u32[]{:S(2)}, u32[]{:S(2)}) collective-permute-start(f32[136,128]{1,0:T(8,128)S(1)} %get-tuple-element.75), channel_id=1, source_target_pairs={{0,12},{4,8},{8,4},{12,0},{1,13},{5,9},{9,5},{13,1},{2,14},{6,10},... | collective-permute-start | bytes 208904 | tf_op jit(solution)/shard_map/ppermute | solution.py:769
  15.8 6.1 %collective-permute-start.7 = (f32[136,128]{1,0:T(8,128)S(1)}, f32[136,128]{1,0:T(8,128)S(1)}, u32[]{:S(2)}, u32[]{:S(2)}) collective-permute-start(f32[136,128]{1,0:T(8,128)S(1)} %get-tuple-element.76), channel_id=1, source_target_pairs={{0,8},{4,12},{8,0},{12,4},{1,9},{5,13},{9,1},{13,5},{2,10},{6,14},... | collective-permute-start | bytes 208904 | tf_op jit(solution)/shard_map/ppermute | solution.py:769
  15.8 6.1 %collective-permute-start.8 = (f32[136,128]{1,0:T(8,128)S(1)}, f32[136,128]{1,0:T(8,128)S(1)}, u32[]{:S(2)}, u32[]{:S(2)}) collective-permute-start(f32[136,128]{1,0:T(8,128)S(1)} %get-tuple-element.77), channel_id=1, source_target_pairs={{0,4},{4,0},{8,12},{12,8},{1,5},{5,1},{9,13},{13,9},{2,6},{6,2},{1... | collective-permute-start | bytes 208904 | tf_op jit(solution)/shard_map/ppermute | solution.py:769
  16.4 9.2 %collective-permute-start.5 = (f32[128,512]{1,0:T(8,128)S(1)}, f32[128,512]{1,0:T(8,128)S(1)}, u32[]{:S(2)}, u32[]{:S(2)}) collective-permute-start(f32[128,512]{1,0:T(8,128)S(1)} %get-tuple-element.64), channel_id=1, source_target_pairs={{0,2},{1,3},{2,0},{3,1},{4,6},{5,7},{6,4},{7,5},{8,10},{9,11},{10,... | collective-permute-start | bytes 786440 | tf_op jit(solution)/shard_map/ppermute | solution.py:769
  17.1 11.8 %collective-permute-start.3 = (f32[128,512]{1,0:T(8,128)S(1)}, f32[128,512]{1,0:T(8,128)S(1)}, u32[]{:S(2)}, u32[]{:S(2)}) collective-permute-start(f32[128,512]{1,0:T(8,128)S(1)} %get-tuple-element.62), channel_id=1, source_target_pairs={{0,3},{1,2},{2,1},{3,0},{4,7},{5,6},{6,5},{7,4},{8,11},{9,10},{10,... | collective-permute-start | bytes 786440 | tf_op jit(solution)/shard_map/ppermute | solution.py:769
  19.6 9.3 %collective-permute-start.4 = (f32[128,512]{1,0:T(8,128)S(1)}, f32[128,512]{1,0:T(8,128)S(1)}, u32[]{:S(2)}, u32[]{:S(2)}) collective-permute-start(f32[128,512]{1,0:T(8,128)S(1)} %get-tuple-element.63), channel_id=1, source_target_pairs={{0,1},{1,0},{2,3},{3,2},{4,5},{5,4},{6,7},{7,6},{8,9},{9,8},{10,11... | collective-permute-start | bytes 786440 | tf_op jit(solution)/shard_map/ppermute | solution.py:769
  21.9 7.8 %collective-permute-start.11 = (f32[136,128]{1,0:T(8,128)S(1)}, f32[136,128]{1,0:T(8,128)S(1)}, u32[]{:S(2)}, u32[]{:S(2)}) collective-permute-start(f32[136,128]{1,0:T(8,128)S(1)} %add_add_fusion.share_ref.rest_0_), channel_id=1, source_target_pairs={{0,12},{4,8},{8,4},{12,0},{1,13},{5,9},{9,5},{13,1},{2,14},{6,10},... | collective-permute-start | bytes 208904 | tf_op jit(solution)/shard_map/ppermute | solution.py:769
  24.9 6.3 %collective-permute-start.10 = (f32[136,128]{1,0:T(8,128)S(1)}, f32[136,128]{1,0:T(8,128)S(1)}, u32[]{:S(2)}, u32[]{:S(2)}) collective-permute-start(f32[136,128]{1,0:T(8,128)S(1)} %add_add_fusion.share_ref.rest_0_), channel_id=1, source_target_pairs={{0,8},{4,12},{8,0},{12,4},{1,9},{5,13},{9,1},{13,5},{2,10},{6,14},... | collective-permute-start | bytes 208904 | tf_op jit(solution)/shard_map/ppermute | solution.py:769
  25.7 5.6 %collective-permute-start.9 = (f32[136,128]{1,0:T(8,128)S(1)}, f32[136,128]{1,0:T(8,128)S(1)}, u32[]{:S(2)}, u32[]{:S(2)}) collective-permute-start(f32[136,128]{1,0:T(8,128)S(1)} %add_add_fusion.share_ref.rest_0_), channel_id=1, source_target_pairs={{0,4},{4,0},{8,12},{12,8},{1,5},{5,1},{9,13},{13,9},{2,6},{6,2},{1... | collective-permute-start | bytes 208904 | tf_op jit(solution)/shard_map/ppermute | solution.py:769
  28.9 2.4 %copy-start.2 = (bf16[2,2,256,512]{3,2,1,0:T(8,128)(2,1)S(1)}, bf16[2,2,256,512]{3,2,1,0:T(8,128)(2,1)}, u32[]{:S(2)}) copy-start(bf16[2,2,256,512]{3,2,1,0:T(8,128)(2,1)} %constant.19.clone.rest_4_) | copy-start | bytes 3145732
  32.1 4.3 %collective-permute-start.12 = (f32[2,144,128]{2,1,0:T(8,128)S(1)}, f32[2,144,128]{2,1,0:T(8,128)S(1)}, u32[]{:S(2)}, u32[]{:S(2)}) collective-permute-start(f32[2,144,128]{2,1,0:T(8,128)S(1)} %get-tuple-element.87), channel_id=1, source_target_pairs={{0,1},{1,0},{2,3},{3,2},{4,5},{5,4},{6,7},{7,6},{8,9},{9,8},{10,11... | collective-permute-start | bytes 442376 | tf_op jit(solution)/shard_map/ppermute | solution.py:769
  32.2 6.7 %collective-permute-start.13 = (f32[2,144,128]{2,1,0:T(8,128)S(1)}, f32[2,144,128]{2,1,0:T(8,128)S(1)}, u32[]{:S(2)}, u32[]{:S(2)}) collective-permute-start(f32[2,144,128]{2,1,0:T(8,128)S(1)} %get-tuple-element.88), channel_id=1, source_target_pairs={{0,2},{1,3},{2,0},{3,1},{4,6},{5,7},{6,4},{7,5},{8,10},{9,11},{10,... | collective-permute-start | bytes 442376 | tf_op jit(solution)/shard_map/ppermute | solution.py:769
  33.4 3.4 %copy-start.10 = (s32[4096]{0:T(1024)S(1)}, s32[4096]{0:T(1024)}, u32[]{:S(2)}) copy-start(s32[4096]{0:T(1024)} %param.19) | copy-start | bytes 49156
  33.4 3.4 %copy-start.11 = (s32[4096]{0:T(1024)S(1)}, s32[4096]{0:T(1024)}, u32[]{:S(2)}) copy-start(s32[4096]{0:T(1024)} %param.20) | copy-start | bytes 49156
  33.4 7.7 %collective-permute-start.14 = (f32[2,144,128]{2,1,0:T(8,128)S(1)}, f32[2,144,128]{2,1,0:T(8,128)S(1)}, u32[]{:S(2)}, u32[]{:S(2)}) collective-permute-start(f32[2,144,128]{2,1,0:T(8,128)S(1)} %get-tuple-element.89), channel_id=1, source_target_pairs={{0,3},{1,2},{2,1},{3,0},{4,7},{5,6},{6,5},{7,4},{8,11},{9,10},{10,... | collective-permute-start | bytes 442376 | tf_op jit(solution)/shard_map/ppermute | solution.py:769
  34.9 10.7 %collective-permute-start.15 = (f32[2,144,128]{2,1,0:T(8,128)S(1)}, f32[2,144,128]{2,1,0:T(8,128)S(1)}, u32[]{:S(2)}, u32[]{:S(2)}) collective-permute-start(f32[2,144,128]{2,1,0:T(8,128)S(1)} %get-tuple-element.91), channel_id=1, source_target_pairs={{0,1},{1,0},{2,3},{3,2},{4,5},{5,4},{6,7},{7,6},{8,9},{9,8},{10,11... | collective-permute-start | bytes 442376 | tf_op jit(solution)/shard_map/ppermute | solution.py:769
  35.3 10.3 %collective-permute-start.16 = (f32[2,144,128]{2,1,0:T(8,128)S(1)}, f32[2,144,128]{2,1,0:T(8,128)S(1)}, u32[]{:S(2)}, u32[]{:S(2)}) collective-permute-start(f32[2,144,128]{2,1,0:T(8,128)S(1)} %get-tuple-element.92), channel_id=1, source_target_pairs={{0,2},{1,3},{2,0},{3,1},{4,6},{5,7},{6,4},{7,5},{8,10},{9,11},{10,... | collective-permute-start | bytes 442376 | tf_op jit(solution)/shard_map/ppermute | solution.py:769
  36.5 11.0 %collective-permute-start.17 = (f32[2,144,128]{2,1,0:T(8,128)S(1)}, f32[2,144,128]{2,1,0:T(8,128)S(1)}, u32[]{:S(2)}, u32[]{:S(2)}) collective-permute-start(f32[2,144,128]{2,1,0:T(8,128)S(1)} %get-tuple-element.93), channel_id=1, source_target_pairs={{0,3},{1,2},{2,1},{3,0},{4,7},{5,6},{6,5},{7,4},{8,11},{9,10},{10,... | collective-permute-start | bytes 442376 | tf_op jit(solution)/shard_map/ppermute | solution.py:769
  36.8 4.3 %copy-start.1 = (bf16[2,4,128,256]{3,2,1,0:T(8,128)(2,1)S(1)}, bf16[2,4,128,256]{3,2,1,0:T(8,128)(2,1)}, u32[]{:S(2)}) copy-start(bf16[2,4,128,256]{3,2,1,0:T(8,128)(2,1)} %constant.20.clone.rest_8_.rest_4_) | copy-start | bytes 1572868
  50.8 4.2 %collective-permute-start.18 = (f32[4,1024]{1,0:T(4,128)S(1)}, f32[4,1024]{1,0:T(4,128)S(1)}, u32[]{:S(2)}, u32[]{:S(2)}) collective-permute-start(f32[4,1024]{1,0:T(4,128)S(1)} %get-tuple-element.96), channel_id=1, source_target_pairs={{0,3},{1,2},{2,1},{3,0},{4,7},{5,6},{6,5},{7,4},{8,11},{9,10},{10,... | collective-permute-start | bytes 49160 | tf_op jit(solution)/shard_map/ppermute | solution.py:769
  51.9 3.7 %collective-permute-start.19 = (f32[4,1024]{1,0:T(4,128)S(1)}, f32[4,1024]{1,0:T(4,128)S(1)}, u32[]{:S(2)}, u32[]{:S(2)}) collective-permute-start(f32[4,1024]{1,0:T(4,128)S(1)} %get-tuple-element.97), channel_id=1, source_target_pairs={{0,2},{1,3},{2,0},{3,1},{4,6},{5,7},{6,4},{7,5},{8,10},{9,11},{10,... | collective-permute-start | bytes 49160 | tf_op jit(solution)/shard_map/ppermute | solution.py:769
  52.8 2.9 %collective-permute-start.20 = (f32[4,1024]{1,0:T(4,128)S(1)}, f32[4,1024]{1,0:T(4,128)S(1)}, u32[]{:S(2)}, u32[]{:S(2)}) collective-permute-start(f32[4,1024]{1,0:T(4,128)S(1)} %get-tuple-element.98), channel_id=1, source_target_pairs={{0,1},{1,0},{2,3},{3,2},{4,5},{5,4},{6,7},{7,6},{8,9},{9,8},{10,11... | collective-permute-start | bytes 49160 | tf_op jit(solution)/shard_map/ppermute | solution.py:769

commit v5 on v4

--- a/solution.py
+++ b/solution.py
@@ -800,7 +800,8 @@
         spectrum, power, taps = psf_planes(plan, bank, psf_index)
         blocks = trade(blocks, slab_axes, slabs)
         if direct:
-            own = sum(trade(numer, "epoch", ranks)[::-1])
+            own = trade(numer, "epoch", ranks)
+            own = sum(own[m] for m in [3, 1, 2, 0])
             own, spectrum = lax.optimization_barrier((own, spectrum))
             numer = trade([own] * ranks, "epoch", ranks)
         else:

time: 56.4 us -> 56 us (level)
  waiting for transfers between devices: 10.5 us -> 9.77 us
    ppermute x21, waiting for transfers between devices: 10.5 us -> 9.77 us  [trade(): result[m] = lax.ppermute(parts[m], axes, [(i, i ^ m) for i in range(count)])]
  transfers between devices with their start and end apart: 21 -> 21, of which waited for: 9 -> 9; matrix products, arithmetic and copies ran while one was open for 0% -> 0% of each run, Pallas kernels for 28% -> 29%
where the time goes in v5:
time: 56 us; the launch traced here: 55.8 us
  Pallas kernels  24.1 us (43%)
  starting transfers between devices  20.3 us (36%)
  waiting for transfers between devices  9.77 us (17%)
  between operations  0.91 us (2%)
  other arithmetic  0.64 us (1%)
    pallas_call x16, Pallas kernels, call(): pl.pallas_call(kernel, out_shape=tuple((jax.ShapeDtypeStruct(shape, (*kin...  24.1 us
    ppermute x21, starting transfers between devices, trade(): result[m] = lax.ppermute(parts[m], axes, [(i, i ^ m) for i in range(count)])  20.3 us
    ppermute x21, waiting for transfers between devices, trade(): result[m] = lax.ppermute(parts[m], axes, [(i, i ^ m) for i in range(count)])  9.77 us
  transfers between devices with their start and end apart: 21, of which 9 were waited for; matrix products, arithmetic and copies ran while one was open for 0% of the time, Pallas kernels for 29%

profile of v5, /device:TPU:0, one launch (start us, length us, event | category | flops | bytes accessed | tf_op | source)
XLA Modules:
  0.0 55.8 jit_solution(8507493839685586430)
XLA Ops:
  0.6 3.4 %shard_map.149 = (f32[144,128]{1,0:T(8,128)S(1)}, f32[144,128]{1,0:T(8,128)S(1)}, f32[1,128]{1,0:T(1,128)S(1)}, f32[2,4,64,128]{3,2,1,0:T(8,128)S(1)}, f32[4,128...) custom-call(s32[4]{0:T(128)} %index_ref.1, f32[4]{0:T(128)} %flux_ref.1, f32[4]{0:T(128)} %noise_ref.1, ...), custom_call_target="tpu_custom_call" | custom-call | bytes 11808000 | tf_op jit(solution)/shard_map/pallas_call | solution.py:112
  4.1 3.0 %collective-permute-start = (f32[144,128]{1,0:T(8,128)S(1)}, f32[144,128]{1,0:T(8,128)S(1)}, u32[]{:S(2)}, u32[]{:S(2)}) collective-permute-start(f32[144,128]{1,0:T(8,128)S(1)} %get-tuple-element.51), channel_id=1, source_target_pairs={{0,2},{1,3},{2,0},{3,1},{4,6},{5,7},{6,4},{7,5},{8,10},{9,11},{10,... | collective-permute-start | bytes 221192 | tf_op jit(solution)/shard_map/ppermute | solution.py:769
  7.1 1.0 %shard_map.150 = (f32[144,128]{1,0:T(8,128)S(1)}, f32[2,4,160,128]{3,2,1,0:T(8,128)S(1)}) custom-call(f32[2,4,64,128]{3,2,1,0:T(8,128)S(1)} %get-tuple-element.53.taps_ref, f32[4,128,512]{2,1,0:T(8,128)S(1)} %get-tuple-element.54.x_ref, bf16[2,4,128,256]{3,2,1,0:T(8,128)(2,1)S(1)} %get-tuple-element.55.table_ref), custom_call_target="tpu_custom_call" | custom-call | bytes 5904000 | tf_op jit(solution)/shard_map/pallas_call | solution.py:112
  8.1 0.3 collective-permute-start.2
  8.4 0.6 %shard_map.152 = (f32[128,512]{1,0:T(8,128)S(1)}, f32[128,512]{1,0:T(8,128)S(1)}, f32[128,512]{1,0:T(8,128)S(1)}, f32[128,512]{1,0:T(8,128)S(1)}) custom-call(f32[4,128,512]{2,1,0:T(8,128)S(1)} %get-tuple-element.54.x_ref, bf16[2,4,128,256]{3,2,1,0:T(8,128)(2,1)S(1)} %get-tuple-element.55.table_ref), custom_call_target="tpu_custom_call" | custom-call | bytes 4797000 | tf_op jit(solution)/shard_map/pallas_call | solution.py:112
  9.0 0.0 copy-start.4
  9.0 0.0 copy-start.5
  9.0 0.0 copy-start.6
  9.1 1.0 %shard_map.151.rest_3_ = f32[144,128]{1,0:T(8,128)S(1)} custom-call(f32[2,4,64,128]{3,2,1,0:T(8,128)S(1)} %get-tuple-element.53.taps_ref, f32[2,4,160,128]{3,2,1,0:T(8,128)S(1)} %get-tuple-element.57.padded_ref), custom_call_target="tpu_custom_call" | custom-call | bytes 3690000 | tf_op jit(solution)/shard_map/pallas_call | solution.py:112
  10.0 1.3 %collective-permute-done.1.rest_1_ = f32[144,128]{1,0:T(8,128)S(1)} collective-permute-done((f32[144,128]{1,0:T(8,128)S(1)}, f32[144,128]{1,0:T(8,128)S(1)}, u32[]{:S(2)}, u32[]{:S(2)}) %collective-permute-start.1) | collective-permute-done | bytes 73760 | tf_op jit(solution)/shard_map/ppermute | solution.py:769
  11.4 0.6 %shard_map.155 = (f32[136,128]{1,0:T(8,128)S(1)}, f32[136,128]{1,0:T(8,128)S(1)}, f32[136,128]{1,0:T(8,128)S(1)}, f32[136,128]{1,0:T(8,128)S(1)}) custom-call(f32[1,128]{1,0:T(1,128)S(1)} %get-tuple-element.66.shares_ref, f32[144,128]{1,0:T(8,128)S(1)} %collective-permute-done.rest_0_, f32[144,128]{1,0:T(8,128)S(1)} %collective-permute-done.1.rest_1_, ...), custom_call_target="tpu_custom_call" | custom-call | bytes 4243500 | tf_op jit(solution)/shard_map/pallas_call | solution.py:112
  12.0 3.8 %collective-permute-start.6 = (f32[136,128]{1,0:T(8,128)S(1)}, f32[136,128]{1,0:T(8,128)S(1)}, u32[]{:S(2)}, u32[]{:S(2)}) collective-permute-start(f32[136,128]{1,0:T(8,128)S(1)} %get-tuple-element.75), channel_id=1, source_target_pairs={{0,12},{4,8},{8,4},{12,0},{1,13},{5,9},{9,5},{13,1},{2,14},{6,10},... | collective-permute-start | bytes 208904 | tf_op jit(solution)/shard_map/ppermute | solution.py:769
  15.8 0.6 %collective-permute-start.8 = (f32[136,128]{1,0:T(8,128)S(1)}, f32[136,128]{1,0:T(8,128)S(1)}, u32[]{:S(2)}, u32[]{:S(2)}) collective-permute-start(f32[136,128]{1,0:T(8,128)S(1)} %get-tuple-element.77), channel_id=1, source_target_pairs={{0,8},{4,12},{8,0},{12,4},{1,9},{5,13},{9,1},{13,5},{2,10},{6,14},... | collective-permute-start | bytes 208904 | tf_op jit(solution)/shard_map/ppermute | solution.py:769
  16.4 0.7 %collective-permute-start.5 = (f32[128,512]{1,0:T(8,128)S(1)}, f32[128,512]{1,0:T(8,128)S(1)}, u32[]{:S(2)}, u32[]{:S(2)}) collective-permute-start(f32[128,512]{1,0:T(8,128)S(1)} %get-tuple-element.64), channel_id=1, source_target_pairs={{0,2},{1,3},{2,0},{3,1},{4,6},{5,7},{6,4},{7,5},{8,10},{9,11},{10,... | collective-permute-start | bytes 786440 | tf_op jit(solution)/shard_map/ppermute | solution.py:769
  17.1 0.1 collective-permute-start.3
  17.3 2.3 %shard_map.156 = (f32[544,512]{1,0:T(8,128)S(1)}, f32[16,72,512]{2,1,0:T(8,128)S(1)}, f32[2,4,64,128]{3,2,1,0:T(8,128)S(1)}) custom-call(s32[4]{0:T(128)S(1)} %copy-done.9, f32[16,16,16]{2,1,0:T(8,128)S(1)} %copy-done.3, bf16[2,4,144,32]{3,2,1,0:T(8,128)(2,1)S(1)} %copy-done.4, bf16[128,512]{1,0:T(8,128)(2,1)S(1)} %copy-done.6, f32[16,1024]{1,0:T(8,128)S(1)} %copy-done.5), custom_call_target="tpu_custom_call" | custom-call | bytes 8671500 | tf_op jit(solution)/shard_map/pallas_call | solution.py:112
  19.6 1.4 %collective-permute-start.4 = (f32[128,512]{1,0:T(8,128)S(1)}, f32[128,512]{1,0:T(8,128)S(1)}, u32[]{:S(2)}, u32[]{:S(2)}) collective-permute-start(f32[128,512]{1,0:T(8,128)S(1)} %get-tuple-element.63), channel_id=1, source_target_pairs={{0,1},{1,0},{2,3},{3,2},{4,5},{5,4},{6,7},{7,6},{8,9},{9,8},{10,11... | collective-permute-start | bytes 786440 | tf_op jit(solution)/shard_map/ppermute | solution.py:769
  21.0 0.7 %collective-permute-done.8 = f32[136,128]{1,0:T(8,128)S(1)} collective-permute-done((f32[136,128]{1,0:T(8,128)S(1)}, f32[136,128]{1,0:T(8,128)S(1)}, u32[]{:S(2)}, u32[]{:S(2)}) %collective-permute-start.8) | collective-permute-done | bytes 69664 | tf_op jit(solution)/shard_map/ppermute | solution.py:769
  21.7 3.2 %collective-permute-start.11 = (f32[136,128]{1,0:T(8,128)S(1)}, f32[136,128]{1,0:T(8,128)S(1)}, u32[]{:S(2)}, u32[]{:S(2)}) collective-permute-start(f32[136,128]{1,0:T(8,128)S(1)} %add_add_fusion.share_ref.rest_0_), channel_id=1, source_target_pairs={{0,12},{4,8},{8,4},{12,0},{1,13},{5,9},{9,5},{13,1},{2,14},{6,10},... | collective-permute-start | bytes 208904 | tf_op jit(solution)/shard_map/ppermute | solution.py:769
  24.9 0.8 %collective-permute-done.5.rest_0_ = f32[128,512]{1,0:T(8,128)S(1)} collective-permute-done((f32[128,512]{1,0:T(8,128)S(1)}, f32[128,512]{1,0:T(8,128)S(1)}, u32[]{:S(2)}, u32[]{:S(2)}) %collective-permute-start.5) | collective-permute-done | bytes 262176 | tf_op jit(solution)/shard_map/ppermute | solution.py:769
  25.7 1.4 %collective-permute-start.9 = (f32[136,128]{1,0:T(8,128)S(1)}, f32[136,128]{1,0:T(8,128)S(1)}, u32[]{:S(2)}, u32[]{:S(2)}) collective-permute-start(f32[136,128]{1,0:T(8,128)S(1)} %add_add_fusion.share_ref.rest_0_), channel_id=1, source_target_pairs={{0,4},{4,0},{8,12},{12,8},{1,5},{5,1},{9,13},{13,9},{2,6},{6,2},{1... | collective-permute-start | bytes 208904 | tf_op jit(solution)/shard_map/ppermute | solution.py:769
  27.1 1.1 %shard_map.157 = (f32[272,512]{1,0:T(8,128)S(1)}, f32[544,512]{1,0:T(8,128)S(1)}) custom-call(f32[4]{0:T(128)S(1)} %copy-done.7, f32[4]{0:T(128)S(1)} %copy-done.8, f32[136,128]{1,0:T(8,128)S(1)} %add_add_fusion.share_ref.rest_0_, f32[544,512]{1,0:T(8,128)S(1)} %get-tuple-element.82.spectrum_ref, f32[16,72,512]{2,1,0:T(8,128)S(1)} %get-tuple-element.83.power_ref), custom_call_target="tpu_custom_call" | custom-call | bytes 4243500 | tf_op jit(solution)/shard_map/pallas_call | solution.py:112
  28.2 0.7 %shard_map.153.rest_3_ = f32[544,512]{1,0:T(8,128)S(1)} custom-call(f32[128,512]{1,0:T(8,128)S(1)} %collective-permute-done.5.rest_0_, f32[128,512]{1,0:T(8,128)S(1)} %get-tuple-element.65.rest_1_, bf16[2,2,2,2,128,256]{5,4,3,2,1,0:T(8,128)(2,1)S(1)} %copy-done), custom_call_target="tpu_custom_call" | custom-call | bytes 3690000 | tf_op jit(solution)/shard_map/pallas_call | solution.py:112
  28.9 0.0 copy-start.2
  29.0 0.7 %shard_map.154.spectrum_ref = f32[544,512]{1,0:T(8,128)S(1)} custom-call(f32[128,512]{1,0:T(8,128)S(1)} %collective-permute-done.3.rest_0_, f32[128,512]{1,0:T(8,128)S(1)} %collective-permute-done.4.rest_1_, bf16[2,2,2,2,128,256]{5,4,3,2,1,0:T(8,128)(2,1)S(1)} %copy-done, f32[544,512]{1,0:T(8,128)S(1)} %shard_map.153.rest_3_), custom_call_target="tpu_custom_call" | custom-call | bytes 3690000 | tf_op jit(solution)/shard_map/pallas_call | solution.py:112
  29.7 1.4 %collective-permute-done.10.rest_2_ = f32[136,128]{1,0:T(8,128)S(1)} collective-permute-done((f32[136,128]{1,0:T(8,128)S(1)}, f32[136,128]{1,0:T(8,128)S(1)}, u32[]{:S(2)}, u32[]{:S(2)}) %collective-permute-start.10) | collective-permute-done | bytes 69664 | tf_op jit(solution)/shard_map/ppermute | solution.py:769
  31.1 0.3 collective-permute-done.9.rest_1_
  31.3 0.8 %shard_map.158 = (f32[2,144,128]{2,1,0:T(8,128)S(1)}, f32[2,144,128]{2,1,0:T(8,128)S(1)}, f32[2,144,128]{2,1,0:T(8,128)S(1)}, f32[2,144,128]{2,1,0:T(8,128)S(1)}) custom-call(f32[544,512]{1,0:T(8,128)S(1)} %shard_map.154.spectrum_ref, f32[272,512]{1,0:T(8,128)S(1)} %get-tuple-element.84.gain_ref, f32[544,512]{1,0:T(8,128)S(1)} %get-tuple-element.85.cross_ref, ...), custom_call_target="tpu_custom_call" | custom-call | bytes 4981500 | tf_op jit(solution)/shard_map/pallas_call | solution.py:112
  32.1 0.1 collective-permute-start.12
  32.2 0.7 %collective-permute-start.13 = (f32[2,144,128]{2,1,0:T(8,128)S(1)}, f32[2,144,128]{2,1,0:T(8,128)S(1)}, u32[]{:S(2)}, u32[]{:S(2)}) collective-permute-start(f32[2,144,128]{2,1,0:T(8,128)S(1)} %get-tuple-element.88), channel_id=1, source_target_pairs={{0,2},{1,3},{2,0},{3,1},{4,6},{5,7},{6,4},{7,5},{8,10},{9,11},{10,... | collective-permute-start | bytes 442376 | tf_op jit(solution)/shard_map/ppermute | solution.py:769
  32.9 1.2 %collective-permute-start.14 = (f32[2,144,128]{2,1,0:T(8,128)S(1)}, f32[2,144,128]{2,1,0:T(8,128)S(1)}, u32[]{:S(2)}, u32[]{:S(2)}) collective-permute-start(f32[2,144,128]{2,1,0:T(8,128)S(1)} %get-tuple-element.89), channel_id=1, source_target_pairs={{0,3},{1,2},{2,1},{3,0},{4,7},{5,6},{6,5},{7,4},{8,11},{9,10},{10,... | collective-permute-start | bytes 442376 | tf_op jit(solution)/shard_map/ppermute | solution.py:769
  34.1 0.8 %shard_map.159 = (f32[2,144,128]{2,1,0:T(8,128)S(1)}, f32[2,144,128]{2,1,0:T(8,128)S(1)}, f32[2,144,128]{2,1,0:T(8,128)S(1)}, f32[2,144,128]{2,1,0:T(8,128)S(1)}) custom-call(f32[544,512]{1,0:T(8,128)S(1)} %shard_map.154.spectrum_ref, f32[272,512]{1,0:T(8,128)S(1)} %get-tuple-element.84.gain_ref, f32[544,512]{1,0:T(8,128)S(1)} %get-tuple-element.85.cross_ref, ...), custom_call_target="tpu_custom_call" | custom-call | bytes 4981500 | tf_op jit(solution)/shard_map/pallas_call | solution.py:112
  34.9 0.4 collective-permute-start.15
  35.3 0.6 %collective-permute-start.16 = (f32[2,144,128]{2,1,0:T(8,128)S(1)}, f32[2,144,128]{2,1,0:T(8,128)S(1)}, u32[]{:S(2)}, u32[]{:S(2)}) collective-permute-start(f32[2,144,128]{2,1,0:T(8,128)S(1)} %get-tuple-element.92), channel_id=1, source_target_pairs={{0,2},{1,3},{2,0},{3,1},{4,6},{5,7},{6,4},{7,5},{8,10},{9,11},{10,... | collective-permute-start | bytes 442376 | tf_op jit(solution)/shard_map/ppermute | solution.py:769
  35.9 0.9 %collective-permute-start.17 = (f32[2,144,128]{2,1,0:T(8,128)S(1)}, f32[2,144,128]{2,1,0:T(8,128)S(1)}, u32[]{:S(2)}, u32[]{:S(2)}) collective-permute-start(f32[2,144,128]{2,1,0:T(8,128)S(1)} %get-tuple-element.93), channel_id=1, source_target_pairs={{0,3},{1,2},{2,1},{3,0},{4,7},{5,6},{6,5},{7,4},{8,11},{9,10},{10,... | collective-permute-start | bytes 442376 | tf_op jit(solution)/shard_map/ppermute | solution.py:769
  36.8 0.0 copy-start.1
  36.8 1.0 %shard_map.161.chosen_ref = bf16[8,512,512]{2,1,0:T(8,128)(2,1)S(1)} custom-call(s32[8,512]{1,0:T(8,128)S(1)} %reshape.11.col_ref), custom_call_target="tpu_custom_call" | custom-call | bytes 7380000 | tf_op jit(solution)/shard_map/pallas_call | solution.py:112
  37.8 1.1 %collective-permute-done.13.rest_2_.rest_0_ = f32[2,144,128]{2,1,0:T(8,128)S(1)} collective-permute-done((f32[2,144,128]{2,1,0:T(8,128)S(1)}, f32[2,144,128]{2,1,0:T(8,128)S(1)}, u32[]{:S(2)}, u32[]{:S(2)}) %collective-permute-start.13) | collective-permute-done | bytes 147488 | tf_op jit(solution)/shard_map/ppermute | solution.py:769
  38.9 2.3 %collective-permute-done.14.rest_3_.rest_1_ = f32[2,144,128]{2,1,0:T(8,128)S(1)} collective-permute-done((f32[2,144,128]{2,1,0:T(8,128)S(1)}, f32[2,144,128]{2,1,0:T(8,128)S(1)}, u32[]{:S(2)}, u32[]{:S(2)}) %collective-permute-start.14) | collective-permute-done | bytes 147488 | tf_op jit(solution)/shard_map/ppermute | solution.py:769
  41.2 4.4 %shard_map.162 = (bf16[512,512]{1,0:T(8,128)(2,1)}, f32[4,2,1024]{2,1,0:T(2,128)S(1)}) custom-call(s32[8,512]{1,0:T(8,128)S(1)} %reshape.10.row_ref, bf16[8,512,512]{2,1,0:T(8,128)(2,1)S(1)} %shard_map.161.chosen_ref, f32[2,4,64,128]{3,2,1,0:T(8,128)S(1)} %get-tuple-element.94.taps_ref, f32[2,144,128]{2,1,0:T(8,128)S(1)} %collective-permute-done.13.rest_2_.rest_0_, ...), custom_call_target="tpu_custom_call" | custom-call | bytes 12915000 | tf_op jit(solution)/shard_map/pallas_call | solution.py:112
  45.6 1.9 %collective-permute-done.17.rest_7_.rest_1_ = f32[2,144,128]{2,1,0:T(8,128)S(1)} collective-permute-done((f32[2,144,128]{2,1,0:T(8,128)S(1)}, f32[2,144,128]{2,1,0:T(8,128)S(1)}, u32[]{:S(2)}, u32[]{:S(2)}) %collective-permute-start.17) | collective-permute-done | bytes 147488 | tf_op jit(solution)/shard_map/ppermute | solution.py:769
  47.5 3.3 %shard_map.163 = (bf16[512,512]{1,0:T(8,128)(2,1)S(1)}, f32[4,1024]{1,0:T(4,128)S(1)}, f32[4,1024]{1,0:T(4,128)S(1)}, f32[4,1024]{1,0:T(4,128)S(1)}) custom-call(s32[8,512]{1,0:T(8,128)S(1)} %reshape.10.row_ref, bf16[8,512,512]{2,1,0:T(8,128)(2,1)S(1)} %shard_map.161.chosen_ref, f32[2,4,64,128]{3,2,1,0:T(8,128)S(1)} %get-tuple-element.94.taps_ref, ...), custom_call_target="tpu_custom_call" | custom-call | bytes 12915000 | tf_op jit(solution)/shard_map/pallas_call | solution.py:112
  50.8 0.6 %collective-permute-start.18 = (f32[4,1024]{1,0:T(4,128)S(1)}, f32[4,1024]{1,0:T(4,128)S(1)}, u32[]{:S(2)}, u32[]{:S(2)}) collective-permute-start(f32[4,1024]{1,0:T(4,128)S(1)} %get-tuple-element.96), channel_id=1, source_target_pairs={{0,3},{1,2},{2,1},{3,0},{4,7},{5,6},{6,5},{7,4},{8,11},{9,10},{10,... | collective-permute-start | bytes 49160 | tf_op jit(solution)/shard_map/ppermute | solution.py:769
  51.4 1.4 %collective-permute-start.19 = (f32[4,1024]{1,0:T(4,128)S(1)}, f32[4,1024]{1,0:T(4,128)S(1)}, u32[]{:S(2)}, u32[]{:S(2)}) collective-permute-start(f32[4,1024]{1,0:T(4,128)S(1)} %get-tuple-element.97), channel_id=1, source_target_pairs={{0,2},{1,3},{2,0},{3,1},{4,6},{5,7},{6,4},{7,5},{8,10},{9,11},{10,... | collective-permute-start | bytes 49160 | tf_op jit(solution)/shard_map/ppermute | solution.py:769
  52.8 0.7 %shard_map.164 = f32[4,1024]{1,0:T(4,128)S(1)} custom-call(s32[8,512]{1,0:T(8,128)S(1)} %reshape.10.row_ref, bf16[8,512,512]{2,1,0:T(8,128)(2,1)S(1)} %shard_map.161.chosen_ref, bf16[512,512]{1,0:T(8,128)(2,1)S(1)} %get-tuple-element.99.flux_ref, f32[4,2,1024]{2,1,0:T(2,128)S(1)} %get-tuple-element.95.rest_5_.rest_0_), custom_call_target="tpu_custom_call" | custom-call | bytes 3321000 | tf_op jit(solution)/shard_map/pallas_call | solution.py:112
  53.5 1.5 %shard_map.160 = f32[4,128,512]{2,1,0:T(8,128)} custom-call(f32[2,144,128]{2,1,0:T(8,128)S(1)} %get-tuple-element.86.rest_0_.rest_3_, f32[2,144,128]{2,1,0:T(8,128)S(1)} %collective-permute-done.12.rest_1_.rest_2_, f32[2,144,128]{2,1,0:T(8,128)S(1)} %collective-permute-done.13.rest_2_.rest_0_, f32[2,144,128]{2,1,0:T(8,128)S(1)} %collective-permute-done.14.rest_3_.rest_1_, ...), custom_call_target="tpu_custom_call" | custom-call | bytes 8118000 | tf_op jit(solution)/shard_map/pallas_call | solution.py:112
  55.1 0.1 collective-permute-done.19
  55.2 0.6 %add_add_fusion.1 = f32[4,1024]{1,0:T(4,128)} fusion(f32[4,1024]{1,0:T(4,128)S(1)} %shard_map.164, f32[4,1024]{1,0:T(4,128)S(1)} %collective-permute-done.20, f32[4,1024]{1,0:T(4,128)S(1)} %collective-permute-done.18, f32[4,1024]{1,0:T(4,128)S(1)} %collective-permute-done.19), kind=kLoop, calls=%fused_computation.1 | loop fusion | flops 12288 | bytes 81920 | tf_op jit(solution)/shard_map/add | solution.py:828
  (38 shorter events, 0.1 us)
Async XLA Ops:
  4.1 6.0 %collective-permute-start = (f32[144,128]{1,0:T(8,128)S(1)}, f32[144,128]{1,0:T(8,128)S(1)}, u32[]{:S(2)}, u32[]{:S(2)}) collective-permute-start(f32[144,128]{1,0:T(8,128)S(1)} %get-tuple-element.51), channel_id=1, source_target_pairs={{0,2},{1,3},{2,0},{3,1},{4,6},{5,7},{6,4},{7,5},{8,10},{9,11},{10,... | collective-permute-start | bytes 221192 | tf_op jit(solution)/shard_map/ppermute | solution.py:769
  7.1 4.3 %collective-permute-start.1 = (f32[144,128]{1,0:T(8,128)S(1)}, f32[144,128]{1,0:T(8,128)S(1)}, u32[]{:S(2)}, u32[]{:S(2)}) collective-permute-start(f32[144,128]{1,0:T(8,128)S(1)} %get-tuple-element.52), channel_id=1, source_target_pairs={{0,3},{1,2},{2,1},{3,0},{4,7},{5,6},{6,5},{7,4},{8,11},{9,10},{10,... | collective-permute-start | bytes 221192 | tf_op jit(solution)/shard_map/ppermute | solution.py:769
  8.1 3.3 %copy-start = (bf16[2,2,2,2,128,256]{5,4,3,2,1,0:T(8,128)(2,1)S(1)}, bf16[2,2,2,2,128,256]{5,4,3,2,1,0:T(8,128)(2,1)}, u32[]{:S(2)}) copy-start(bf16[2,2,2,2,128,256]{5,4,3,2,1,0:T(8,128)(2,1)} %constant.16.clone.rest_2_.rest_4_) | copy-start | bytes 3145732
  8.1 3.3 %collective-permute-start.2 = (f32[144,128]{1,0:T(8,128)S(1)}, f32[144,128]{1,0:T(8,128)S(1)}, u32[]{:S(2)}, u32[]{:S(2)}) collective-permute-start(f32[144,128]{1,0:T(8,128)S(1)} %get-tuple-element.56), channel_id=1, source_target_pairs={{0,1},{1,0},{2,3},{3,2},{4,5},{5,4},{6,7},{7,6},{8,9},{9,8},{10,11... | collective-permute-start | bytes 221192 | tf_op jit(solution)/shard_map/ppermute | solution.py:769
  9.0 8.2 %copy-start.3 = (f32[16,16,16]{2,1,0:T(8,128)S(1)}, f32[16,16,16]{2,1,0:T(8,128)}, u32[]{:S(2)}) copy-start(f32[16,16,16]{2,1,0:T(8,128)} %bank_ref) | copy-start | bytes 49156
  9.0 8.2 %copy-start.4 = (bf16[2,4,144,32]{3,2,1,0:T(8,128)(2,1)S(1)}, bf16[2,4,144,32]{3,2,1,0:T(8,128)(2,1)}, u32[]{:S(2)}) copy-start(bf16[2,4,144,32]{3,2,1,0:T(8,128)(2,1)} %constant.17.clone.shift_ref) | copy-start | bytes 221188
  9.0 8.2 %copy-start.5 = (f32[16,1024]{1,0:T(8,128)S(1)}, f32[16,1024]{1,0:T(8,128)}, u32[]{:S(2)}) copy-start(f32[16,1024]{1,0:T(8,128)} %constant.14.clone.rest_4_.coef_ref) | copy-start | bytes 196612
  9.0 8.2 %copy-start.6 = (bf16[128,512]{1,0:T(8,128)(2,1)S(1)}, bf16[128,512]{1,0:T(8,128)(2,1)}, u32[]{:S(2)}) copy-start(bf16[128,512]{1,0:T(8,128)(2,1)} %constant.18.clone.spread_ref) | copy-start | bytes 393220
  9.1 8.2 %copy-start.9 = (s32[4]{0:T(128)S(1)}, s32[4]{0:T(128)}, u32[]{:S(2)}) copy-start(s32[4]{0:T(128)} %index_ref.1) | copy-start | bytes 52
  11.4 15.7 %copy-start.7 = (f32[4]{0:T(128)S(1)}, f32[4]{0:T(128)}, u32[]{:S(2)}) copy-start(f32[4]{0:T(128)} %flux_ref.1) | copy-start | bytes 52
  11.4 15.7 %copy-start.8 = (f32[4]{0:T(128)S(1)}, f32[4]{0:T(128)}, u32[]{:S(2)}) copy-start(f32[4]{0:T(128)} %noise_ref.1) | copy-start | bytes 52
  12.0 7.6 %collective-permute-start.6 = (f32[136,128]{1,0:T(8,128)S(1)}, f32[136,128]{1,0:T(8,128)S(1)}, u32[]{:S(2)}, u32[]{:S(2)}) collective-permute-start(f32[136,128]{1,0:T(8,128)S(1)} %get-tuple-element.75), channel_id=1, source_target_pairs={{0,12},{4,8},{8,4},{12,0},{1,13},{5,9},{9,5},{13,1},{2,14},{6,10},... | collective-permute-start | bytes 208904 | tf_op jit(solution)/shard_map/ppermute | solution.py:769
  15.8 5.2 %collective-permute-start.7 = (f32[136,128]{1,0:T(8,128)S(1)}, f32[136,128]{1,0:T(8,128)S(1)}, u32[]{:S(2)}, u32[]{:S(2)}) collective-permute-start(f32[136,128]{1,0:T(8,128)S(1)} %get-tuple-element.76), channel_id=1, source_target_pairs={{0,4},{4,0},{8,12},{12,8},{1,5},{5,1},{9,13},{13,9},{2,6},{6,2},{1... | collective-permute-start | bytes 208904 | tf_op jit(solution)/shard_map/ppermute | solution.py:769
  15.8 5.9 %collective-permute-start.8 = (f32[136,128]{1,0:T(8,128)S(1)}, f32[136,128]{1,0:T(8,128)S(1)}, u32[]{:S(2)}, u32[]{:S(2)}) collective-permute-start(f32[136,128]{1,0:T(8,128)S(1)} %get-tuple-element.77), channel_id=1, source_target_pairs={{0,8},{4,12},{8,0},{12,4},{1,9},{5,13},{9,1},{13,5},{2,10},{6,14},... | collective-permute-start | bytes 208904 | tf_op jit(solution)/shard_map/ppermute | solution.py:769
  16.4 9.2 %collective-permute-start.5 = (f32[128,512]{1,0:T(8,128)S(1)}, f32[128,512]{1,0:T(8,128)S(1)}, u32[]{:S(2)}, u32[]{:S(2)}) collective-permute-start(f32[128,512]{1,0:T(8,128)S(1)} %get-tuple-element.64), channel_id=1, source_target_pairs={{0,2},{1,3},{2,0},{3,1},{4,6},{5,7},{6,4},{7,5},{8,10},{9,11},{10,... | collective-permute-start | bytes 786440 | tf_op jit(solution)/shard_map/ppermute | solution.py:769
  17.1 11.8 %collective-permute-start.3 = (f32[128,512]{1,0:T(8,128)S(1)}, f32[128,512]{1,0:T(8,128)S(1)}, u32[]{:S(2)}, u32[]{:S(2)}) collective-permute-start(f32[128,512]{1,0:T(8,128)S(1)} %get-tuple-element.62), channel_id=1, source_target_pairs={{0,3},{1,2},{2,1},{3,0},{4,7},{5,6},{6,5},{7,4},{8,11},{9,10},{10,... | collective-permute-start | bytes 786440 | tf_op jit(solution)/shard_map/ppermute | solution.py:769
  19.6 9.3 %collective-permute-start.4 = (f32[128,512]{1,0:T(8,128)S(1)}, f32[128,512]{1,0:T(8,128)S(1)}, u32[]{:S(2)}, u32[]{:S(2)}) collective-permute-start(f32[128,512]{1,0:T(8,128)S(1)} %get-tuple-element.63), channel_id=1, source_target_pairs={{0,1},{1,0},{2,3},{3,2},{4,5},{5,4},{6,7},{7,6},{8,9},{9,8},{10,11... | collective-permute-start | bytes 786440 | tf_op jit(solution)/shard_map/ppermute | solution.py:769
  21.7 8.0 %collective-permute-start.11 = (f32[136,128]{1,0:T(8,128)S(1)}, f32[136,128]{1,0:T(8,128)S(1)}, u32[]{:S(2)}, u32[]{:S(2)}) collective-permute-start(f32[136,128]{1,0:T(8,128)S(1)} %add_add_fusion.share_ref.rest_0_), channel_id=1, source_target_pairs={{0,12},{4,8},{8,4},{12,0},{1,13},{5,9},{9,5},{13,1},{2,14},{6,10},... | collective-permute-start | bytes 208904 | tf_op jit(solution)/shard_map/ppermute | solution.py:769
  24.9 6.2 %collective-permute-start.10 = (f32[136,128]{1,0:T(8,128)S(1)}, f32[136,128]{1,0:T(8,128)S(1)}, u32[]{:S(2)}, u32[]{:S(2)}) collective-permute-start(f32[136,128]{1,0:T(8,128)S(1)} %add_add_fusion.share_ref.rest_0_), channel_id=1, source_target_pairs={{0,8},{4,12},{8,0},{12,4},{1,9},{5,13},{9,1},{13,5},{2,10},{6,14},... | collective-permute-start | bytes 208904 | tf_op jit(solution)/shard_map/ppermute | solution.py:769
  25.7 5.6 %collective-permute-start.9 = (f32[136,128]{1,0:T(8,128)S(1)}, f32[136,128]{1,0:T(8,128)S(1)}, u32[]{:S(2)}, u32[]{:S(2)}) collective-permute-start(f32[136,128]{1,0:T(8,128)S(1)} %add_add_fusion.share_ref.rest_0_), channel_id=1, source_target_pairs={{0,4},{4,0},{8,12},{12,8},{1,5},{5,1},{9,13},{13,9},{2,6},{6,2},{1... | collective-permute-start | bytes 208904 | tf_op jit(solution)/shard_map/ppermute | solution.py:769
  28.9 2.4 %copy-start.2 = (bf16[2,2,256,512]{3,2,1,0:T(8,128)(2,1)S(1)}, bf16[2,2,256,512]{3,2,1,0:T(8,128)(2,1)}, u32[]{:S(2)}) copy-start(bf16[2,2,256,512]{3,2,1,0:T(8,128)(2,1)} %constant.19.clone.rest_4_) | copy-start | bytes 3145732
  32.1 3.8 %collective-permute-start.12 = (f32[2,144,128]{2,1,0:T(8,128)S(1)}, f32[2,144,128]{2,1,0:T(8,128)S(1)}, u32[]{:S(2)}, u32[]{:S(2)}) collective-permute-start(f32[2,144,128]{2,1,0:T(8,128)S(1)} %get-tuple-element.87), channel_id=1, source_target_pairs={{0,1},{1,0},{2,3},{3,2},{4,5},{5,4},{6,7},{7,6},{8,9},{9,8},{10,11... | collective-permute-start | bytes 442376 | tf_op jit(solution)/shard_map/ppermute | solution.py:769
  32.2 6.7 %collective-permute-start.13 = (f32[2,144,128]{2,1,0:T(8,128)S(1)}, f32[2,144,128]{2,1,0:T(8,128)S(1)}, u32[]{:S(2)}, u32[]{:S(2)}) collective-permute-start(f32[2,144,128]{2,1,0:T(8,128)S(1)} %get-tuple-element.88), channel_id=1, source_target_pairs={{0,2},{1,3},{2,0},{3,1},{4,6},{5,7},{6,4},{7,5},{8,10},{9,11},{10,... | collective-permute-start | bytes 442376 | tf_op jit(solution)/shard_map/ppermute | solution.py:769
  32.9 3.9 %copy-start.10 = (s32[4096]{0:T(1024)S(1)}, s32[4096]{0:T(1024)}, u32[]{:S(2)}) copy-start(s32[4096]{0:T(1024)} %param.19) | copy-start | bytes 49156
  32.9 3.9 %copy-start.11 = (s32[4096]{0:T(1024)S(1)}, s32[4096]{0:T(1024)}, u32[]{:S(2)}) copy-start(s32[4096]{0:T(1024)} %param.20) | copy-start | bytes 49156
  32.9 8.3 %collective-permute-start.14 = (f32[2,144,128]{2,1,0:T(8,128)S(1)}, f32[2,144,128]{2,1,0:T(8,128)S(1)}, u32[]{:S(2)}, u32[]{:S(2)}) collective-permute-start(f32[2,144,128]{2,1,0:T(8,128)S(1)} %get-tuple-element.89), channel_id=1, source_target_pairs={{0,3},{1,2},{2,1},{3,0},{4,7},{5,6},{6,5},{7,4},{8,11},{9,10},{10,... | collective-permute-start | bytes 442376 | tf_op jit(solution)/shard_map/ppermute | solution.py:769
  34.9 10.7 %collective-permute-start.15 = (f32[2,144,128]{2,1,0:T(8,128)S(1)}, f32[2,144,128]{2,1,0:T(8,128)S(1)}, u32[]{:S(2)}, u32[]{:S(2)}) collective-permute-start(f32[2,144,128]{2,1,0:T(8,128)S(1)} %get-tuple-element.91), channel_id=1, source_target_pairs={{0,1},{1,0},{2,3},{3,2},{4,5},{5,4},{6,7},{7,6},{8,9},{9,8},{10,11... | collective-permute-start | bytes 442376 | tf_op jit(solution)/shard_map/ppermute | solution.py:769
  35.3 10.3 %collective-permute-start.16 = (f32[2,144,128]{2,1,0:T(8,128)S(1)}, f32[2,144,128]{2,1,0:T(8,128)S(1)}, u32[]{:S(2)}, u32[]{:S(2)}) collective-permute-start(f32[2,144,128]{2,1,0:T(8,128)S(1)} %get-tuple-element.92), channel_id=1, source_target_pairs={{0,2},{1,3},{2,0},{3,1},{4,6},{5,7},{6,4},{7,5},{8,10},{9,11},{10,... | collective-permute-start | bytes 442376 | tf_op jit(solution)/shard_map/ppermute | solution.py:769
  35.9 11.6 %collective-permute-start.17 = (f32[2,144,128]{2,1,0:T(8,128)S(1)}, f32[2,144,128]{2,1,0:T(8,128)S(1)}, u32[]{:S(2)}, u32[]{:S(2)}) collective-permute-start(f32[2,144,128]{2,1,0:T(8,128)S(1)} %get-tuple-element.93), channel_id=1, source_target_pairs={{0,3},{1,2},{2,1},{3,0},{4,7},{5,6},{6,5},{7,4},{8,11},{9,10},{10,... | collective-permute-start | bytes 442376 | tf_op jit(solution)/shard_map/ppermute | solution.py:769
  36.8 4.3 %copy-start.1 = (bf16[2,4,128,256]{3,2,1,0:T(8,128)(2,1)S(1)}, bf16[2,4,128,256]{3,2,1,0:T(8,128)(2,1)}, u32[]{:S(2)}) copy-start(bf16[2,4,128,256]{3,2,1,0:T(8,128)(2,1)} %constant.20.clone.rest_8_.rest_4_) | copy-start | bytes 1572868
  50.8 4.2 %collective-permute-start.18 = (f32[4,1024]{1,0:T(4,128)S(1)}, f32[4,1024]{1,0:T(4,128)S(1)}, u32[]{:S(2)}, u32[]{:S(2)}) collective-permute-start(f32[4,1024]{1,0:T(4,128)S(1)} %get-tuple-element.96), channel_id=1, source_target_pairs={{0,3},{1,2},{2,1},{3,0},{4,7},{5,6},{6,5},{7,4},{8,11},{9,10},{10,... | collective-permute-start | bytes 49160 | tf_op jit(solution)/shard_map/ppermute | solution.py:769
  51.4 3.7 %collective-permute-start.19 = (f32[4,1024]{1,0:T(4,128)S(1)}, f32[4,1024]{1,0:T(4,128)S(1)}, u32[]{:S(2)}, u32[]{:S(2)}) collective-permute-start(f32[4,1024]{1,0:T(4,128)S(1)} %get-tuple-element.97), channel_id=1, source_target_pairs={{0,2},{1,3},{2,0},{3,1},{4,6},{5,7},{6,4},{7,5},{8,10},{9,11},{10,... | collective-permute-start | bytes 49160 | tf_op jit(solution)/shard_map/ppermute | solution.py:769
  52.8 2.4 %collective-permute-start.20 = (f32[4,1024]{1,0:T(4,128)S(1)}, f32[4,1024]{1,0:T(4,128)S(1)}, u32[]{:S(2)}, u32[]{:S(2)}) collective-permute-start(f32[4,1024]{1,0:T(4,128)S(1)} %get-tuple-element.98), channel_id=1, source_target_pairs={{0,1},{1,0},{2,3},{3,2},{4,5},{5,4},{6,7},{7,6},{8,9},{9,8},{10,11... | collective-permute-start | bytes 49160 | tf_op jit(solution)/shard_map/ppermute | solution.py:769

commit v6 on v5

--- a/solution.py
+++ b/solution.py
@@ -801,7 +801,7 @@
         blocks = trade(blocks, slab_axes, slabs)
         if direct:
             own = trade(numer, "epoch", ranks)
-            own = sum(own[m] for m in [3, 1, 2, 0])
+            own = sum(own[m] for m in [*range(1, ranks)[-1:], *range(1, ranks - 1), 0])
             own, spectrum = lax.optimization_barrier((own, spectrum))
             numer = trade([own] * ranks, "epoch", ranks)
         else:

time: 56 us -> 56 us (level)
  no operation moved by 1% of the time
where the time goes in v6:
time: 56 us; the launch traced here: 55.8 us
  Pallas kernels  24.1 us (43%)
  starting transfers between devices  20.3 us (36%)
  waiting for transfers between devices  9.77 us (17%)
  between operations  0.91 us (2%)
  other arithmetic  0.64 us (1%)
    pallas_call x16, Pallas kernels, call(): pl.pallas_call(kernel, out_shape=tuple((jax.ShapeDtypeStruct(shape, (*kin...  24.1 us
    ppermute x21, starting transfers between devices, trade(): result[m] = lax.ppermute(parts[m], axes, [(i, i ^ m) for i in range(count)])  20.3 us
    ppermute x21, waiting for transfers between devices, trade(): result[m] = lax.ppermute(parts[m], axes, [(i, i ^ m) for i in range(count)])  9.77 us
  transfers between devices with their start and end apart: 21, of which 9 were waited for; matrix products, arithmetic and copies ran while one was open for 0% of the time, Pallas kernels for 29%

profile of v6, /device:TPU:0, one launch (start us, length us, event | category | flops | bytes accessed | tf_op | source)
XLA Modules:
  0.0 55.8 jit_solution(8507493839685586430)
XLA Ops:
  0.6 3.4 %shard_map.149 = (f32[144,128]{1,0:T(8,128)S(1)}, f32[144,128]{1,0:T(8,128)S(1)}, f32[1,128]{1,0:T(1,128)S(1)}, f32[2,4,64,128]{3,2,1,0:T(8,128)S(1)}, f32[4,128...) custom-call(s32[4]{0:T(128)} %index_ref.1, f32[4]{0:T(128)} %flux_ref.1, f32[4]{0:T(128)} %noise_ref.1, ...), custom_call_target="tpu_custom_call" | custom-call | bytes 11808000 | tf_op jit(solution)/shard_map/pallas_call | solution.py:112
  4.1 3.0 %collective-permute-start = (f32[144,128]{1,0:T(8,128)S(1)}, f32[144,128]{1,0:T(8,128)S(1)}, u32[]{:S(2)}, u32[]{:S(2)}) collective-permute-start(f32[144,128]{1,0:T(8,128)S(1)} %get-tuple-element.51), channel_id=1, source_target_pairs={{0,2},{1,3},{2,0},{3,1},{4,6},{5,7},{6,4},{7,5},{8,10},{9,11},{10,... | collective-permute-start | bytes 221192 | tf_op jit(solution)/shard_map/ppermute | solution.py:769
  7.1 1.0 %shard_map.150 = (f32[144,128]{1,0:T(8,128)S(1)}, f32[2,4,160,128]{3,2,1,0:T(8,128)S(1)}) custom-call(f32[2,4,64,128]{3,2,1,0:T(8,128)S(1)} %get-tuple-element.53.taps_ref, f32[4,128,512]{2,1,0:T(8,128)S(1)} %get-tuple-element.54.x_ref, bf16[2,4,128,256]{3,2,1,0:T(8,128)(2,1)S(1)} %get-tuple-element.55.table_ref), custom_call_target="tpu_custom_call" | custom-call | bytes 5904000 | tf_op jit(solution)/shard_map/pallas_call | solution.py:112
  8.1 0.3 collective-permute-start.2
  8.4 0.6 %shard_map.152 = (f32[128,512]{1,0:T(8,128)S(1)}, f32[128,512]{1,0:T(8,128)S(1)}, f32[128,512]{1,0:T(8,128)S(1)}, f32[128,512]{1,0:T(8,128)S(1)}) custom-call(f32[4,128,512]{2,1,0:T(8,128)S(1)} %get-tuple-element.54.x_ref, bf16[2,4,128,256]{3,2,1,0:T(8,128)(2,1)S(1)} %get-tuple-element.55.table_ref), custom_call_target="tpu_custom_call" | custom-call | bytes 4797000 | tf_op jit(solution)/shard_map/pallas_call | solution.py:112
  9.0 0.0 copy-start.4
  9.0 0.0 copy-start.5
  9.0 0.0 copy-start.6
  9.1 1.0 %shard_map.151.rest_3_ = f32[144,128]{1,0:T(8,128)S(1)} custom-call(f32[2,4,64,128]{3,2,1,0:T(8,128)S(1)} %get-tuple-element.53.taps_ref, f32[2,4,160,128]{3,2,1,0:T(8,128)S(1)} %get-tuple-element.57.padded_ref), custom_call_target="tpu_custom_call" | custom-call | bytes 3690000 | tf_op jit(solution)/shard_map/pallas_call | solution.py:112
  10.0 1.3 %collective-permute-done.1.rest_1_ = f32[144,128]{1,0:T(8,128)S(1)} collective-permute-done((f32[144,128]{1,0:T(8,128)S(1)}, f32[144,128]{1,0:T(8,128)S(1)}, u32[]{:S(2)}, u32[]{:S(2)}) %collective-permute-start.1) | collective-permute-done | bytes 73760 | tf_op jit(solution)/shard_map/ppermute | solution.py:769
  11.4 0.6 %shard_map.155 = (f32[136,128]{1,0:T(8,128)S(1)}, f32[136,128]{1,0:T(8,128)S(1)}, f32[136,128]{1,0:T(8,128)S(1)}, f32[136,128]{1,0:T(8,128)S(1)}) custom-call(f32[1,128]{1,0:T(1,128)S(1)} %get-tuple-element.66.shares_ref, f32[144,128]{1,0:T(8,128)S(1)} %collective-permute-done.rest_0_, f32[144,128]{1,0:T(8,128)S(1)} %collective-permute-done.1.rest_1_, ...), custom_call_target="tpu_custom_call" | custom-call | bytes 4243500 | tf_op jit(solution)/shard_map/pallas_call | solution.py:112
  12.0 3.8 %collective-permute-start.6 = (f32[136,128]{1,0:T(8,128)S(1)}, f32[136,128]{1,0:T(8,128)S(1)}, u32[]{:S(2)}, u32[]{:S(2)}) collective-permute-start(f32[136,128]{1,0:T(8,128)S(1)} %get-tuple-element.75), channel_id=1, source_target_pairs={{0,12},{4,8},{8,4},{12,0},{1,13},{5,9},{9,5},{13,1},{2,14},{6,10},... | collective-permute-start | bytes 208904 | tf_op jit(solution)/shard_map/ppermute | solution.py:769
  15.8 0.6 %collective-permute-start.8 = (f32[136,128]{1,0:T(8,128)S(1)}, f32[136,128]{1,0:T(8,128)S(1)}, u32[]{:S(2)}, u32[]{:S(2)}) collective-permute-start(f32[136,128]{1,0:T(8,128)S(1)} %get-tuple-element.77), channel_id=1, source_target_pairs={{0,8},{4,12},{8,0},{12,4},{1,9},{5,13},{9,1},{13,5},{2,10},{6,14},... | collective-permute-start | bytes 208904 | tf_op jit(solution)/shard_map/ppermute | solution.py:769
  16.4 0.7 %collective-permute-start.5 = (f32[128,512]{1,0:T(8,128)S(1)}, f32[128,512]{1,0:T(8,128)S(1)}, u32[]{:S(2)}, u32[]{:S(2)}) collective-permute-start(f32[128,512]{1,0:T(8,128)S(1)} %get-tuple-element.64), channel_id=1, source_target_pairs={{0,2},{1,3},{2,0},{3,1},{4,6},{5,7},{6,4},{7,5},{8,10},{9,11},{10,... | collective-permute-start | bytes 786440 | tf_op jit(solution)/shard_map/ppermute | solution.py:769
  17.1 0.1 collective-permute-start.3
  17.3 2.3 %shard_map.156 = (f32[544,512]{1,0:T(8,128)S(1)}, f32[16,72,512]{2,1,0:T(8,128)S(1)}, f32[2,4,64,128]{3,2,1,0:T(8,128)S(1)}) custom-call(s32[4]{0:T(128)S(1)} %copy-done.9, f32[16,16,16]{2,1,0:T(8,128)S(1)} %copy-done.3, bf16[2,4,144,32]{3,2,1,0:T(8,128)(2,1)S(1)} %copy-done.4, bf16[128,512]{1,0:T(8,128)(2,1)S(1)} %copy-done.6, f32[16,1024]{1,0:T(8,128)S(1)} %copy-done.5), custom_call_target="tpu_custom_call" | custom-call | bytes 8671500 | tf_op jit(solution)/shard_map/pallas_call | solution.py:112
  19.6 1.4 %collective-permute-start.4 = (f32[128,512]{1,0:T(8,128)S(1)}, f32[128,512]{1,0:T(8,128)S(1)}, u32[]{:S(2)}, u32[]{:S(2)}) collective-permute-start(f32[128,512]{1,0:T(8,128)S(1)} %get-tuple-element.63), channel_id=1, source_target_pairs={{0,1},{1,0},{2,3},{3,2},{4,5},{5,4},{6,7},{7,6},{8,9},{9,8},{10,11... | collective-permute-start | bytes 786440 | tf_op jit(solution)/shard_map/ppermute | solution.py:769
  21.0 0.7 %collective-permute-done.8 = f32[136,128]{1,0:T(8,128)S(1)} collective-permute-done((f32[136,128]{1,0:T(8,128)S(1)}, f32[136,128]{1,0:T(8,128)S(1)}, u32[]{:S(2)}, u32[]{:S(2)}) %collective-permute-start.8) | collective-permute-done | bytes 69664 | tf_op jit(solution)/shard_map/ppermute | solution.py:769
  21.7 3.2 %collective-permute-start.11 = (f32[136,128]{1,0:T(8,128)S(1)}, f32[136,128]{1,0:T(8,128)S(1)}, u32[]{:S(2)}, u32[]{:S(2)}) collective-permute-start(f32[136,128]{1,0:T(8,128)S(1)} %add_add_fusion.share_ref.rest_0_), channel_id=1, source_target_pairs={{0,12},{4,8},{8,4},{12,0},{1,13},{5,9},{9,5},{13,1},{2,14},{6,10},... | collective-permute-start | bytes 208904 | tf_op jit(solution)/shard_map/ppermute | solution.py:769
  24.9 0.8 %collective-permute-done.5.rest_0_ = f32[128,512]{1,0:T(8,128)S(1)} collective-permute-done((f32[128,512]{1,0:T(8,128)S(1)}, f32[128,512]{1,0:T(8,128)S(1)}, u32[]{:S(2)}, u32[]{:S(2)}) %collective-permute-start.5) | collective-permute-done | bytes 262176 | tf_op jit(solution)/shard_map/ppermute | solution.py:769
  25.7 1.4 %collective-permute-start.9 = (f32[136,128]{1,0:T(8,128)S(1)}, f32[136,128]{1,0:T(8,128)S(1)}, u32[]{:S(2)}, u32[]{:S(2)}) collective-permute-start(f32[136,128]{1,0:T(8,128)S(1)} %add_add_fusion.share_ref.rest_0_), channel_id=1, source_target_pairs={{0,4},{4,0},{8,12},{12,8},{1,5},{5,1},{9,13},{13,9},{2,6},{6,2},{1... | collective-permute-start | bytes 208904 | tf_op jit(solution)/shard_map/ppermute | solution.py:769
  27.1 1.1 %shard_map.157 = (f32[272,512]{1,0:T(8,128)S(1)}, f32[544,512]{1,0:T(8,128)S(1)}) custom-call(f32[4]{0:T(128)S(1)} %copy-done.7, f32[4]{0:T(128)S(1)} %copy-done.8, f32[136,128]{1,0:T(8,128)S(1)} %add_add_fusion.share_ref.rest_0_, f32[544,512]{1,0:T(8,128)S(1)} %get-tuple-element.82.spectrum_ref, f32[16,72,512]{2,1,0:T(8,128)S(1)} %get-tuple-element.83.power_ref), custom_call_target="tpu_custom_call" | custom-call | bytes 4243500 | tf_op jit(solution)/shard_map/pallas_call | solution.py:112
  28.2 0.7 %shard_map.153.rest_3_ = f32[544,512]{1,0:T(8,128)S(1)} custom-call(f32[128,512]{1,0:T(8,128)S(1)} %collective-permute-done.5.rest_0_, f32[128,512]{1,0:T(8,128)S(1)} %get-tuple-element.65.rest_1_, bf16[2,2,2,2,128,256]{5,4,3,2,1,0:T(8,128)(2,1)S(1)} %copy-done), custom_call_target="tpu_custom_call" | custom-call | bytes 3690000 | tf_op jit(solution)/shard_map/pallas_call | solution.py:112
  28.9 0.0 copy-start.2
  29.0 0.7 %shard_map.154.spectrum_ref = f32[544,512]{1,0:T(8,128)S(1)} custom-call(f32[128,512]{1,0:T(8,128)S(1)} %collective-permute-done.3.rest_0_, f32[128,512]{1,0:T(8,128)S(1)} %collective-permute-done.4.rest_1_, bf16[2,2,2,2,128,256]{5,4,3,2,1,0:T(8,128)(2,1)S(1)} %copy-done, f32[544,512]{1,0:T(8,128)S(1)} %shard_map.153.rest_3_), custom_call_target="tpu_custom_call" | custom-call | bytes 3690000 | tf_op jit(solution)/shard_map/pallas_call | solution.py:112
  29.7 1.4 %collective-permute-done.10.rest_2_ = f32[136,128]{1,0:T(8,128)S(1)} collective-permute-done((f32[136,128]{1,0:T(8,128)S(1)}, f32[136,128]{1,0:T(8,128)S(1)}, u32[]{:S(2)}, u32[]{:S(2)}) %collective-permute-start.10) | collective-permute-done | bytes 69664 | tf_op jit(solution)/shard_map/ppermute | solution.py:769
  31.1 0.3 collective-permute-done.9.rest_1_
  31.3 0.8 %shard_map.158 = (f32[2,144,128]{2,1,0:T(8,128)S(1)}, f32[2,144,128]{2,1,0:T(8,128)S(1)}, f32[2,144,128]{2,1,0:T(8,128)S(1)}, f32[2,144,128]{2,1,0:T(8,128)S(1)}) custom-call(f32[544,512]{1,0:T(8,128)S(1)} %shard_map.154.spectrum_ref, f32[272,512]{1,0:T(8,128)S(1)} %get-tuple-element.84.gain_ref, f32[544,512]{1,0:T(8,128)S(1)} %get-tuple-element.85.cross_ref, ...), custom_call_target="tpu_custom_call" | custom-call | bytes 4981500 | tf_op jit(solution)/shard_map/pallas_call | solution.py:112
  32.1 0.1 collective-permute-start.12
  32.2 0.7 %collective-permute-start.13 = (f32[2,144,128]{2,1,0:T(8,128)S(1)}, f32[2,144,128]{2,1,0:T(8,128)S(1)}, u32[]{:S(2)}, u32[]{:S(2)}) collective-permute-start(f32[2,144,128]{2,1,0:T(8,128)S(1)} %get-tuple-element.88), channel_id=1, source_target_pairs={{0,2},{1,3},{2,0},{3,1},{4,6},{5,7},{6,4},{7,5},{8,10},{9,11},{10,... | collective-permute-start | bytes 442376 | tf_op jit(solution)/shard_map/ppermute | solution.py:769
  32.9 1.2 %collective-permute-start.14 = (f32[2,144,128]{2,1,0:T(8,128)S(1)}, f32[2,144,128]{2,1,0:T(8,128)S(1)}, u32[]{:S(2)}, u32[]{:S(2)}) collective-permute-start(f32[2,144,128]{2,1,0:T(8,128)S(1)} %get-tuple-element.89), channel_id=1, source_target_pairs={{0,3},{1,2},{2,1},{3,0},{4,7},{5,6},{6,5},{7,4},{8,11},{9,10},{10,... | collective-permute-start | bytes 442376 | tf_op jit(solution)/shard_map/ppermute | solution.py:769
  34.1 0.8 %shard_map.159 = (f32[2,144,128]{2,1,0:T(8,128)S(1)}, f32[2,144,128]{2,1,0:T(8,128)S(1)}, f32[2,144,128]{2,1,0:T(8,128)S(1)}, f32[2,144,128]{2,1,0:T(8,128)S(1)}) custom-call(f32[544,512]{1,0:T(8,128)S(1)} %shard_map.154.spectrum_ref, f32[272,512]{1,0:T(8,128)S(1)} %get-tuple-element.84.gain_ref, f32[544,512]{1,0:T(8,128)S(1)} %get-tuple-element.85.cross_ref, ...), custom_call_target="tpu_custom_call" | custom-call | bytes 4981500 | tf_op jit(solution)/shard_map/pallas_call | solution.py:112
  34.9 0.4 collective-permute-start.15
  35.3 0.6 %collective-permute-start.16 = (f32[2,144,128]{2,1,0:T(8,128)S(1)}, f32[2,144,128]{2,1,0:T(8,128)S(1)}, u32[]{:S(2)}, u32[]{:S(2)}) collective-permute-start(f32[2,144,128]{2,1,0:T(8,128)S(1)} %get-tuple-element.92), channel_id=1, source_target_pairs={{0,2},{1,3},{2,0},{3,1},{4,6},{5,7},{6,4},{7,5},{8,10},{9,11},{10,... | collective-permute-start | bytes 442376 | tf_op jit(solution)/shard_map/ppermute | solution.py:769
  35.9 0.9 %collective-permute-start.17 = (f32[2,144,128]{2,1,0:T(8,128)S(1)}, f32[2,144,128]{2,1,0:T(8,128)S(1)}, u32[]{:S(2)}, u32[]{:S(2)}) collective-permute-start(f32[2,144,128]{2,1,0:T(8,128)S(1)} %get-tuple-element.93), channel_id=1, source_target_pairs={{0,3},{1,2},{2,1},{3,0},{4,7},{5,6},{6,5},{7,4},{8,11},{9,10},{10,... | collective-permute-start | bytes 442376 | tf_op jit(solution)/shard_map/ppermute | solution.py:769
  36.8 0.0 copy-start.1
  36.8 1.0 %shard_map.161.chosen_ref = bf16[8,512,512]{2,1,0:T(8,128)(2,1)S(1)} custom-call(s32[8,512]{1,0:T(8,128)S(1)} %reshape.11.col_ref), custom_call_target="tpu_custom_call" | custom-call | bytes 7380000 | tf_op jit(solution)/shard_map/pallas_call | solution.py:112
  37.8 1.1 %collective-permute-done.13.rest_2_.rest_0_ = f32[2,144,128]{2,1,0:T(8,128)S(1)} collective-permute-done((f32[2,144,128]{2,1,0:T(8,128)S(1)}, f32[2,144,128]{2,1,0:T(8,128)S(1)}, u32[]{:S(2)}, u32[]{:S(2)}) %collective-permute-start.13) | collective-permute-done | bytes 147488 | tf_op jit(solution)/shard_map/ppermute | solution.py:769
  38.9 2.3 %collective-permute-done.14.rest_3_.rest_1_ = f32[2,144,128]{2,1,0:T(8,128)S(1)} collective-permute-done((f32[2,144,128]{2,1,0:T(8,128)S(1)}, f32[2,144,128]{2,1,0:T(8,128)S(1)}, u32[]{:S(2)}, u32[]{:S(2)}) %collective-permute-start.14) | collective-permute-done | bytes 147488 | tf_op jit(solution)/shard_map/ppermute | solution.py:769
  41.2 4.4 %shard_map.162 = (bf16[512,512]{1,0:T(8,128)(2,1)}, f32[4,2,1024]{2,1,0:T(2,128)S(1)}) custom-call(s32[8,512]{1,0:T(8,128)S(1)} %reshape.10.row_ref, bf16[8,512,512]{2,1,0:T(8,128)(2,1)S(1)} %shard_map.161.chosen_ref, f32[2,4,64,128]{3,2,1,0:T(8,128)S(1)} %get-tuple-element.94.taps_ref, f32[2,144,128]{2,1,0:T(8,128)S(1)} %collective-permute-done.13.rest_2_.rest_0_, ...), custom_call_target="tpu_custom_call" | custom-call | bytes 12915000 | tf_op jit(solution)/shard_map/pallas_call | solution.py:112
  45.6 1.9 %collective-permute-done.17.rest_7_.rest_1_ = f32[2,144,128]{2,1,0:T(8,128)S(1)} collective-permute-done((f32[2,144,128]{2,1,0:T(8,128)S(1)}, f32[2,144,128]{2,1,0:T(8,128)S(1)}, u32[]{:S(2)}, u32[]{:S(2)}) %collective-permute-start.17) | collective-permute-done | bytes 147488 | tf_op jit(solution)/shard_map/ppermute | solution.py:769
  47.5 3.3 %shard_map.163 = (bf16[512,512]{1,0:T(8,128)(2,1)S(1)}, f32[4,1024]{1,0:T(4,128)S(1)}, f32[4,1024]{1,0:T(4,128)S(1)}, f32[4,1024]{1,0:T(4,128)S(1)}) custom-call(s32[8,512]{1,0:T(8,128)S(1)} %reshape.10.row_ref, bf16[8,512,512]{2,1,0:T(8,128)(2,1)S(1)} %shard_map.161.chosen_ref, f32[2,4,64,128]{3,2,1,0:T(8,128)S(1)} %get-tuple-element.94.taps_ref, ...), custom_call_target="tpu_custom_call" | custom-call | bytes 12915000 | tf_op jit(solution)/shard_map/pallas_call | solution.py:112
  50.8 0.6 %collective-permute-start.18 = (f32[4,1024]{1,0:T(4,128)S(1)}, f32[4,1024]{1,0:T(4,128)S(1)}, u32[]{:S(2)}, u32[]{:S(2)}) collective-permute-start(f32[4,1024]{1,0:T(4,128)S(1)} %get-tuple-element.96), channel_id=1, source_target_pairs={{0,3},{1,2},{2,1},{3,0},{4,7},{5,6},{6,5},{7,4},{8,11},{9,10},{10,... | collective-permute-start | bytes 49160 | tf_op jit(solution)/shard_map/ppermute | solution.py:769
  51.4 1.4 %collective-permute-start.19 = (f32[4,1024]{1,0:T(4,128)S(1)}, f32[4,1024]{1,0:T(4,128)S(1)}, u32[]{:S(2)}, u32[]{:S(2)}) collective-permute-start(f32[4,1024]{1,0:T(4,128)S(1)} %get-tuple-element.97), channel_id=1, source_target_pairs={{0,2},{1,3},{2,0},{3,1},{4,6},{5,7},{6,4},{7,5},{8,10},{9,11},{10,... | collective-permute-start | bytes 49160 | tf_op jit(solution)/shard_map/ppermute | solution.py:769
  52.8 0.7 %shard_map.164 = f32[4,1024]{1,0:T(4,128)S(1)} custom-call(s32[8,512]{1,0:T(8,128)S(1)} %reshape.10.row_ref, bf16[8,512,512]{2,1,0:T(8,128)(2,1)S(1)} %shard_map.161.chosen_ref, bf16[512,512]{1,0:T(8,128)(2,1)S(1)} %get-tuple-element.99.flux_ref, f32[4,2,1024]{2,1,0:T(2,128)S(1)} %get-tuple-element.95.rest_5_.rest_0_), custom_call_target="tpu_custom_call" | custom-call | bytes 3321000 | tf_op jit(solution)/shard_map/pallas_call | solution.py:112
  53.5 1.5 %shard_map.160 = f32[4,128,512]{2,1,0:T(8,128)} custom-call(f32[2,144,128]{2,1,0:T(8,128)S(1)} %get-tuple-element.86.rest_0_.rest_3_, f32[2,144,128]{2,1,0:T(8,128)S(1)} %collective-permute-done.12.rest_1_.rest_2_, f32[2,144,128]{2,1,0:T(8,128)S(1)} %collective-permute-done.13.rest_2_.rest_0_, f32[2,144,128]{2,1,0:T(8,128)S(1)} %collective-permute-done.14.rest_3_.rest_1_, ...), custom_call_target="tpu_custom_call" | custom-call | bytes 8118000 | tf_op jit(solution)/shard_map/pallas_call | solution.py:112
  55.1 0.1 collective-permute-done.19
  55.2 0.6 %add_add_fusion.1 = f32[4,1024]{1,0:T(4,128)} fusion(f32[4,1024]{1,0:T(4,128)S(1)} %shard_map.164, f32[4,1024]{1,0:T(4,128)S(1)} %collective-permute-done.20, f32[4,1024]{1,0:T(4,128)S(1)} %collective-permute-done.18, f32[4,1024]{1,0:T(4,128)S(1)} %collective-permute-done.19), kind=kLoop, calls=%fused_computation.1 | loop fusion | flops 12288 | bytes 81920 | tf_op jit(solution)/shard_map/add | solution.py:828
  (38 shorter events, 0.1 us)
Async XLA Ops:
  4.1 6.0 %collective-permute-start = (f32[144,128]{1,0:T(8,128)S(1)}, f32[144,128]{1,0:T(8,128)S(1)}, u32[]{:S(2)}, u32[]{:S(2)}) collective-permute-start(f32[144,128]{1,0:T(8,128)S(1)} %get-tuple-element.51), channel_id=1, source_target_pairs={{0,2},{1,3},{2,0},{3,1},{4,6},{5,7},{6,4},{7,5},{8,10},{9,11},{10,... | collective-permute-start | bytes 221192 | tf_op jit(solution)/shard_map/ppermute | solution.py:769
  7.1 4.3 %collective-permute-start.1 = (f32[144,128]{1,0:T(8,128)S(1)}, f32[144,128]{1,0:T(8,128)S(1)}, u32[]{:S(2)}, u32[]{:S(2)}) collective-permute-start(f32[144,128]{1,0:T(8,128)S(1)} %get-tuple-element.52), channel_id=1, source_target_pairs={{0,3},{1,2},{2,1},{3,0},{4,7},{5,6},{6,5},{7,4},{8,11},{9,10},{10,... | collective-permute-start | bytes 221192 | tf_op jit(solution)/shard_map/ppermute | solution.py:769
  8.1 3.3 %copy-start = (bf16[2,2,2,2,128,256]{5,4,3,2,1,0:T(8,128)(2,1)S(1)}, bf16[2,2,2,2,128,256]{5,4,3,2,1,0:T(8,128)(2,1)}, u32[]{:S(2)}) copy-start(bf16[2,2,2,2,128,256]{5,4,3,2,1,0:T(8,128)(2,1)} %constant.16.clone.rest_2_.rest_4_) | copy-start | bytes 3145732
  8.1 3.3 %collective-permute-start.2 = (f32[144,128]{1,0:T(8,128)S(1)}, f32[144,128]{1,0:T(8,128)S(1)}, u32[]{:S(2)}, u32[]{:S(2)}) collective-permute-start(f32[144,128]{1,0:T(8,128)S(1)} %get-tuple-element.56), channel_id=1, source_target_pairs={{0,1},{1,0},{2,3},{3,2},{4,5},{5,4},{6,7},{7,6},{8,9},{9,8},{10,11... | collective-permute-start | bytes 221192 | tf_op jit(solution)/shard_map/ppermute | solution.py:769
  9.0 8.2 %copy-start.3 = (f32[16,16,16]{2,1,0:T(8,128)S(1)}, f32[16,16,16]{2,1,0:T(8,128)}, u32[]{:S(2)}) copy-start(f32[16,16,16]{2,1,0:T(8,128)} %bank_ref) | copy-start | bytes 49156
  9.0 8.2 %copy-start.4 = (bf16[2,4,144,32]{3,2,1,0:T(8,128)(2,1)S(1)}, bf16[2,4,144,32]{3,2,1,0:T(8,128)(2,1)}, u32[]{:S(2)}) copy-start(bf16[2,4,144,32]{3,2,1,0:T(8,128)(2,1)} %constant.17.clone.shift_ref) | copy-start | bytes 221188
  9.0 8.2 %copy-start.5 = (f32[16,1024]{1,0:T(8,128)S(1)}, f32[16,1024]{1,0:T(8,128)}, u32[]{:S(2)}) copy-start(f32[16,1024]{1,0:T(8,128)} %constant.14.clone.rest_4_.coef_ref) | copy-start | bytes 196612
  9.0 8.2 %copy-start.6 = (bf16[128,512]{1,0:T(8,128)(2,1)S(1)}, bf16[128,512]{1,0:T(8,128)(2,1)}, u32[]{:S(2)}) copy-start(bf16[128,512]{1,0:T(8,128)(2,1)} %constant.18.clone.spread_ref) | copy-start | bytes 393220
  9.1 8.2 %copy-start.9 = (s32[4]{0:T(128)S(1)}, s32[4]{0:T(128)}, u32[]{:S(2)}) copy-start(s32[4]{0:T(128)} %index_ref.1) | copy-start | bytes 52
  11.4 15.7 %copy-start.7 = (f32[4]{0:T(128)S(1)}, f32[4]{0:T(128)}, u32[]{:S(2)}) copy-start(f32[4]{0:T(128)} %flux_ref.1) | copy-start | bytes 52
  11.4 15.7 %copy-start.8 = (f32[4]{0:T(128)S(1)}, f32[4]{0:T(128)}, u32[]{:S(2)}) copy-start(f32[4]{0:T(128)} %noise_ref.1) | copy-start | bytes 52
  12.0 7.6 %collective-permute-start.6 = (f32[136,128]{1,0:T(8,128)S(1)}, f32[136,128]{1,0:T(8,128)S(1)}, u32[]{:S(2)}, u32[]{:S(2)}) collective-permute-start(f32[136,128]{1,0:T(8,128)S(1)} %get-tuple-element.75), channel_id=1, source_target_pairs={{0,12},{4,8},{8,4},{12,0},{1,13},{5,9},{9,5},{13,1},{2,14},{6,10},... | collective-permute-start | bytes 208904 | tf_op jit(solution)/shard_map/ppermute | solution.py:769
  15.8 5.2 %collective-permute-start.7 = (f32[136,128]{1,0:T(8,128)S(1)}, f32[136,128]{1,0:T(8,128)S(1)}, u32[]{:S(2)}, u32[]{:S(2)}) collective-permute-start(f32[136,128]{1,0:T(8,128)S(1)} %get-tuple-element.76), channel_id=1, source_target_pairs={{0,4},{4,0},{8,12},{12,8},{1,5},{5,1},{9,13},{13,9},{2,6},{6,2},{1... | collective-permute-start | bytes 208904 | tf_op jit(solution)/shard_map/ppermute | solution.py:769
  15.8 5.9 %collective-permute-start.8 = (f32[136,128]{1,0:T(8,128)S(1)}, f32[136,128]{1,0:T(8,128)S(1)}, u32[]{:S(2)}, u32[]{:S(2)}) collective-permute-start(f32[136,128]{1,0:T(8,128)S(1)} %get-tuple-element.77), channel_id=1, source_target_pairs={{0,8},{4,12},{8,0},{12,4},{1,9},{5,13},{9,1},{13,5},{2,10},{6,14},... | collective-permute-start | bytes 208904 | tf_op jit(solution)/shard_map/ppermute | solution.py:769
  16.4 9.2 %collective-permute-start.5 = (f32[128,512]{1,0:T(8,128)S(1)}, f32[128,512]{1,0:T(8,128)S(1)}, u32[]{:S(2)}, u32[]{:S(2)}) collective-permute-start(f32[128,512]{1,0:T(8,128)S(1)} %get-tuple-element.64), channel_id=1, source_target_pairs={{0,2},{1,3},{2,0},{3,1},{4,6},{5,7},{6,4},{7,5},{8,10},{9,11},{10,... | collective-permute-start | bytes 786440 | tf_op jit(solution)/shard_map/ppermute | solution.py:769
  17.1 11.8 %collective-permute-start.3 = (f32[128,512]{1,0:T(8,128)S(1)}, f32[128,512]{1,0:T(8,128)S(1)}, u32[]{:S(2)}, u32[]{:S(2)}) collective-permute-start(f32[128,512]{1,0:T(8,128)S(1)} %get-tuple-element.62), channel_id=1, source_target_pairs={{0,3},{1,2},{2,1},{3,0},{4,7},{5,6},{6,5},{7,4},{8,11},{9,10},{10,... | collective-permute-start | bytes 786440 | tf_op jit(solution)/shard_map/ppermute | solution.py:769
  19.6 9.3 %collective-permute-start.4 = (f32[128,512]{1,0:T(8,128)S(1)}, f32[128,512]{1,0:T(8,128)S(1)}, u32[]{:S(2)}, u32[]{:S(2)}) collective-permute-start(f32[128,512]{1,0:T(8,128)S(1)} %get-tuple-element.63), channel_id=1, source_target_pairs={{0,1},{1,0},{2,3},{3,2},{4,5},{5,4},{6,7},{7,6},{8,9},{9,8},{10,11... | collective-permute-start | bytes 786440 | tf_op jit(solution)/shard_map/ppermute | solution.py:769
  21.7 8.0 %collective-permute-start.11 = (f32[136,128]{1,0:T(8,128)S(1)}, f32[136,128]{1,0:T(8,128)S(1)}, u32[]{:S(2)}, u32[]{:S(2)}) collective-permute-start(f32[136,128]{1,0:T(8,128)S(1)} %add_add_fusion.share_ref.rest_0_), channel_id=1, source_target_pairs={{0,12},{4,8},{8,4},{12,0},{1,13},{5,9},{9,5},{13,1},{2,14},{6,10},... | collective-permute-start | bytes 208904 | tf_op jit(solution)/shard_map/ppermute | solution.py:769
  24.9 6.2 %collective-permute-start.10 = (f32[136,128]{1,0:T(8,128)S(1)}, f32[136,128]{1,0:T(8,128)S(1)}, u32[]{:S(2)}, u32[]{:S(2)}) collective-permute-start(f32[136,128]{1,0:T(8,128)S(1)} %add_add_fusion.share_ref.rest_0_), channel_id=1, source_target_pairs={{0,8},{4,12},{8,0},{12,4},{1,9},{5,13},{9,1},{13,5},{2,10},{6,14},... | collective-permute-start | bytes 208904 | tf_op jit(solution)/shard_map/ppermute | solution.py:769
  25.7 5.6 %collective-permute-start.9 = (f32[136,128]{1,0:T(8,128)S(1)}, f32[136,128]{1,0:T(8,128)S(1)}, u32[]{:S(2)}, u32[]{:S(2)}) collective-permute-start(f32[136,128]{1,0:T(8,128)S(1)} %add_add_fusion.share_ref.rest_0_), channel_id=1, source_target_pairs={{0,4},{4,0},{8,12},{12,8},{1,5},{5,1},{9,13},{13,9},{2,6},{6,2},{1... | collective-permute-start | bytes 208904 | tf_op jit(solution)/shard_map/ppermute | solution.py:769
  28.9 2.4 %copy-start.2 = (bf16[2,2,256,512]{3,2,1,0:T(8,128)(2,1)S(1)}, bf16[2,2,256,512]{3,2,1,0:T(8,128)(2,1)}, u32[]{:S(2)}) copy-start(bf16[2,2,256,512]{3,2,1,0:T(8,128)(2,1)} %constant.19.clone.rest_4_) | copy-start | bytes 3145732
  32.1 3.8 %collective-permute-start.12 = (f32[2,144,128]{2,1,0:T(8,128)S(1)}, f32[2,144,128]{2,1,0:T(8,128)S(1)}, u32[]{:S(2)}, u32[]{:S(2)}) collective-permute-start(f32[2,144,128]{2,1,0:T(8,128)S(1)} %get-tuple-element.87), channel_id=1, source_target_pairs={{0,1},{1,0},{2,3},{3,2},{4,5},{5,4},{6,7},{7,6},{8,9},{9,8},{10,11... | collective-permute-start | bytes 442376 | tf_op jit(solution)/shard_map/ppermute | solution.py:769
  32.2 6.7 %collective-permute-start.13 = (f32[2,144,128]{2,1,0:T(8,128)S(1)}, f32[2,144,128]{2,1,0:T(8,128)S(1)}, u32[]{:S(2)}, u32[]{:S(2)}) collective-permute-start(f32[2,144,128]{2,1,0:T(8,128)S(1)} %get-tuple-element.88), channel_id=1, source_target_pairs={{0,2},{1,3},{2,0},{3,1},{4,6},{5,7},{6,4},{7,5},{8,10},{9,11},{10,... | collective-permute-start | bytes 442376 | tf_op jit(solution)/shard_map/ppermute | solution.py:769
  32.9 3.9 %copy-start.10 = (s32[4096]{0:T(1024)S(1)}, s32[4096]{0:T(1024)}, u32[]{:S(2)}) copy-start(s32[4096]{0:T(1024)} %param.19) | copy-start | bytes 49156
  32.9 3.9 %copy-start.11 = (s32[4096]{0:T(1024)S(1)}, s32[4096]{0:T(1024)}, u32[]{:S(2)}) copy-start(s32[4096]{0:T(1024)} %param.20) | copy-start | bytes 49156
  32.9 8.3 %collective-permute-start.14 = (f32[2,144,128]{2,1,0:T(8,128)S(1)}, f32[2,144,128]{2,1,0:T(8,128)S(1)}, u32[]{:S(2)}, u32[]{:S(2)}) collective-permute-start(f32[2,144,128]{2,1,0:T(8,128)S(1)} %get-tuple-element.89), channel_id=1, source_target_pairs={{0,3},{1,2},{2,1},{3,0},{4,7},{5,6},{6,5},{7,4},{8,11},{9,10},{10,... | collective-permute-start | bytes 442376 | tf_op jit(solution)/shard_map/ppermute | solution.py:769
  34.9 10.7 %collective-permute-start.15 = (f32[2,144,128]{2,1,0:T(8,128)S(1)}, f32[2,144,128]{2,1,0:T(8,128)S(1)}, u32[]{:S(2)}, u32[]{:S(2)}) collective-permute-start(f32[2,144,128]{2,1,0:T(8,128)S(1)} %get-tuple-element.91), channel_id=1, source_target_pairs={{0,1},{1,0},{2,3},{3,2},{4,5},{5,4},{6,7},{7,6},{8,9},{9,8},{10,11... | collective-permute-start | bytes 442376 | tf_op jit(solution)/shard_map/ppermute | solution.py:769
  35.3 10.3 %collective-permute-start.16 = (f32[2,144,128]{2,1,0:T(8,128)S(1)}, f32[2,144,128]{2,1,0:T(8,128)S(1)}, u32[]{:S(2)}, u32[]{:S(2)}) collective-permute-start(f32[2,144,128]{2,1,0:T(8,128)S(1)} %get-tuple-element.92), channel_id=1, source_target_pairs={{0,2},{1,3},{2,0},{3,1},{4,6},{5,7},{6,4},{7,5},{8,10},{9,11},{10,... | collective-permute-start | bytes 442376 | tf_op jit(solution)/shard_map/ppermute | solution.py:769
  35.9 11.6 %collective-permute-start.17 = (f32[2,144,128]{2,1,0:T(8,128)S(1)}, f32[2,144,128]{2,1,0:T(8,128)S(1)}, u32[]{:S(2)}, u32[]{:S(2)}) collective-permute-start(f32[2,144,128]{2,1,0:T(8,128)S(1)} %get-tuple-element.93), channel_id=1, source_target_pairs={{0,3},{1,2},{2,1},{3,0},{4,7},{5,6},{6,5},{7,4},{8,11},{9,10},{10,... | collective-permute-start | bytes 442376 | tf_op jit(solution)/shard_map/ppermute | solution.py:769
  36.8 4.3 %copy-start.1 = (bf16[2,4,128,256]{3,2,1,0:T(8,128)(2,1)S(1)}, bf16[2,4,128,256]{3,2,1,0:T(8,128)(2,1)}, u32[]{:S(2)}) copy-start(bf16[2,4,128,256]{3,2,1,0:T(8,128)(2,1)} %constant.20.clone.rest_8_.rest_4_) | copy-start | bytes 1572868
  50.8 4.2 %collective-permute-start.18 = (f32[4,1024]{1,0:T(4,128)S(1)}, f32[4,1024]{1,0:T(4,128)S(1)}, u32[]{:S(2)}, u32[]{:S(2)}) collective-permute-start(f32[4,1024]{1,0:T(4,128)S(1)} %get-tuple-element.96), channel_id=1, source_target_pairs={{0,3},{1,2},{2,1},{3,0},{4,7},{5,6},{6,5},{7,4},{8,11},{9,10},{10,... | collective-permute-start | bytes 49160 | tf_op jit(solution)/shard_map/ppermute | solution.py:769
  51.4 3.7 %collective-permute-start.19 = (f32[4,1024]{1,0:T(4,128)S(1)}, f32[4,1024]{1,0:T(4,128)S(1)}, u32[]{:S(2)}, u32[]{:S(2)}) collective-permute-start(f32[4,1024]{1,0:T(4,128)S(1)} %get-tuple-element.97), channel_id=1, source_target_pairs={{0,2},{1,3},{2,0},{3,1},{4,6},{5,7},{6,4},{7,5},{8,10},{9,11},{10,... | collective-permute-start | bytes 49160 | tf_op jit(solution)/shard_map/ppermute | solution.py:769
  52.8 2.4 %collective-permute-start.20 = (f32[4,1024]{1,0:T(4,128)S(1)}, f32[4,1024]{1,0:T(4,128)S(1)}, u32[]{:S(2)}, u32[]{:S(2)}) collective-permute-start(f32[4,1024]{1,0:T(4,128)S(1)} %get-tuple-element.98), channel_id=1, source_target_pairs={{0,1},{1,0},{2,3},{3,2},{4,5},{5,4},{6,7},{7,6},{8,9},{9,8},{10,11... | collective-permute-start | bytes 49160 | tf_op jit(solution)/shard_map/ppermute | solution.py:769
